TPU v7x, 512 devices: a whole 4x8x8 slice. The times are simulated.
512 devices in a mesh: pipe: 4 (over y_lo), dp: 64 (over z, x, core), param: 2 (over y_hi).
Axes of the slice: x: 4, y: 8 (y_hi: 2, y_lo: 4; y = y_hi * 4 + y_lo), z: 8, core: 2. Of those that a mesh axis runs over, the one named last changes fastest.
Arguments:
- hidden: bfloat16 [4, 32768, 1920], P('pipe', 'dp'), may hold values from -16 to 16
- targets: bfloat16 [4, 32768, 1024], P('pipe', 'dp', 'param'), may hold values from -0.1875 to 0.1875
- w_proj: bfloat16 [1920, 1024], P('dp', 'param'), may hold values from -0.125 to 0.125
- mask_counts: int32 [4, 64], P('pipe', 'dp'), may hold values from 32 to 256, as said below
- mask_pos: int32 [4, 64, 256], P('pipe', 'dp'), may hold values from 0 to 32767, as said below
- negatives: int32 [4, 64, 100, 256], P('pipe', 'dp'), may hold values from 0 to 32767, as said below
Outputs:
- grad_w: float32 [1920, 1024], P('dp', 'param')
- upstream: bfloat16 [4, 32768, 1920], P('pipe', 'dp', 'param')
- grad_targets: bfloat16 [4, 32768, 1024], P('pipe', 'dp', 'param')
Inputs may be any that keep to these rules, and one draw needn't show every extreme that they name: In every micro-batch some data shard has all 256 slots live; the first mask_counts slots of a shard are live, the others are ignored. `mask_pos`: the 256 slots of data shard j name distinct frames of that shard, j * 512 to (j + 1) * 512 - 1. `negatives`: distractors of a slot are frames of the same utterance as the slot's frame, never that frame, possibly repeated; each lies in the slot's data shard or an adjacent one.
All inputs are finite; a program needn't handle non-finite values.
Results may differ from a plain program's by a relative error of at most 0.0065.
Values may be sent and summed in bfloat16 or wider, within the bound.
No kernel may reach another device: no remote copies, remote signals or barrier semaphores. Data moves between devices by JAX's collectives and lax.ppermute only.
A program may use at most 64 MiB of HBM per device.

v0:
```python
import jax
import jax.numpy as jnp
from jax import lax
from jax.sharding import PartitionSpec as P

sharpness_divisor = 0.1
loss_multiplier = 32.0
epsilon = 1e-06


def with_halo(block, sides, width):
    for axis, dim in sides:
        count = lax.axis_size(axis)
        forward = [(i, i + 1) for i in range(count - 1)]
        backward = [(target, source) for source, target in forward]
        low = lax.ppermute(
            lax.slice_in_dim(block, block.shape[dim] - width, None, axis=dim), axis, forward
        )
        high = lax.ppermute(lax.slice_in_dim(block, 0, width, axis=dim), axis, backward)
        block = jnp.concatenate([low, block, high], axis=dim)
    return block


def from_behind(value, axis, by):
    peers = lax.axis_size(axis)
    return lax.ppermute(value, axis, [(i, (i + by) % peers) for i in range(peers)])


def contract_rows(left, right):
    return lax.dot_general(
        left, right, (((0,), (0,)), ((), ())), preferred_element_type=jnp.float32
    )


def contract_cols(left, right):
    return lax.dot_general(
        left, right, (((1,), (1,)), ((), ())), preferred_element_type=jnp.float32
    )


def pick_columns(table, entries):
    column_ids = jnp.arange(table.shape[1], dtype=jnp.int32)
    hits = entries[:, :, None] == column_ids[None, None, :]
    return jnp.sum(jnp.where(hits, table[:, None, :], 0.0), axis=2)


def spread_columns(values, entries, columns):
    column_ids = jnp.arange(columns, dtype=jnp.int32)
    hits = entries[:, :, None] == column_ids[None, None, :]
    return jnp.sum(jnp.where(hits, values[:, :, None], 0.0), axis=1)


def local(hidden, targets, w_proj, mask_counts, mask_pos, negatives):
    width = hidden.shape[1]
    shard_index = lax.axis_index("dp")
    positions = mask_pos[0, 0] - shard_index * width
    selector = (positions[:, None] == jnp.arange(width, dtype=jnp.int32)[None, :]).astype(
        jnp.bfloat16
    )
    rows = jnp.dot(selector, hidden[0], preferred_element_type=jnp.float32).astype(jnp.bfloat16)
    capacity = positions.shape[0]
    full_w = lax.all_gather(w_proj, "dp", axis=0, tiled=True)
    context = jnp.dot(rows, full_w, preferred_element_type=jnp.float32)
    target_f = targets[0].astype(jnp.float32)
    ctx_sq, tgt_sq = lax.psum(
        (jnp.sum(context * context, axis=1), jnp.sum(target_f * target_f, axis=1)), "param"
    )
    inverse = 1.0 / jnp.sqrt(ctx_sq + epsilon)
    ctx_unit = (context * inverse[:, None]).astype(jnp.bfloat16)
    inv_tgt = 1.0 / jnp.sqrt(tgt_sq + epsilon)
    tgt_unit = (target_f * inv_tgt[:, None]).astype(jnp.bfloat16)
    window = with_halo(tgt_unit, (("dp", 0),), width)
    candidate_similarity_entries = (
        jnp.concatenate([mask_pos[0, 0][None, :], negatives[0, 0]], axis=0)
        - (shard_index - 1) * width
    ).T
    partial_scores = contract_cols(ctx_unit, window)
    similarity_table = lax.psum(partial_scores, "param")
    picked_entries = pick_columns(similarity_table, candidate_similarity_entries)
    unnormalized_table = picked_entries / sharpness_divisor
    expon = jnp.exp(unnormalized_table)
    normalized_probabilities = expon / jnp.sum(expon, axis=1, keepdims=True)
    slot_ids = jnp.arange(capacity, dtype=jnp.int32)
    usable_flags = (slot_ids < mask_counts[0, 0]).astype(jnp.float32)
    first_position = (
        jnp.arange(candidate_similarity_entries.shape[1], dtype=jnp.int32) == 0
    ).astype(jnp.float32)
    unnormalized_derivative = (
        loss_multiplier
        * usable_flags[:, None]
        * (normalized_probabilities - first_position[None, :])
        / sharpness_divisor
    )
    dscore = spread_columns(
        unnormalized_derivative, candidate_similarity_entries, 3 * width
    ).astype(jnp.bfloat16)
    dunit = jnp.dot(dscore, window, preferred_element_type=jnp.float32)
    along = lax.psum(jnp.sum(context * dunit, axis=1), "param")
    dctx = (dunit * inverse[:, None] - context * (along * inverse**3)[:, None]).astype(jnp.bfloat16)
    grad_w = lax.psum_scatter(contract_rows(rows, dctx), "dp", scatter_dimension=0, tiled=True)
    grad_w = lax.psum(grad_w, "pipe")
    row_part = contract_cols(dctx, full_w)
    drows = lax.psum(row_part, "param").astype(jnp.bfloat16)
    half_d = hidden.shape[2] // lax.axis_size("param")
    own_cols = lax.dynamic_slice_in_dim(drows, lax.axis_index("param") * half_d, half_d, 1)
    dhidden = contract_rows(selector, own_cols).astype(jnp.bfloat16)
    upstream = from_behind(dhidden[None], "pipe", -1)
    dwindow = contract_rows(dscore, ctx_unit)
    rims = jnp.concatenate([dwindow[:width], dwindow[2 * width :]], axis=0)
    arrived = with_halo(rims, (("dp", 0),), width)
    dtgt_unit = dwindow[width : 2 * width] + arrived[:width] + arrived[3 * width :]
    along_t = lax.psum(jnp.sum(target_f * dtgt_unit, axis=1), "param")
    grad_t = dtgt_unit * inv_tgt[:, None] - target_f * (along_t * inv_tgt**3)[:, None]
    return (grad_w, upstream, grad_t.astype(jnp.bfloat16)[None])


def solution(mesh):
    return jax.shard_map(
        local,
        mesh=mesh,
        in_specs=(
            P("pipe", "dp", None),
            P("pipe", "dp", "param"),
            P("dp", "param"),
            P("pipe", "dp"),
            P("pipe", "dp", None),
            P("pipe", "dp", None, None),
        ),
        out_specs=(P("dp", "param"), P("pipe", "dp", "param"), P("pipe", "dp", "param")),
        check_vma=False,
    )
```

profile of v0, /device:TPU:56, one launch (start us, length us, event | category | flops | bytes accessed | tf_op | source)
XLA Modules:
  0.0 587.5 jit_solution(8256187356340287754)
XLA Ops:
  10.8 87.9 %all-gather.3.cloned.1.call-done = bf16[64,30,512]{2,1,0:T(8,128)(2,1)} async-done(((bf16[1,30,512]{2,1,0:T(8,128)(2,1)}), bf16[64,30,512]{2,1,0:T(8,128)(2,1)}) %all-gather.3.cloned.1.call-update) | async-done | bytes 1966096 | tf_op jit(solution)/shard_map/all_gather | solution.py:62
  98.7 3.9 reshape.83
  102.7 3.0 multiply_reduce_fusion.1
  105.7 8.8 %all-reduce.3 = (f32[512]{0:T(512)S(1)}, f32[256]{0:T(256)S(1)}) all-reduce(f32[512]{0:T(512)S(1)} %fusion.3, f32[256]{0:T(256)S(1)} %get-tuple-element.21), channel_id=1, replica_groups=mesh['pipe'=4,'dp'=64,'param'=2] {'param'}, use_global_device_ids=true, to_apply=%region_3.0 | all-reduce | flops 768 | bytes 6144 | tf_op jit(solution)/shard_map/psum | solution.py:65
  116.0 3.1 collective-permute-start
  121.3 2.8 fusion.10
  128.0 102.1 %all-reduce.7.cloned.1.call-done = f32[256,1536]{1,0:T(8,128)} async-done(((f32[256,1536]{1,0:T(8,128)}), f32[256,1536]{1,0:T(8,128)}) %all-reduce.7.cloned.1.call-update) | async-done | bytes 1572880 | tf_op jit(solution)/shard_map/psum | solution.py:78
  230.1 28.6 %select_reduce_fusion.1 = f32[256,101]{0,1:T(8,128)S(1)} fusion(f32[256,1536]{1,0:T(8,128)} %all-reduce.7.cloned.1.call-done, s32[256,101]{0,1:T(8,128)} %fusion.17), kind=kLoop, calls=%fused_computation.1 | loop fusion | flops 119118592 | bytes 1779712 | tf_op jit(solution)/shard_map/reduce_sum | solution.py:44
  258.9 31.0 %select_reduce_fusion = bf16[256,1536]{1,0:T(8,128)(2,1)S(1)} fusion(f32[256,101]{0,1:T(8,128)S(1)} %multiply_multiply_fusion, s32[256,101]{0,1:T(8,128)} %fusion.17), kind=kLoop, calls=%fused_computation | loop fusion | flops 118751232 | bytes 993280 | tf_op jit(solution)/shard_map/reduce_sum | solution.py:50
  289.8 2.4 fusion.12
  293.6 8.8 %psum.52 = f32[256]{0:T(256)S(1)} all-reduce(f32[256]{0:T(256)S(1)} %get-tuple-element.23), channel_id=1, replica_groups=mesh['pipe'=4,'dp'=64,'param'=2] {'param'}, use_global_device_ids=true, to_apply=%region_9.10 | all-reduce | flops 256 | bytes 2048 | tf_op jit(solution)/shard_map/psum | solution.py:98
  305.6 3.1 collective-permute-start.3
  311.0 2.6 fusion.25
  317.1 52.4 %all-reduce.8 = (bf16[256,1920]{0,1:T(8,128)(2,1)}, f32[512]{0:T(512)S(1)}) all-reduce(f32[256,1920]{0,1:T(8,128)} %fusion.26, f32[512]{0:T(512)S(1)} %fusion.5), channel_id=1, replica_groups=mesh['pipe'=4,'dp'=64,'param'=2] {'param'}, use_global_device_ids=true, to_apply=%region_12.13 | all-reduce | flops 492032 | bytes 2953216 | tf_op jit(solution)/shard_map/psum | solution.py:103
  369.5 2.6 fusion.2
  372.1 50.7 %collective-permute-start.2 = (bf16[1,512,960]{1,2,0:T(8,128)(2,1)}, bf16[1,512,960]{1,2,0:T(8,128)(2,1)}, u32[]{:S(2)}, u32[]{:S(2)}) collective-permute-start(bf16[1,512,960]{1,2,0:T(8,128)(2,1)} %fusion.2), channel_id=1, source_target_pairs={{0,384},{128,0},{256,128},{384,256},{1,385},{129,1},{257,129},{385... | collective-permute-start | bytes 2949128 | tf_op jit(solution)/shard_map/ppermute | solution.py:26
  422.8 106.0 %fusion = f32[32,512]{1,0:T(8,128)} fusion(f32[1920,512]{1,0:T(8,128)} %fusion.25), kind=kCustom, calls=%all-reduce-scatter | all-reduce-scatter fusion | flops 1048577 | bytes 3999744
  528.8 2.6 collective-permute-start.7
  531.3 3.4 collective-permute-start.6
  534.7 3.5 collective-permute-start.5
  539.7 4.5 collective-permute-start.8
  546.1 7.4 %concatenate.8 = f32[158,512]{1,0:T(8,128)} concatenate(f32[30,512]{1,0:T(8,128)} %collective-permute-done.8, f32[32,512]{1,0:T(8,128)} %collective-permute-done.7, f32[32,512]{1,0:T(8,128)} %collective-permute-done.6, f32[32,512]{1,0:T(8,128)} %collective-permute-done.5, f32[32,512]{1,0:T(8,128)} %fusion), dimensions={0} | concatenate | bytes 647168
  555.0 18.6 %psum.53 = f32[30,512]{1,0:T(8,128)} all-reduce(f32[30,512]{1,0:T(8,128)} %constant_dynamic-slice_fusion), channel_id=1, replica_groups=mesh['pipe'=4,'dp'=64,'param'=2] {'pipe'}, use_global_device_ids=true, to_apply=%region_11.12 | all-reduce | flops 15360 | bytes 122880 | tf_op jit(solution)/shard_map/psum | solution.py:101
  573.6 2.8 fusion.11
  (70 shorter events, 29.4 us)
Async XLA Ops:
  7.2 2.9 copy-start
  7.2 91.6 %all-gather.3.cloned.1.call-start = ((), (), s32[]{:S(2)}) async-start(), calls=%async_computation.1 | async-start | bytes 2129920 | tf_op jit(solution)/shard_map/all_gather | solution.py:62
  7.9 222.2 %all-reduce.7.cloned.1.call-start = ((), (), s32[]{:S(2)}) async-start(), calls=%async_computation | async-start | bytes 3145728 | tf_op jit(solution)/shard_map/psum | solution.py:78
  114.6 5.9 copy-start.8
  114.7 4.4 collective-permute-start.1
  116.0 4.6 collective-permute-start
  119.0 1.5 copy-start.11
  121.3 5.1 copy-start.10
  230.1 59.7 %copy-start.5 = (f32[256,512]{1,0:T(8,128)S(1)}, f32[256,512]{1,0:T(8,128)}, u32[]{:S(2)}) copy-start(f32[256,512]{1,0:T(8,128)} %get-tuple-element.22) | copy-start | bytes 1572868
  258.7 33.5 %copy-start.9 = (bf16[512,512]{0,1:T(8,128)(2,1)S(1)}, bf16[512,512]{0,1:T(8,128)(2,1)}, u32[]{:S(2)}) copy-start(bf16[512,512]{0,1:T(8,128)(2,1)} %copy-done.8) | copy-start | bytes 1572868
  258.7 33.5 %copy-start.12 = (bf16[512,512]{0,1:T(8,128)(2,1)S(1)}, bf16[512,512]{0,1:T(8,128)(2,1)}, u32[]{:S(2)}) copy-start(bf16[512,512]{0,1:T(8,128)(2,1)} %copy-done.11) | copy-start | bytes 1572868
  258.7 33.5 %copy-start.14 = (bf16[512,512]{0,1:T(8,128)(2,1)S(1)}, bf16[512,512]{0,1:T(8,128)(2,1)}, u32[]{:S(2)}) copy-start(bf16[512,512]{0,1:T(8,128)(2,1)} %copy-done.13) | copy-start | bytes 1572868
  302.5 6.3 %copy-start.6 = (f32[256,512]{1,0:T(8,128)S(1)}, f32[256,512]{1,0:T(8,128)}, u32[]{:S(2)}) copy-start(f32[256,512]{1,0:T(8,128)} %get-tuple-element.22) | copy-start | bytes 1572868
  302.5 6.3 %copy-start.7 = (f32[256,512]{1,0:T(8,128)S(1)}, f32[256,512]{1,0:T(8,128)}, u32[]{:S(2)}) copy-start(f32[256,512]{1,0:T(8,128)} %get-tuple-element.24) | copy-start | bytes 1572868
  302.5 6.5 %copy-start.1 = (bf16[1920,512]{1,0:T(8,128)(2,1)S(1)}, bf16[1920,512]{1,0:T(8,128)(2,1)}, u32[]{:S(2)}) copy-start(bf16[1920,512]{1,0:T(8,128)(2,1)} %reshape.83) | copy-start | bytes 5898244
  304.3 9.2 %collective-permute-start.4 = (f32[512,512]{0,1:T(8,128)S(1)}, f32[512,512]{0,1:T(8,128)S(1)}, u32[]{:S(2)}, u32[]{:S(2)}) collective-permute-start(f32[512,512]{0,1:T(8,128)S(1)} %get-tuple-element.20), channel_id=1, source_target_pairs={{2,0},{4,2},{6,4},{8,6},{10,8},{12,10},{14,12},{16,14},{18,16},{20... | collective-permute-start | bytes 3145736 | tf_op jit(solution)/shard_map/ppermute | solution.py:19
  305.6 8.0 %collective-permute-start.3 = (f32[512,512]{0,1:T(8,128)S(1)}, f32[512,512]{0,1:T(8,128)S(1)}, u32[]{:S(2)}, u32[]{:S(2)}) collective-permute-start(f32[512,512]{0,1:T(8,128)S(1)} %get-tuple-element.19), channel_id=1, source_target_pairs={{0,2},{2,4},{4,6},{6,8},{8,10},{10,12},{12,14},{14,16},{16,18},{18... | collective-permute-start | bytes 3145736 | tf_op jit(solution)/shard_map/ppermute | solution.py:16
  313.6 1.0 copy-start.2
  369.5 204.1 %copy-start.3 = (f32[512,512]{0,1:T(8,128)S(1)}, f32[512,512]{0,1:T(8,128)}, u32[]{:S(2)}) copy-start(f32[512,512]{0,1:T(8,128)} %copy-done.2) | copy-start | bytes 3145732
  372.1 206.3 %collective-permute-start.2 = (bf16[1,512,960]{1,2,0:T(8,128)(2,1)}, bf16[1,512,960]{1,2,0:T(8,128)(2,1)}, u32[]{:S(2)}, u32[]{:S(2)}) collective-permute-start(bf16[1,512,960]{1,2,0:T(8,128)(2,1)} %fusion.2), channel_id=1, source_target_pairs={{0,384},{128,0},{256,128},{384,256},{1,385},{129,1},{257,129},{385... | collective-permute-start | bytes 2949128 | tf_op jit(solution)/shard_map/ppermute | solution.py:26
  528.8 17.3 %collective-permute-start.7 = (f32[32,512]{1,0:T(8,128)}, f32[32,512]{1,0:T(8,128)}, u32[]{:S(2)}, u32[]{:S(2)}) collective-permute-start(f32[32,512]{1,0:T(8,128)} %fusion), channel_id=1, source_target_pairs={{0,6},{2,8},{4,10},{6,12},{8,14},{10,16},{12,18},{14,20},{16,22},{... | collective-permute-start | bytes 196616
  531.3 14.8 %collective-permute-start.6 = (f32[32,512]{1,0:T(8,128)}, f32[32,512]{1,0:T(8,128)}, u32[]{:S(2)}, u32[]{:S(2)}) collective-permute-start(f32[32,512]{1,0:T(8,128)} %fusion), channel_id=1, source_target_pairs={{0,4},{2,6},{4,8},{6,10},{8,12},{10,14},{12,16},{14,18},{16,20},{1... | collective-permute-start | bytes 196616
  534.7 11.4 %collective-permute-start.5 = (f32[32,512]{1,0:T(8,128)}, f32[32,512]{1,0:T(8,128)}, u32[]{:S(2)}, u32[]{:S(2)}) collective-permute-start(f32[32,512]{1,0:T(8,128)} %fusion), channel_id=1, source_target_pairs={{0,2},{2,4},{4,6},{6,8},{8,10},{10,12},{12,14},{14,16},{16,18},{18... | collective-permute-start | bytes 196616
  539.7 6.4 %collective-permute-start.8 = (f32[30,512]{1,0:T(8,128)}, f32[30,512]{1,0:T(8,128)}, u32[]{:S(2)}, u32[]{:S(2)}) collective-permute-start(f32[30,512]{1,0:T(8,128)} %slice.15), channel_id=1, source_target_pairs={{0,8},{2,10},{4,12},{6,14},{8,16},{10,18},{12,20},{14,22},{16,24},... | collective-permute-start | bytes 184328
  (2 other events, 1.8 us)
Sparse Core Ops, SparseCore 0:
  11.4 87.3 all-gather.2
  124.3 105.7 all-reduce.6
where the time goes:
time: 593 us; the launch traced here: 588 us
  blocking collectives  195 us (33%)
  waiting for transfers between devices  192 us (32%)
  starting transfers between devices  73.4 us (12%)
  other arithmetic  66.6 us (11%)
  local copies, waits for them, and re-layouts  27.3 us (5%)
  matrix products  17.7 us (3%)
  between operations  15.6 us (3%)
    unnamed x1, blocking collectives  106 us
    psum x1, waiting for transfers between devices, local(): similarity_table = lax.psum(partial_scores, 'param')  102 us
    all_gather x1, waiting for transfers between devices, local(): full_w = lax.all_gather(w_proj, 'dp', axis=0, tiled=True)  87.9 us
    psum x1, blocking collectives, local(): drows = lax.psum(row_part, 'param').astype(jnp.bfloat16)  52.4 us
    ppermute x1, starting transfers between devices, from_behind(): lax.ppermute(value, axis, [(i, (i + by) % peers) for i in range(peers)])  50.7 us
    reduce_sum x1, other arithmetic, spread_columns(): return jnp.sum(jnp.where(hits, values[:, :, None], 0.0), axis=1)  31 us
    reduce_sum x1, other arithmetic, pick_columns(): return jnp.sum(jnp.where(hits, table[:, None, :], 0.0), axis=2)  28.6 us
    unnamed x39, local copies, waits for them, and re-layouts  25.5 us
  transfers between devices with their start and end apart: 11, of which 3 were waited for; matrix products, arithmetic and copies ran while one was open for 23% of the time, Pallas kernels for 0%

commit v1 on v0

v1 whole, which is shorter than its diff:
```python
import jax
import jax.numpy as jnp
from jax import lax
from jax.experimental import pallas as pl
from jax.experimental.pallas import tpu as pltpu
from jax.sharding import PartitionSpec as P

sharpness_divisor = 0.1
loss_multiplier = 32.0
epsilon = 1e-06

F32 = jnp.float32
BF16 = jnp.bfloat16
I32 = jnp.int32

LANES = 128
SLOTS = 256
FRAMES = 512
WINDOW = 3 * FRAMES
TILES = WINDOW // LANES
COLUMNS = 101
SPARE = LANES - 1
MODEL = 1920
FEATS = 512
BLOCK = 30
PAD = 32
PEERS = 32
HALF = PEERS * PAD


def iota(shape, dim):
    return lax.broadcasted_iota(I32, shape, dim)


def one_hot(hits):
    return jnp.where(hits, 1.0, 0.0).astype(BF16)


def dot(left, right):
    return jnp.dot(left, right, preferred_element_type=F32)


def dot_cols(left, right):
    return lax.dot_general(left, right, (((1,), (1,)), ((), ())), preferred_element_type=F32)


def dot_rows(left, right):
    return lax.dot_general(left, right, (((0,), (0,)), ((), ())), preferred_element_type=F32)


def lookup(table, index):
    return jnp.take_along_axis(table, index, axis=1, mode="promise_in_bounds")


def call(body, outs, n_scalars, n_arrays, scratch=(), flops=0, bytes_accessed=0):
    return pl.pallas_call(
        body,
        out_shape=tuple(jax.ShapeDtypeStruct(shape, dtype) for shape, dtype in outs),
        in_specs=[pl.BlockSpec(memory_space=pltpu.SMEM)] * n_scalars
        + [pl.BlockSpec(memory_space=pltpu.VMEM)] * n_arrays,
        out_specs=tuple(pl.BlockSpec(memory_space=pltpu.VMEM) for _ in outs),
        scratch_shapes=list(scratch),
        compiler_params=pltpu.CompilerParams(vmem_limit_bytes=32 * 1024 * 1024),
        cost_estimate=pl.CostEstimate(
            flops=flops, bytes_accessed=bytes_accessed, transcendentals=0
        ),
    )


def rows_body(core_ref, pos_ref, hidden_ref, own_ref, other_ref, own_t_ref, other_t_ref):
    chosen = one_hot(pos_ref[...] == iota((SLOTS, FRAMES), 1))
    rows = dot(chosen, hidden_ref[...]).astype(BF16)
    core = core_ref[0]
    step = 256
    for parity, straight, turned in ((core, own_ref, own_t_ref), (1 - core, other_ref, other_t_ref)):
        for k in range(HALF // step):
            low = (2 * BLOCK * step // PAD * k) // LANES * LANES
            wide = min(MODEL, low + 640) - low
            piece = rows[:, low : low + wide]
            q = iota((step, wide), 0) + step * k
            wanted = BLOCK * (2 * (q >> 5) + parity) + (q & 31)
            spread = one_hot((wanted == iota((step, wide), 1) + low) & ((q & 31) < BLOCK))
            straight[:, step * k : step * (k + 1)] = dot_cols(piece, spread).astype(BF16)
            turned[step * k : step * (k + 1), :] = dot_cols(spread, piece).astype(BF16)


def index_body(frame_ref, column_ref, times_ref):
    lane = iota((8, LANES), 1)
    tiles = [lane + LANES * t for t in range(TILES)]

    def group(g, carry):
        rows = pl.ds(pl.multiple_of(g * 8, 8), 8)
        frame = frame_ref[rows, :]
        found = [jnp.full((8, LANES), SPARE, I32) for _ in range(TILES)]
        times = jnp.zeros((8, LANES), F32)
        for c in range(COLUMNS):
            this = jnp.broadcast_to(frame[:, c : c + 1], (8, LANES))
            times = times + jnp.where(frame == this, 1.0, 0.0)
            for t in range(TILES):
                found[t] = jnp.where(this == tiles[t], c, found[t])
        for t in range(TILES):
            column_ref[rows, LANES * t : LANES * (t + 1)] = found[t]
        times_ref[rows, :] = times
        return carry

    lax.fori_loop(0, SLOTS // 8, group, 0)


def score_body(own_ref, other_ref, w_own_ref, w_other_ref, window_ref, frame_ref, norm_ref, sent_ref, context_ref, table_ref):
    context = dot(own_ref[...], w_own_ref[...]) + dot(other_ref[...], w_other_ref[...])
    context_ref[...] = context
    table_ref[...] = dot_cols(context.astype(BF16), window_ref[...])
    sent_ref[0:SLOTS, :] = jnp.broadcast_to(
        jnp.sum(context * context, axis=1, keepdims=True), (SLOTS, LANES)
    )
    sent_ref[SLOTS : SLOTS + 16, :] = norm_ref[...]
    lane = iota((16, LANES), 1)

    def group(g, carry):
        rows = pl.ds(pl.multiple_of(g * 16, 16), 16)
        frame = frame_ref[rows, :]
        tile, place = frame >> 7, frame & 127
        picked = jnp.where(lane == COLUMNS, sent_ref[rows, :], 0.0)
        for t in range(TILES):
            found = lookup(table_ref[rows, LANES * t : LANES * (t + 1)], place)
            picked = jnp.where((tile == t) & (lane < COLUMNS), found, picked)
        sent_ref[rows, :] = picked
        return carry

    lax.fori_loop(0, SLOTS // 16, group, 0)


def slots_body(
    count_ref, sent_ref, got_ref, context_ref, frame_ref, times_ref, column_ref, window_ref,
    dctx_ref, unit_ref, step_ref, along_ref, inverse_ref, shift_ref, scores_ref,
):
    inv_tgt = 1.0 / jnp.sqrt(
        sent_ref[SLOTS : SLOTS + 16, :] + got_ref[SLOTS : SLOTS + 16, :] + epsilon
    )
    lane = iota((16, LANES), 1)
    named = lane < COLUMNS
    count = count_ref[0]

    def group(g, carry):
        rows = pl.ds(pl.multiple_of(g * 16, 16), 16)
        raw = sent_ref[rows, :] + got_ref[rows, :]
        inverse = 1.0 / jnp.sqrt(raw[:, COLUMNS : COLUMNS + 1] + epsilon)
        frame = frame_ref[rows, :]
        tile, place = frame >> 7, frame & 127
        scale = jnp.zeros((16, LANES), F32)
        for t in range(TILES):
            line = jnp.broadcast_to(inv_tgt[t : t + 1, :], (16, LANES))
            scale = jnp.where(tile == t, lookup(line, place), scale)
        logits = raw * inverse * scale / sharpness_divisor
        expon = jnp.where(named, jnp.exp(jnp.where(named, logits, 0.0)), 0.0)
        probs = expon / jnp.sum(expon, axis=1, keepdims=True)
        live = iota((16, LANES), 0) + g * 16 < count
        first = jnp.where(lane == 0, 1.0, 0.0)
        step = jnp.where(live & named, loss_multiplier * (probs - first) / sharpness_divisor, 0.0)
        times = jnp.maximum(times_ref[rows, :], 1.0)
        step = step * times
        weight = (step * scale).astype(BF16).astype(F32)
        along = jnp.sum(jnp.where(named, weight * raw / times, 0.0), axis=1, keepdims=True)
        step_ref[rows, :] = step
        along_ref[rows, :] = jnp.where(named, step.astype(BF16).astype(F32) * raw * inverse, 0.0)
        inverse_ref[rows, :] = jnp.broadcast_to(inverse, (16, LANES))
        shift_ref[rows, :] = jnp.broadcast_to(along * inverse * inverse * inverse, (16, LANES))
        for t in range(TILES):
            span = slice(LANES * t, LANES * (t + 1))
            scores_ref[rows, span] = lookup(weight, column_ref[rows, span]).astype(BF16)
        return carry

    lax.fori_loop(0, SLOTS // 16, group, 0)
    context = context_ref[...]
    inverse = inverse_ref[:, 0:1]
    dunit = dot(scores_ref[...], window_ref[...])
    dctx_ref[...] = (dunit * inverse - context * shift_ref[:, 0:1]).astype(BF16)
    unit_ref[...] = (context * inverse).astype(BF16)


def frames_body(step_ref, along_ref, column_ref, unit_ref, low_ref, own_ref, high_ref, line_ref, scores_ref, sums_ref):
    sums_ref[...] = jnp.zeros((16, WINDOW), F32)

    def group(g, carry):
        rows = pl.ds(pl.multiple_of(g * 16, 16), 16)
        step = step_ref[rows, :]
        along = along_ref[rows, :]
        for t in range(TILES):
            span = slice(LANES * t, LANES * (t + 1))
            index = column_ref[rows, span]
            scores_ref[rows, span] = lookup(step, index).astype(BF16)
            sums_ref[:, span] += lookup(along, index)
        return carry

    lax.fori_loop(0, SLOTS // 16, group, 0)
    line = jnp.sum(sums_ref[...], axis=0, keepdims=True)
    line_ref[...] = jnp.broadcast_to(line[:, FRAMES : 2 * FRAMES], (8, FRAMES))
    row = iota((16, FRAMES), 0)
    for part, ref in ((0, low_ref), (1, own_ref), (2, high_ref)):
        span = slice(FRAMES * part, FRAMES * (part + 1))
        ref[0:FRAMES, :] = dot_rows(scores_ref[:, span], unit_ref[...]).astype(ref.dtype)
        if part != 1:
            left = jnp.broadcast_to(line[:, span], (16, FRAMES))
            first = left.astype(BF16).astype(F32)
            second = (left - first).astype(BF16).astype(F32)
            third = left - first - second
            ref[FRAMES : FRAMES + 16, :] = jnp.where(
                row == 0, first, jnp.where(row == 1, second, jnp.where(row == 2, third, 0.0))
            ).astype(BF16)


def drows_body(half_ref, dctx_ref, w_own_ref, w_other_ref, same_ref, cross_ref):
    half = half_ref[0]
    dctx = dctx_ref[...]
    for ref, which in ((same_ref, half), (cross_ref, 1 - half)):
        rows = pl.ds(pl.multiple_of(which * (HALF // 2), HALF // 2), HALF // 2)
        ref[:, 0 : HALF // 2] = dot_cols(dctx, w_own_ref[rows, :]).astype(BF16)
        ref[:, HALF // 2 : HALF] = dot_cols(dctx, w_other_ref[rows, :]).astype(BF16)


def spread_body(core_ref, pos_ref, same_ref, cross_ref, out_ref):
    core = core_ref[0]
    drows = (same_ref[...].astype(F32) + cross_ref[...].astype(F32)).astype(BF16)
    q = iota((HALF, MODEL // 2), 0)
    parity = jnp.where(q < HALF // 2, core, 1 - core)
    wanted = BLOCK * (2 * ((q >> 5) & 15) + parity) + (q & 31)
    unpad = one_hot((wanted == iota((HALF, MODEL // 2), 1)) & ((q & 31) < BLOCK))
    rows = dot(drows, unpad).astype(BF16)
    placed = one_hot(iota((FRAMES, SLOTS), 0) == pos_ref[...])
    out_ref[...] = dot(placed, rows).astype(BF16)


def local(hidden, targets, w_proj, mask_counts, mask_pos, negatives):
    shard = lax.axis_index("dp")
    core = (shard % 2).astype(I32).reshape(1)
    half = lax.axis_index("param").astype(I32).reshape(1)
    n_dp = lax.axis_size("dp")
    n_pipe = lax.axis_size("pipe")
    peers = [[2 * i + c for i in range(n_dp // 2)] for c in range(2)]
    swap = [(i, i ^ 1) for i in range(n_dp)]
    upward = [(i, i + 1) for i in range(n_dp - 1)]
    downward = [(i + 1, i) for i in range(n_dp - 1)]
    back = [(i, (i - 1) % n_pipe) for i in range(n_pipe)]
    back_across = [
        (2 * i + a, 2 * ((i - 1) % n_pipe) + 1 - a) for i in range(n_pipe) for a in range(2)
    ]

    w_block = jnp.pad(w_proj, ((0, PAD - BLOCK), (0, 0)))
    w_own = lax.all_to_all(
        jnp.broadcast_to(w_block[None], (PEERS, PAD, FEATS)), "dp", 0, 0, axis_index_groups=peers, tiled=True
    ).reshape(HALF, FEATS)
    w_other = lax.ppermute(w_own, "dp", swap)

    own_targets = targets[0]
    low = lax.ppermute(own_targets, "dp", upward)
    high = lax.ppermute(own_targets, "dp", downward)
    positions = mask_pos[0, 0] - shard * FRAMES
    next_positions = lax.ppermute(positions, "pipe", back)

    frames = jnp.concatenate([mask_pos[0, 0][None, :], negatives[0, 0]], axis=0) - (shard - 1) * FRAMES
    frames = jnp.pad(frames, ((0, LANES - COLUMNS), (0, 0)), constant_values=-1).T

    rows_own, rows_other, turned_own, turned_other = call(
        rows_body,
        [((SLOTS, HALF), BF16)] * 2 + [((HALF, SLOTS), BF16)] * 2,
        1, 2, flops=3 * 10**9, bytes_accessed=4 * 10**6,
    )(core, positions[:, None], hidden[0])
    turned_got = lax.ppermute(turned_other, "dp", swap)

    column, times = call(
        index_body, [((SLOTS, WINDOW), I32), ((SLOTS, LANES), F32)], 0, 1,
        flops=10**10, bytes_accessed=2 * 10**6,
    )(frames)

    window = jnp.concatenate([low, own_targets, high], axis=0)
    window_f = window.astype(F32)
    norms = jnp.sum(window_f * window_f, axis=1).reshape(TILES, LANES)
    norms = jnp.pad(norms, ((0, 16 - TILES), (0, 0)))

    sent, context = call(
        score_body, [((SLOTS + 16, LANES), F32), ((SLOTS, FEATS), F32)], 0, 7,
        scratch=[pltpu.VMEM((SLOTS, WINDOW), F32)], flops=10**9, bytes_accessed=6 * 10**6,
    )(rows_own, rows_other, w_own, w_other, window, frames, norms)
    got = lax.ppermute(sent, "param", [(0, 1), (1, 0)])

    dctx, unit, step, along = call(
        slots_body,
        [((SLOTS, FEATS), BF16)] * 2 + [((SLOTS, LANES), F32)] * 2,
        1, 7,
        scratch=[pltpu.VMEM((SLOTS, LANES), F32)] * 2 + [pltpu.VMEM((SLOTS, WINDOW), BF16)],
        flops=5 * 10**8, bytes_accessed=5 * 10**6,
    )(mask_counts[0], sent, got, context, frames, times, column, window)
    dctx_got = lax.ppermute(dctx, "dp", swap)

    share = (dot(turned_own, dctx) + dot(turned_got, dctx_got)).astype(BF16)
    shares = lax.all_to_all(
        share.reshape(PEERS, PAD, FEATS), "dp", 0, 0, axis_index_groups=peers, tiled=True
    )
    grad_w = jnp.sum(shares.astype(F32), axis=0)
    grad_w = grad_w + lax.ppermute(grad_w, "pipe", [(i, i ^ 1) for i in range(n_pipe)])
    grad_w = grad_w + lax.ppermute(grad_w, "pipe", [(i, i ^ 2) for i in range(n_pipe)])

    same, cross = call(
        drows_body, [((SLOTS, HALF), BF16)] * 2, 1, 3, flops=10**9, bytes_accessed=3 * 10**6
    )(half, dctx, w_own, w_other)
    same = lax.ppermute(same, "pipe", back)
    cross = lax.ppermute(cross, ("pipe", "param"), back_across)
    (upstream,) = call(
        spread_body, [((FRAMES, MODEL // 2), BF16)], 1, 3, flops=10**9, bytes_accessed=2 * 10**6
    )(core, next_positions[None, :], same, cross)

    to_low, dtgt, to_high, line = call(
        frames_body,
        [((FRAMES + 16, FEATS), BF16), ((FRAMES, FEATS), F32), ((FRAMES + 16, FEATS), BF16), ((8, FRAMES), F32)],
        0, 4,
        scratch=[pltpu.VMEM((SLOTS, WINDOW), BF16), pltpu.VMEM((16, WINDOW), F32)],
        flops=5 * 10**8, bytes_accessed=5 * 10**6,
    )(step, along, column, unit)
    from_low = lax.ppermute(to_high, "dp", upward).astype(F32)
    from_high = lax.ppermute(to_low, "dp", downward).astype(F32)
    dtgt = dtgt + from_low[:FRAMES] + from_high[:FRAMES]
    line = line[0] + jnp.sum(from_low[FRAMES:], axis=0) + jnp.sum(from_high[FRAMES:], axis=0)
    inv_tgt = 1.0 / jnp.sqrt((sent + got)[SLOTS + 4 : SLOTS + 8].reshape(FRAMES) + epsilon)
    grad_t = dtgt * inv_tgt[:, None] - own_targets.astype(F32) * (line * inv_tgt**3)[:, None]
    return (grad_w[:BLOCK], upstream[None], grad_t.astype(BF16)[None])


def solution(mesh):
    return jax.shard_map(
        local,
        mesh=mesh,
        in_specs=(
            P("pipe", "dp", None),
            P("pipe", "dp", "param"),
            P("dp", "param"),
            P("pipe", "dp"),
            P("pipe", "dp", None),
            P("pipe", "dp", None, None),
        ),
        out_specs=(P("dp", "param"), P("pipe", "dp", "param"), P("pipe", "dp", "param")),
        check_vma=False,
    )
```

time: 593 us -> 173 us (0.29)
  waiting for transfers between devices: 192 us -> 31.6 us
  blocking collectives: 195 us -> 41 us
  other arithmetic: 66.6 us -> 10.1 us
  Pallas kernels: 0 us -> 33.2 us
  starting transfers between devices: 73.4 us -> 45.4 us
  local copies, waits for them, and re-layouts: 27.3 us -> 6.17 us
  matrix products: 17.7 us -> 2.91 us
  between operations: 15.6 us -> 1.76 us
    unnamed x1 -> x0, blocking collectives: 106 us -> none
    psum x1 -> x0, waiting for transfers between devices: 102 us -> none  [local(): similarity_table = lax.psum(partial_scores, 'param')]
    psum x4 -> x0, blocking collectives: 88.7 us -> none  [the longest x1 52.4 us: local(): drows = lax.psum(row_part, 'param').astype(jnp.bfloat16)]
    all_gather x1 -> x0, waiting for transfers between devices: 87.9 us -> none  [local(): full_w = lax.all_gather(w_proj, 'dp', axis=0, tiled=True)]
    reduce_sum x5 -> x4, other arithmetic: 61.3 us -> 3.92 us  [the longest x1 1.74 us: local(): norms = jnp.sum(window_f * window_f, axis=1).reshape(TILES, LANES)]
    all_to_all x0 -> x1, blocking collectives: none -> 41 us  [local(): lax.all_to_all(jnp.broadcast_to(w_block[None], (PEERS, PAD, FEATS)), 'dp'...]
    pallas_call x0 -> x7, Pallas kernels: none -> 33.2 us  [the longest x1 14.1 us: local(): call(index_body, [((SLOTS, WINDOW), I32), ((SLOTS, LANES), F32)], 0, 1, f...]
    ppermute x5 -> x13, waiting for transfers between devices: 1.46 us -> 31.6 us  [the longest x1 24.1 us: local(): next_positions = lax.ppermute(positions, 'pipe', back)]
  transfers between devices with their start and end apart: 11 -> 14, of which waited for: 3 -> 4; matrix products, arithmetic and copies ran while one was open for 23% -> 6% of each run, Pallas kernels for 0% -> 19%
where the time goes in v1:
time: 173 us; the launch traced here: 172 us
  starting transfers between devices  45.4 us (26%)
  blocking collectives  41 us (24%)
  Pallas kernels  33.2 us (19%)
  waiting for transfers between devices  31.6 us (18%)
  other arithmetic  10.1 us (6%)
  local copies, waits for them, and re-layouts  6.17 us (4%)
  matrix products  2.91 us (2%)
  between operations  1.76 us (1%)
    all_to_all x1, blocking collectives, local(): lax.all_to_all(jnp.broadcast_to(w_block[None], (PEERS, PAD, FEATS)), 'dp'...  41 us
    ppermute x1, waiting for transfers between devices, local(): next_positions = lax.ppermute(positions, 'pipe', back)  24.1 us
    pallas_call x1, Pallas kernels, local(): call(index_body, [((SLOTS, WINDOW), I32), ((SLOTS, LANES), F32)], 0, 1, f...  14.1 us
    all_to_all x1, starting transfers between devices, local(): lax.all_to_all(share.reshape(PEERS, PAD, FEATS), 'dp', 0, 0, axis_index_g...  8.96 us
    pallas_call x1, Pallas kernels, local(): call(slots_body, [((SLOTS, FEATS), BF16)] * 2 + [((SLOTS, LANES), F32)] *...  6.74 us
    unnamed x30, local copies, waits for them, and re-layouts  5 us
    ppermute x1, starting transfers between devices, local(): cross = lax.ppermute(cross, ('pipe', 'param'), back_across)  4.92 us
    ppermute x1, starting transfers between devices, local(): got = lax.ppermute(sent, 'param', [(0, 1), (1, 0)])  4.71 us
  transfers between devices with their start and end apart: 14, of which 4 were waited for; matrix products, arithmetic and copies ran while one was open for 6% of the time, Pallas kernels for 19%

profile of v1, /device:TPU:56, one launch (start us, length us, event | category | flops | bytes accessed | tf_op | source)
XLA Modules:
  0.0 172.2 jit_solution(15122321714130104559)
XLA Ops:
  1.5 41.0 %all_to_all.10 = bf16[32,32,512]{2,1,0:T(8,128)(2,1)S(1)} all-to-all(bf16[32,32,512]{2,1,0:T(8,128)(2,1)S(1)} %broadcast_in_dim.8), channel_id=1, replica_groups={{0,4,8,12,16,20,24,28,32,36,40,44,48,52,56,60,64,68,72,76,80,84,88,92,9..., dimensions={0} | all-to-all | bytes 2097152 | tf_op jit(solution)/shard_map/all_to_all | solution.py:249
  42.6 1.9 %collective-permute-start = (bf16[1024,512]{1,0:T(8,128)(2,1)S(1)}, bf16[1024,512]{1,0:T(8,128)(2,1)S(1)}, u32[]{:S(2)}, u32[]{:S(2)}) collective-permute-start(bf16[1024,512]{1,0:T(8,128)(2,1)S(1)} %bitcast.29), channel_id=1, source_target_pairs={{0,2},{2,0},{4,6},{6,4},{8,10},{10,8},{12,14},{14,12},{16,18},{18,... | collective-permute-start | bytes 3145736 | tf_op jit(solution)/shard_map/ppermute | solution.py:252
  44.5 3.2 %collective-permute-start.1 = (bf16[512,512]{1,0:T(8,128)(2,1)}, bf16[512,512]{1,0:T(8,128)(2,1)}, u32[]{:S(2)}, u32[]{:S(2)}) collective-permute-start(bf16[512,512]{1,0:T(8,128)(2,1)} %bitcast.5), channel_id=1, source_target_pairs={{0,2},{2,4},{4,6},{6,8},{8,10},{10,12},{12,14},{14,16},{16,18},{18... | collective-permute-start | bytes 1572872 | tf_op jit(solution)/shard_map/ppermute | solution.py:255
  49.2 1.5 copy-done.11
  50.7 3.1 %shard_map.85 = (bf16[256,1024]{1,0:T(8,128)(2,1)S(1)}, bf16[256,1024]{1,0:T(8,128)(2,1)S(1)}, bf16[1024,256]{1,0:T(8,128)(2,1)S(1)}, bf16[1024,256]{1,0:T(8,128)(2,1)}) custom-call(s32[1]{0:T(128)} %bitcast.core_ref, s32[256,1]{1,0:T(8,128)S(1)} %copy.11.pos_ref, bf16[512,1920]{1,0:T(8,128)(2,1)S(1)} %bitcast.33), custom_call_target="tpu_custom_call" | custom-call | flops 3000000000 | bytes 4000000 | tf_op jit(solution)/shard_map/pallas_call | solution.py:263
  54.6 3.1 %collective-permute-start.4 = (bf16[1024,256]{1,0:T(8,128)(2,1)}, bf16[1024,256]{1,0:T(8,128)(2,1)}, u32[]{:S(2)}, u32[]{:S(2)}) collective-permute-start(bf16[1024,256]{1,0:T(8,128)(2,1)} %get-tuple-element.29), channel_id=1, source_target_pairs={{0,2},{2,0},{4,6},{6,4},{8,10},{10,8},{12,14},{14,12},{16,18},{18,... | collective-permute-start | bytes 1572872 | tf_op jit(solution)/shard_map/ppermute | solution.py:268
  58.2 1.7 %multiply_reduce_fusion = (f32[1536]{0:T(1024)S(1)}, bf16[1536,512]{1,0:T(8,128)(2,1)S(1)}) fusion(bf16[512,512]{1,0:T(8,128)(2,1)} %collective-permute-done.2, bf16[512,512]{1,0:T(8,128)(2,1)} %bitcast.5, bf16[512,512]{1,0:T(8,128)(2,1)} %collective-permute-done.1), kind=kLoop, calls=%fused_computation | loop fusion | flops 7076352 | bytes 3151872 | tf_op jit(solution)/shard_map/reduce_sum | solution.py:277
  60.0 2.8 %shard_map.86 = (f32[272,128]{1,0:T(8,128)S(1)}, f32[256,512]{1,0:T(8,128)S(1)}) custom-call(bf16[256,1024]{1,0:T(8,128)(2,1)S(1)} %get-tuple-element.22.own_ref, bf16[256,1024]{1,0:T(8,128)(2,1)S(1)} %copy-done.3, bf16[1024,512]{1,0:T(8,128)(2,1)S(1)} %bitcast.30, bf16[1024,512]{1,0:T(8,128)(2,1)S(1)} %collective-permute-done.w_other_ref, ...), custom_call_target="tpu_custom_call" | custom-call | flops 1000000000 | bytes 6000000 | tf_op jit(solution)/shard_map/pallas_call | solution.py:280
  62.8 4.7 %collective-permute-start.3 = (f32[272,128]{1,0:T(8,128)S(1)}, f32[272,128]{1,0:T(8,128)S(1)}, u32[]{:S(2)}, u32[]{:S(2)}) collective-permute-start(f32[272,128]{1,0:T(8,128)S(1)} %get-tuple-element.24.sent_ref), channel_id=1, source_target_pairs={{0,1},{1,0},{2,3},{3,2},{4,5},{5,4},{6,7},{7,6},{8,9},{9,8},{10,11... | collective-permute-start | bytes 417800 | tf_op jit(solution)/shard_map/ppermute | solution.py:284
  67.5 14.1 %shard_map.87 = (s32[256,1536]{1,0:T(8,128)S(1)}, f32[256,128]{1,0:T(8,128)S(1)}) custom-call(s32[256,128]{1,0:T(8,128)S(1)} %pad_bitcast_fusion.frame_ref), custom_call_target="tpu_custom_call" | custom-call | flops 10000000000 | bytes 2000000 | tf_op jit(solution)/shard_map/pallas_call | solution.py:270
  82.3 6.7 %shard_map.88 = (bf16[256,512]{1,0:T(8,128)(2,1)S(1)}, bf16[256,512]{1,0:T(8,128)(2,1)S(1)}, f32[256,128]{1,0:T(8,128)S(1)}, f32[256,128]{1,0:T(8,128)S(1)}) custom-call(s32[1]{0:T(128)} %bitcast.28.count_ref, f32[272,128]{1,0:T(8,128)S(1)} %get-tuple-element.24.sent_ref, f32[272,128]{1,0:T(8,128)S(1)} %collective-permute-done.3.got_ref, ...), custom_call_target="tpu_custom_call" | custom-call | flops 500000000 | bytes 5000000 | tf_op jit(solution)/shard_map/pallas_call | solution.py:286
  89.1 2.6 %collective-permute-start.5 = (bf16[256,512]{1,0:T(8,128)(2,1)S(1)}, bf16[256,512]{1,0:T(8,128)(2,1)S(1)}, u32[]{:S(2)}, u32[]{:S(2)}) collective-permute-start(bf16[256,512]{1,0:T(8,128)(2,1)S(1)} %get-tuple-element.28.dctx_ref), channel_id=1, source_target_pairs={{0,2},{2,0},{4,6},{6,4},{8,10},{10,8},{12,14},{14,12},{16,18},{18,... | collective-permute-start | bytes 786440 | tf_op jit(solution)/shard_map/ppermute | solution.py:293
  95.8 9.0 %all-to-all-start.1 = ((bf16[32,32,512]{2,1,0:T(8,128)(2,1)}), bf16[32,32,512]{2,1,0:T(8,128)(2,1)}, u32[]{:S(2)}, u32[]{:S(2)}) async-start(bf16[32,32,512]{2,1,0:T(8,128)(2,1)} %bitcast.35), calls=%async_computation.1 | async-start | bytes 2097152 | tf_op jit(solution)/shard_map/all_to_all | solution.py:296
  106.8 4.9 %collective-permute-start.10 = (bf16[256,1024]{1,0:T(8,128)(2,1)S(1)}, bf16[256,1024]{1,0:T(8,128)(2,1)S(1)}, u32[]{:S(2)}, u32[]{:S(2)}) collective-permute-start(bf16[256,1024]{1,0:T(8,128)(2,1)S(1)} %get-tuple-element.31), channel_id=1, source_target_pairs={{0,385},{1,384},{128,1},{129,0},{256,129},{257,128},{384,257},{385... | collective-permute-start | bytes 1572872 | tf_op jit(solution)/shard_map/ppermute | solution.py:307
  111.7 3.2 %collective-permute-start.9 = (bf16[256,1024]{1,0:T(8,128)(2,1)S(1)}, bf16[256,1024]{1,0:T(8,128)(2,1)S(1)}, u32[]{:S(2)}, u32[]{:S(2)}) collective-permute-start(bf16[256,1024]{1,0:T(8,128)(2,1)S(1)} %get-tuple-element.30), channel_id=1, source_target_pairs={{0,384},{128,0},{256,128},{384,256},{1,385},{129,1},{257,129},{385... | collective-permute-start | bytes 1572872 | tf_op jit(solution)/shard_map/ppermute | solution.py:306
  115.0 4.5 %shard_map.91 = (bf16[528,512]{1,0:T(8,128)(2,1)}, f32[512,512]{1,0:T(8,128)S(1)}, bf16[528,512]{1,0:T(8,128)(2,1)}, f32[8,512]{1,0:T(8,128)S(1)}) custom-call(f32[256,128]{1,0:T(8,128)S(1)} %copy-done.8, f32[256,128]{1,0:T(8,128)S(1)} %copy-done.10, s32[256,1536]{1,0:T(8,128)S(1)} %get-tuple-element.27.column_ref, ...), custom_call_target="tpu_custom_call" | custom-call | flops 500000000 | bytes 5000000 | tf_op jit(solution)/shard_map/pallas_call | solution.py:312
  120.8 3.1 %collective-permute-start.11 = (bf16[528,512]{1,0:T(8,128)(2,1)}, bf16[528,512]{1,0:T(8,128)(2,1)S(1)}, u32[]{:S(2)}, u32[]{:S(2)}) collective-permute-start(bf16[528,512]{1,0:T(8,128)(2,1)} %get-tuple-element.36), channel_id=1, source_target_pairs={{0,2},{2,4},{4,6},{6,8},{8,10},{10,12},{12,14},{14,16},{16,18},{18... | collective-permute-start | bytes 1622024 | tf_op jit(solution)/shard_map/ppermute | solution.py:319
  123.9 3.3 %collective-permute-start.8 = (s32[256]{0:T(256)S(1)}, s32[256]{0:T(256)S(1)}, u32[]{:S(2)}, u32[]{:S(2)}) collective-permute-start(s32[256]{0:T(256)S(1)} %bitcast.40), channel_id=1, source_target_pairs={{0,384},{128,0},{256,128},{384,256},{1,385},{129,1},{257,129},{385... | collective-permute-start | bytes 3080 | tf_op jit(solution)/shard_map/ppermute | solution.py:258
  127.2 24.1 %collective-permute-done.8 = s32[256]{0:T(256)S(1)} collective-permute-done((s32[256]{0:T(256)S(1)}, s32[256]{0:T(256)S(1)}, u32[]{:S(2)}, u32[]{:S(2)}) %collective-permute-start.8) | collective-permute-done | bytes 1056 | tf_op jit(solution)/shard_map/ppermute | solution.py:258
  158.2 1.9 %collective-permute-start.6 = (f32[32,512]{1,0:T(8,128)S(1)}, f32[32,512]{1,0:T(8,128)S(1)}, u32[]{:S(2)}, u32[]{:S(2)}) collective-permute-start(f32[32,512]{1,0:T(8,128)S(1)} %convert_reduce_fusion), channel_id=1, source_target_pairs={{0,128},{128,0},{256,384},{384,256},{1,129},{129,1},{257,385},{385... | collective-permute-start | bytes 196616 | tf_op jit(solution)/shard_map/ppermute | solution.py:300
  160.8 3.5 %collective-permute-done.6 = f32[32,512]{1,0:T(8,128)S(1)} collective-permute-done((f32[32,512]{1,0:T(8,128)S(1)}, f32[32,512]{1,0:T(8,128)S(1)}, u32[]{:S(2)}, u32[]{:S(2)}) %collective-permute-start.6) | collective-permute-done | bytes 65568 | tf_op jit(solution)/shard_map/ppermute | solution.py:300
  164.4 1.9 %collective-permute-start.7 = (f32[32,512]{1,0:T(8,128)S(1)}, f32[32,512]{1,0:T(8,128)S(1)}, u32[]{:S(2)}, u32[]{:S(2)}) collective-permute-start(f32[32,512]{1,0:T(8,128)S(1)} %add.59), channel_id=1, source_target_pairs={{0,256},{128,384},{256,0},{384,128},{1,257},{129,385},{257,1},{385... | collective-permute-start | bytes 196616 | tf_op jit(solution)/shard_map/ppermute | solution.py:301
  166.3 2.4 %fusion.3 = bf16[1,512,512]{2,1,0:T(8,128)(2,1)} fusion(f32[528,512]{1,0:T(8,128)S(1)} %convert_element_type.29, f32[512,512]{1,0:T(8,128)S(1)} %get-tuple-element.35, f32[528,512]{1,0:T(8,128)} %convert_element_type.28, f32[512]{0:T(512)S(1)} %get-tuple-element.45, f32[512]{0:T(512)S(1)} %get-tuple-element.46, bf16[1,512,512]{2,1,0:T(8,128)(2,1)} %param.7), kind=kLoop, calls=%fused_computation.9 | loop fusion | flops 1835008 | bytes 4198400 | tf_op jit(solution)/shard_map/broadcast_in_dim | solution.py:325
  168.8 2.8 %collective-permute-done.7 = f32[32,512]{1,0:T(8,128)S(1)} collective-permute-done((f32[32,512]{1,0:T(8,128)S(1)}, f32[32,512]{1,0:T(8,128)S(1)}, u32[]{:S(2)}, u32[]{:S(2)}) %collective-permute-start.7) | collective-permute-done | bytes 65568 | tf_op jit(solution)/shard_map/ppermute | solution.py:301
  (64 shorter events, 19.1 us)
Async XLA Ops:
  0.6 48.4 %copy-start.13 = (s32[1,1,256]{2,1,0:T(1,128)S(1)}, s32[1,1,256]{2,1,0:T(1,128)}, u32[]{:S(2)}) copy-start(s32[1,1,256]{2,1,0:T(1,128)} %param.10) | copy-start | bytes 3076
  42.6 17.3 %collective-permute-start = (bf16[1024,512]{1,0:T(8,128)(2,1)S(1)}, bf16[1024,512]{1,0:T(8,128)(2,1)S(1)}, u32[]{:S(2)}, u32[]{:S(2)}) collective-permute-start(bf16[1024,512]{1,0:T(8,128)(2,1)S(1)} %bitcast.29), channel_id=1, source_target_pairs={{0,2},{2,0},{4,6},{6,4},{8,10},{10,8},{12,14},{14,12},{16,18},{18,... | collective-permute-start | bytes 3145736 | tf_op jit(solution)/shard_map/ppermute | solution.py:252
  44.5 13.7 %collective-permute-start.1 = (bf16[512,512]{1,0:T(8,128)(2,1)}, bf16[512,512]{1,0:T(8,128)(2,1)}, u32[]{:S(2)}, u32[]{:S(2)}) collective-permute-start(bf16[512,512]{1,0:T(8,128)(2,1)} %bitcast.5), channel_id=1, source_target_pairs={{0,2},{2,4},{4,6},{6,8},{8,10},{10,12},{12,14},{14,16},{16,18},{18... | collective-permute-start | bytes 1572872 | tf_op jit(solution)/shard_map/ppermute | solution.py:255
  47.7 10.5 %collective-permute-start.2 = (bf16[512,512]{1,0:T(8,128)(2,1)}, bf16[512,512]{1,0:T(8,128)(2,1)}, u32[]{:S(2)}, u32[]{:S(2)}) collective-permute-start(bf16[512,512]{1,0:T(8,128)(2,1)} %bitcast.5), channel_id=1, source_target_pairs={{2,0},{4,2},{6,4},{8,6},{10,8},{12,10},{14,12},{16,14},{18,16},{20... | collective-permute-start | bytes 1572872 | tf_op jit(solution)/shard_map/ppermute | solution.py:256
  50.7 7.0 %copy-start.12 = (s32[1,1,100,256]{3,1,2,0:T(1,128)S(1)}, s32[1,1,100,256]{3,1,2,0:T(1,128)}, u32[]{:S(2)}) copy-start(s32[1,1,100,256]{3,1,2,0:T(1,128)} %param.11) | copy-start | bytes 307204
  54.6 37.1 %collective-permute-start.4 = (bf16[1024,256]{1,0:T(8,128)(2,1)}, bf16[1024,256]{1,0:T(8,128)(2,1)}, u32[]{:S(2)}, u32[]{:S(2)}) collective-permute-start(bf16[1024,256]{1,0:T(8,128)(2,1)} %get-tuple-element.29), channel_id=1, source_target_pairs={{0,2},{2,0},{4,6},{6,4},{8,10},{10,8},{12,14},{14,12},{16,18},{18,... | collective-permute-start | bytes 1572872 | tf_op jit(solution)/shard_map/ppermute | solution.py:268
  59.9 2.9 %copy-start = (bf16[1024,512]{1,0:T(8,128)(2,1)}, bf16[1024,512]{1,0:T(8,128)(2,1)S(1)}, u32[]{:S(2)}) copy-start(bf16[1024,512]{1,0:T(8,128)(2,1)S(1)} %collective-permute-done.w_other_ref) | copy-start | bytes 3145732
  62.8 19.5 %collective-permute-start.3 = (f32[272,128]{1,0:T(8,128)S(1)}, f32[272,128]{1,0:T(8,128)S(1)}, u32[]{:S(2)}, u32[]{:S(2)}) collective-permute-start(f32[272,128]{1,0:T(8,128)S(1)} %get-tuple-element.24.sent_ref), channel_id=1, source_target_pairs={{0,1},{1,0},{2,3},{3,2},{4,5},{5,4},{6,7},{7,6},{8,9},{9,8},{10,11... | collective-permute-start | bytes 417800 | tf_op jit(solution)/shard_map/ppermute | solution.py:284
  82.3 6.8 %copy-start.6 = (f32[272,128]{1,0:T(8,128)}, f32[272,128]{1,0:T(8,128)S(1)}, u32[]{:S(2)}) copy-start(f32[272,128]{1,0:T(8,128)S(1)} %collective-permute-done.3.got_ref) | copy-start | bytes 417796
  89.1 6.7 %copy-start.4 = (bf16[256,512]{1,0:T(8,128)(2,1)}, bf16[256,512]{1,0:T(8,128)(2,1)S(1)}, u32[]{:S(2)}) copy-start(bf16[256,512]{1,0:T(8,128)(2,1)S(1)} %get-tuple-element.28.dctx_ref) | copy-start | bytes 786436
  89.1 6.7 %copy-start.7 = (f32[256,128]{1,0:T(8,128)}, f32[256,128]{1,0:T(8,128)S(1)}, u32[]{:S(2)}) copy-start(f32[256,128]{1,0:T(8,128)S(1)} %get-tuple-element.32.step_ref) | copy-start | bytes 393220
  89.1 6.7 %copy-start.9 = (f32[256,128]{1,0:T(8,128)}, f32[256,128]{1,0:T(8,128)S(1)}, u32[]{:S(2)}) copy-start(f32[256,128]{1,0:T(8,128)S(1)} %get-tuple-element.33.along_ref) | copy-start | bytes 393220
  89.1 3.7 %collective-permute-start.5 = (bf16[256,512]{1,0:T(8,128)(2,1)S(1)}, bf16[256,512]{1,0:T(8,128)(2,1)S(1)}, u32[]{:S(2)}, u32[]{:S(2)}) collective-permute-start(bf16[256,512]{1,0:T(8,128)(2,1)S(1)} %get-tuple-element.28.dctx_ref), channel_id=1, source_target_pairs={{0,2},{2,0},{4,6},{6,4},{8,10},{10,8},{12,14},{14,12},{16,18},{18,... | collective-permute-start | bytes 786440 | tf_op jit(solution)/shard_map/ppermute | solution.py:293
  95.8 9.0 %copy-start.5 = (bf16[256,512]{1,0:T(8,128)(2,1)S(1)}, bf16[256,512]{1,0:T(8,128)(2,1)}, u32[]{:S(2)}) copy-start(bf16[256,512]{1,0:T(8,128)(2,1)} %copy-done.4) | copy-start | bytes 786436
  95.8 19.2 %copy-start.8 = (f32[256,128]{1,0:T(8,128)S(1)}, f32[256,128]{1,0:T(8,128)}, u32[]{:S(2)}) copy-start(f32[256,128]{1,0:T(8,128)} %copy-done.7) | copy-start | bytes 393220
  95.8 19.2 %copy-start.10 = (f32[256,128]{1,0:T(8,128)S(1)}, f32[256,128]{1,0:T(8,128)}, u32[]{:S(2)}) copy-start(f32[256,128]{1,0:T(8,128)} %copy-done.9) | copy-start | bytes 393220
  95.8 61.0 %all-to-all-start.1 = ((bf16[32,32,512]{2,1,0:T(8,128)(2,1)}), bf16[32,32,512]{2,1,0:T(8,128)(2,1)}, u32[]{:S(2)}, u32[]{:S(2)}) async-start(bf16[32,32,512]{2,1,0:T(8,128)(2,1)} %bitcast.35), calls=%async_computation.1 | async-start | bytes 2097152 | tf_op jit(solution)/shard_map/all_to_all | solution.py:296
  106.8 44.5 %collective-permute-start.10 = (bf16[256,1024]{1,0:T(8,128)(2,1)S(1)}, bf16[256,1024]{1,0:T(8,128)(2,1)S(1)}, u32[]{:S(2)}, u32[]{:S(2)}) collective-permute-start(bf16[256,1024]{1,0:T(8,128)(2,1)S(1)} %get-tuple-element.31), channel_id=1, source_target_pairs={{0,385},{1,384},{128,1},{129,0},{256,129},{257,128},{384,257},{385... | collective-permute-start | bytes 1572872 | tf_op jit(solution)/shard_map/ppermute | solution.py:307
  111.7 39.5 %collective-permute-start.9 = (bf16[256,1024]{1,0:T(8,128)(2,1)S(1)}, bf16[256,1024]{1,0:T(8,128)(2,1)S(1)}, u32[]{:S(2)}, u32[]{:S(2)}) collective-permute-start(bf16[256,1024]{1,0:T(8,128)(2,1)S(1)} %get-tuple-element.30), channel_id=1, source_target_pairs={{0,384},{128,0},{256,128},{384,256},{1,385},{129,1},{257,129},{385... | collective-permute-start | bytes 1572872 | tf_op jit(solution)/shard_map/ppermute | solution.py:306
  119.5 34.2 %collective-permute-start.12 = (bf16[528,512]{1,0:T(8,128)(2,1)}, bf16[528,512]{1,0:T(8,128)(2,1)}, u32[]{:S(2)}, u32[]{:S(2)}) collective-permute-start(bf16[528,512]{1,0:T(8,128)(2,1)} %get-tuple-element.37), channel_id=1, source_target_pairs={{2,0},{4,2},{6,4},{8,6},{10,8},{12,10},{14,12},{16,14},{18,16},{20... | collective-permute-start | bytes 1622024 | tf_op jit(solution)/shard_map/ppermute | solution.py:320
  120.8 34.1 %collective-permute-start.11 = (bf16[528,512]{1,0:T(8,128)(2,1)}, bf16[528,512]{1,0:T(8,128)(2,1)S(1)}, u32[]{:S(2)}, u32[]{:S(2)}) collective-permute-start(bf16[528,512]{1,0:T(8,128)(2,1)} %get-tuple-element.36), channel_id=1, source_target_pairs={{0,2},{2,4},{4,6},{6,8},{8,10},{10,12},{12,14},{14,16},{16,18},{18... | collective-permute-start | bytes 1622024 | tf_op jit(solution)/shard_map/ppermute | solution.py:319
  123.9 27.3 %collective-permute-start.8 = (s32[256]{0:T(256)S(1)}, s32[256]{0:T(256)S(1)}, u32[]{:S(2)}, u32[]{:S(2)}) collective-permute-start(s32[256]{0:T(256)S(1)} %bitcast.40), channel_id=1, source_target_pairs={{0,384},{128,0},{256,128},{384,256},{1,385},{129,1},{257,129},{385... | collective-permute-start | bytes 3080 | tf_op jit(solution)/shard_map/ppermute | solution.py:258
  158.2 6.2 %collective-permute-start.6 = (f32[32,512]{1,0:T(8,128)S(1)}, f32[32,512]{1,0:T(8,128)S(1)}, u32[]{:S(2)}, u32[]{:S(2)}) collective-permute-start(f32[32,512]{1,0:T(8,128)S(1)} %convert_reduce_fusion), channel_id=1, source_target_pairs={{0,128},{128,0},{256,384},{384,256},{1,129},{129,1},{257,385},{385... | collective-permute-start | bytes 196616 | tf_op jit(solution)/shard_map/ppermute | solution.py:300
  164.4 7.2 %collective-permute-start.7 = (f32[32,512]{1,0:T(8,128)S(1)}, f32[32,512]{1,0:T(8,128)S(1)}, u32[]{:S(2)}, u32[]{:S(2)}) collective-permute-start(f32[32,512]{1,0:T(8,128)S(1)} %add.59), channel_id=1, source_target_pairs={{0,256},{128,384},{256,0},{384,128},{1,257},{129,385},{257,1},{385... | collective-permute-start | bytes 196616 | tf_op jit(solution)/shard_map/ppermute | solution.py:301
  (4 other events, 5.5 us)

commit v2 on v1

v2 whole, which is shorter than its diff:
```python
import jax
import jax.numpy as jnp
from jax import lax
from jax.experimental import pallas as pl
from jax.experimental.pallas import tpu as pltpu
from jax.sharding import PartitionSpec as P

sharpness_divisor = 0.1
loss_multiplier = 32.0
epsilon = 1e-06

F32 = jnp.float32
BF16 = jnp.bfloat16
I32 = jnp.int32

LANES = 128
SLOTS = 256
FRAMES = 512
WINDOW = 3 * FRAMES
TILES = WINDOW // LANES
WORDS = TILES // 4
COLUMNS = 101
SPARE = LANES - 1
GROUP = 64
MODEL = 1920
FEATS = 512
BLOCK = 30
PAD = 32
PEERS = 32
HALF = PEERS * PAD


def iota(shape, dim):
    return lax.broadcasted_iota(I32, shape, dim)


def one_hot(hits):
    return jnp.where(hits, 1.0, 0.0).astype(BF16)


def dot(left, right):
    return jnp.dot(left, right, preferred_element_type=F32)


def dot_cols(left, right):
    return lax.dot_general(left, right, (((1,), (1,)), ((), ())), preferred_element_type=F32)


def dot_rows(left, right):
    return lax.dot_general(left, right, (((0,), (0,)), ((), ())), preferred_element_type=F32)


def lookup(table, index):
    return jnp.take_along_axis(table, index, axis=1, mode="promise_in_bounds")


def call(body, outs, n_scalars, n_arrays, scratch=(), flops=0, bytes_accessed=0, vmem=8):
    return pl.pallas_call(
        body,
        out_shape=tuple(jax.ShapeDtypeStruct(shape, dtype) for shape, dtype in outs),
        in_specs=[pl.BlockSpec(memory_space=pltpu.SMEM)] * n_scalars
        + [pl.BlockSpec(memory_space=pltpu.VMEM)] * n_arrays,
        out_specs=tuple(pl.BlockSpec(memory_space=pltpu.VMEM) for _ in outs),
        scratch_shapes=list(scratch),
        compiler_params=pltpu.CompilerParams(vmem_limit_bytes=vmem * 1024 * 1024),
        cost_estimate=pl.CostEstimate(
            flops=flops, bytes_accessed=bytes_accessed, transcendentals=0
        ),
    )


def blocks_body(w_ref, out_ref):
    block = w_ref[...].astype(F32)
    block = jnp.concatenate([block, jnp.zeros((PAD - BLOCK, FEATS), F32)], axis=0).astype(BF16)
    for i in range(PEERS):
        out_ref[i] = block


def window_body(low_ref, own_ref, high_ref, window_ref, norm_ref):
    norm_ref[...] = jnp.zeros((16, LANES), F32)
    for part, ref in enumerate((low_ref, own_ref, high_ref)):
        for k in range(FRAMES // LANES):
            frames = ref[LANES * k : LANES * (k + 1), :]
            at = part * FRAMES + LANES * k
            window_ref[at : at + LANES, :] = frames
            square = frames.astype(F32)
            square = square * square
            partial = sum(square[:, LANES * i : LANES * (i + 1)] for i in range(FEATS // LANES))
            t = at // LANES
            norm_ref[t : t + 1, :] = jnp.sum(partial.T, axis=0, keepdims=True)


def spans_of(core):
    step = 256
    for side, parity in enumerate((core, 1 - core)):
        for k in range(HALF // step):
            low = (2 * BLOCK * step // PAD * k) // LANES * LANES
            wide = min(MODEL, low + 640) - low
            q = iota((step, wide), 0) + step * k
            wanted = BLOCK * (2 * (q >> 5) + parity) + (q & 31)
            spread = one_hot((wanted == iota((step, wide), 1) + low) & ((q & 31) < BLOCK))
            yield side, slice(step * k, step * (k + 1)), slice(low, low + wide), spread


def rows_body(core_ref, pos_ref, hidden_ref, own_ref, other_ref, rows_ref):
    chosen = one_hot(pos_ref[...] == iota((SLOTS, FRAMES), 1))
    rows = dot(chosen, hidden_ref[...]).astype(BF16)
    rows_ref[...] = rows
    for side, to, of, spread in spans_of(core_ref[0]):
        (own_ref, other_ref)[side][:, to] = dot_cols(rows[:, of], spread).astype(BF16)


def turned_body(core_ref, rows_ref, own_ref, other_ref):
    for side, to, of, spread in spans_of(core_ref[0]):
        (own_ref, other_ref)[side][to, :] = dot_cols(spread, rows_ref[:, of]).astype(BF16)


def index_body(named_ref, packed_ref, times_ref, frame_ref, words_ref):
    depth = 32
    here_at, times_at = WORDS, WORDS + 1
    for side in range(SLOTS // LANES):
        across = slice(LANES * side, LANES * (side + 1))

        def prepare(i, carry):
            rows = pl.ds(pl.multiple_of(i * depth, depth), depth)
            part = named_ref[rows, across]
            times = jnp.zeros((depth, LANES), I32)
            first = jnp.full((depth, LANES), SPARE, I32)
            for c in reversed(range(COLUMNS)):
                same = part == jnp.broadcast_to(named_ref[c : c + 1, across], (depth, LANES))
                times = times + jnp.where(same, 1, 0)
                first = jnp.where(same, c, first)
            mine = iota((depth, LANES), 0) + i * depth
            tile = part >> 7
            value = jnp.where((first == mine) & (mine < COLUMNS), (SPARE - mine) << ((tile & 3) * 8), 0)
            for w in range(WORDS):
                words_ref[w, rows, across] = jnp.where((tile >> 2) == w, value, 0)
            words_ref[here_at, rows, across] = part & 127
            words_ref[times_at, rows, across] = times
            return carry

        def pack(i, carry):
            rows = pl.ds(pl.multiple_of(i * depth, depth), depth)
            place = iota((depth, LANES), 0) + i * depth
            packed = [jnp.zeros((depth, LANES), I32) for _ in range(WORDS)]
            for c in range(COLUMNS):
                here = place == jnp.broadcast_to(words_ref[here_at, c : c + 1, across], (depth, LANES))
                for w in range(WORDS):
                    word = jnp.broadcast_to(words_ref[w, c : c + 1, across], (depth, LANES))
                    packed[w] = packed[w] + jnp.where(here, word, 0)
            for w in range(WORDS):
                words_ref[times_at + 1 + w, rows, across] = packed[w]
            return carry

        lax.fori_loop(0, LANES // depth, prepare, 0)
        lax.fori_loop(0, LANES // depth, pack, 0)
        times_ref[across, :] = words_ref[times_at, :, across].T.astype(F32)
        frame_ref[across, :] = named_ref[:, across].T
        for w in range(WORDS):
            packed_ref[across, LANES * w : LANES * (w + 1)] = words_ref[times_at + 1 + w, :, across].T


def columns_of(packed_ref, rows):
    for w in range(WORDS):
        word = packed_ref[rows, LANES * w : LANES * (w + 1)]
        for k in range(4):
            yield 4 * w + k, SPARE - ((word >> (8 * k)) & 127)


def part_body(rows_ref, w_ref, out_ref):
    out_ref[...] = dot(rows_ref[...], w_ref[...])


def score_body(part_ref, other_ref, w_other_ref, window_ref, frame_ref, norm_ref, sent_ref, context_ref, table_ref):
    context = part_ref[...] + dot(other_ref[...], w_other_ref[...])
    context_ref[...] = context
    table_ref[...] = dot_cols(context.astype(BF16), window_ref[...])
    sent_ref[0:SLOTS, :] = jnp.broadcast_to(
        jnp.sum(context * context, axis=1, keepdims=True), (SLOTS, LANES)
    )
    sent_ref[SLOTS : SLOTS + 16, :] = norm_ref[...]
    lane = iota((GROUP, LANES), 1)

    def group(g, carry):
        rows = pl.ds(pl.multiple_of(g * GROUP, GROUP), GROUP)
        frame = frame_ref[rows, :]
        tile, place = frame >> 7, frame & 127
        picked = jnp.where(lane == COLUMNS, sent_ref[rows, :], 0.0)
        for t in range(TILES):
            found = lookup(table_ref[rows, LANES * t : LANES * (t + 1)], place)
            picked = jnp.where((tile == t) & (lane < COLUMNS), found, picked)
        sent_ref[rows, :] = picked
        return carry

    lax.fori_loop(0, SLOTS // GROUP, group, 0)


def slots_body(
    count_ref, place_ref, sent_ref, got_ref, context_ref, frame_ref, times_ref, packed_ref, window_ref,
    dctx_ref, unit_ref, step_ref, along_ref, inverse_ref, shift_ref, scores_ref,
):
    inv_tgt = 1.0 / jnp.sqrt(
        sent_ref[SLOTS : SLOTS + 16, :] + got_ref[SLOTS : SLOTS + 16, :] + epsilon
    )
    lane = iota((GROUP, LANES), 1)
    named = lane < COLUMNS
    count = count_ref[0]

    def group(g, carry):
        rows = pl.ds(pl.multiple_of(g * GROUP, GROUP), GROUP)
        raw = sent_ref[rows, :] + got_ref[rows, :]
        inverse = 1.0 / jnp.sqrt(raw[:, COLUMNS : COLUMNS + 1] + epsilon)
        frame = frame_ref[rows, :]
        tile, place = frame >> 7, frame & 127
        scale = jnp.zeros((GROUP, LANES), F32)
        for t in range(TILES):
            line = jnp.broadcast_to(inv_tgt[t : t + 1, :], (GROUP, LANES))
            scale = jnp.where(tile == t, lookup(line, place), scale)
        logits = raw * inverse * scale / sharpness_divisor
        expon = jnp.where(named, jnp.exp(jnp.where(named, logits, 0.0)), 0.0)
        probs = expon / jnp.sum(expon, axis=1, keepdims=True)
        live = iota((GROUP, LANES), 0) + g * GROUP < count
        first = jnp.where(lane == 0, 1.0, 0.0)
        step = jnp.where(live & named, loss_multiplier * (probs - first) / sharpness_divisor, 0.0)
        times = jnp.maximum(times_ref[rows, :], 1.0)
        step = step * times
        weight = (step * scale).astype(BF16).astype(F32)
        along = jnp.sum(jnp.where(named, weight * raw / times, 0.0), axis=1, keepdims=True)
        step_ref[rows, :] = step
        along_ref[rows, :] = jnp.where(named, step.astype(BF16).astype(F32) * raw * inverse, 0.0)
        inverse_ref[rows, :] = jnp.broadcast_to(inverse, (GROUP, LANES))
        shift_ref[rows, :] = jnp.broadcast_to(along * inverse * inverse * inverse, (GROUP, LANES))
        for t, column in columns_of(packed_ref, rows):
            scores_ref[rows, LANES * t : LANES * (t + 1)] = lookup(weight, column).astype(BF16)
        return carry

    lax.fori_loop(0, SLOTS // GROUP, group, 0)
    context = context_ref[...]
    inverse = inverse_ref[:, 0:1]
    dunit = dot(scores_ref[...], window_ref[...])
    dctx_ref[0:SLOTS, :] = (dunit * inverse - context * shift_ref[:, 0:1]).astype(BF16)
    places = jnp.broadcast_to(place_ref[...], (16, SLOTS))
    parts = jnp.where(iota((16, SLOTS), 0) == 0, places >> 4, places & 15)
    dctx_ref[SLOTS : SLOTS + 16, :] = jnp.zeros((16, FEATS), BF16)
    dctx_ref[SLOTS : SLOTS + 16, 0:SLOTS] = parts.astype(F32).astype(BF16)
    unit_ref[...] = (context * inverse).astype(BF16)


def frames_body(step_ref, along_ref, packed_ref, unit_ref, low_ref, own_ref, high_ref, line_ref, scores_ref, sums_ref):
    sums_ref[...] = jnp.zeros((8, WINDOW), F32)

    def group(g, carry):
        rows = pl.ds(pl.multiple_of(g * GROUP, GROUP), GROUP)
        step = step_ref[rows, :]
        along = along_ref[rows, :]
        for t, column in columns_of(packed_ref, rows):
            span = slice(LANES * t, LANES * (t + 1))
            scores_ref[rows, span] = lookup(step, column).astype(BF16)
            sums_ref[:, span] += jnp.sum(lookup(along, column).reshape(GROUP // 8, 8, LANES), axis=0)
        return carry

    lax.fori_loop(0, SLOTS // GROUP, group, 0)
    line = jnp.sum(sums_ref[...], axis=0, keepdims=True)
    line_ref[...] = jnp.broadcast_to(line[:, FRAMES : 2 * FRAMES], (8, FRAMES))
    row = iota((16, FRAMES), 0)
    for part, ref in ((0, low_ref), (1, own_ref), (2, high_ref)):
        span = slice(FRAMES * part, FRAMES * (part + 1))
        ref[0:FRAMES, :] = dot_rows(scores_ref[:, span], unit_ref[...]).astype(ref.dtype)
        if part != 1:
            left = jnp.broadcast_to(line[:, span], (16, FRAMES))
            first = left.astype(BF16).astype(F32)
            second = (left - first).astype(BF16).astype(F32)
            third = left - first - second
            ref[FRAMES : FRAMES + 16, :] = jnp.where(
                row == 0, first, jnp.where(row == 1, second, jnp.where(row == 2, third, 0.0))
            ).astype(BF16)


def share_body(turned_own_ref, turned_got_ref, own_ref, got_ref, out_ref):
    own = dot(turned_own_ref[...], own_ref[0:SLOTS, :])
    out_ref[...] = (own + dot(turned_got_ref[...], got_ref[0:SLOTS, :])).astype(BF16)


def total_body(parts_ref, out_ref):
    total = jnp.sum(parts_ref[...].astype(F32), axis=0)
    for i in range(out_ref.shape[0]):
        out_ref[i] = total


def sum_body(parts_ref, out_ref):
    out_ref[...] = jnp.sum(parts_ref[...], axis=0)[0:BLOCK, :]


def cross_body(half_ref, dctx_ref, w_own_ref, w_other_ref, cross_ref):
    rows = pl.ds(pl.multiple_of((1 - half_ref[0]) * (HALF // 2), HALF // 2), HALF // 2)
    dctx = dctx_ref[0:SLOTS, :]
    cross_ref[:, 0 : HALF // 2] = dot_cols(dctx, w_own_ref[rows, :]).astype(BF16)
    cross_ref[:, HALF // 2 : HALF] = dot_cols(dctx, w_other_ref[rows, :]).astype(BF16)


def spread_body(core_ref, half_ref, same_ref, cross_ref, w_own_ref, w_other_ref, line_ref, out_ref, rows_ref):
    core = core_ref[0]
    which = pl.ds(pl.multiple_of(half_ref[0] * (HALF // 2), HALF // 2), HALF // 2)
    dctx = same_ref[0:SLOTS, :]
    parts = same_ref[SLOTS : SLOTS + 16, 0:SLOTS].astype(F32)
    places = (parts[0:1, :] * 16.0 + parts[1:2, :]).astype(I32)
    placed = one_hot(iota((FRAMES, SLOTS), 0) == places)
    rows_ref[...] = jnp.zeros((SLOTS, MODEL // 2), F32)
    step = 256
    for side, (parity, w_ref) in enumerate(((core, w_own_ref), (1 - core, w_other_ref))):
        span = slice(HALF // 2 * side, HALF // 2 * (side + 1))
        drows = (dot_cols(dctx, w_ref[which, :]) + cross_ref[:, span].astype(F32)).astype(BF16)
        for k in range(HALF // 2 // step):
            first = 2 * BLOCK * step // PAD * k
            low = first // LANES * LANES
            high = min(MODEL // 2, -(-(first + 2 * BLOCK * step // PAD) // LANES) * LANES)
            q = iota((step, high - low), 0) + step * k
            wanted = BLOCK * (2 * (q >> 5) + parity) + (q & 31)
            unpad = one_hot((wanted == iota((step, high - low), 1) + low) & ((q & 31) < BLOCK))
            rows_ref[:, low:high] += dot(drows[:, step * k : step * (k + 1)], unpad)
    out_ref[...] = dot(placed, rows_ref[...].astype(BF16)).astype(BF16)


def targets_body(targets_ref, own_ref, low_ref, high_ref, line_ref, sent_ref, got_ref, out_ref):
    tail = slice(FRAMES, FRAMES + 16)
    line = line_ref[0:1, :] + jnp.sum(
        low_ref[tail, :].astype(F32) + high_ref[tail, :].astype(F32), axis=0, keepdims=True
    )
    inv_tgt = 1.0 / jnp.sqrt(
        sent_ref[SLOTS : SLOTS + 16, :] + got_ref[SLOTS : SLOTS + 16, :] + epsilon
    )
    for t in range(FRAMES // LANES):
        span = slice(LANES * t, LANES * (t + 1))
        scale = inv_tgt[TILES // 3 + t : TILES // 3 + t + 1, :]
        shift = line[:, span] * scale * scale * scale
        scale = jnp.broadcast_to(scale, (LANES, LANES)).T[:, 0:1]
        shift = jnp.broadcast_to(shift, (LANES, LANES)).T[:, 0:1]
        dtgt = own_ref[span, :] + low_ref[span, :].astype(F32) + high_ref[span, :].astype(F32)
        out_ref[span, :] = (dtgt * scale - targets_ref[span, :].astype(F32) * shift).astype(BF16)


def local(hidden, targets, w_proj, mask_counts, mask_pos, negatives):
    shard = lax.axis_index("dp")
    core = (shard % 2).astype(I32).reshape(1)
    half = lax.axis_index("param").astype(I32).reshape(1)
    n_dp = lax.axis_size("dp")
    n_pipe = lax.axis_size("pipe")
    peers = [[2 * i + c for i in range(n_dp // 2)] for c in range(2)]
    swap = [(i, i ^ 1) for i in range(n_dp)]
    upward = [(i, i + 1) for i in range(n_dp - 1)]
    downward = [(i + 1, i) for i in range(n_dp - 1)]
    back = [(i, (i - 1) % n_pipe) for i in range(n_pipe)]
    back_across = [
        (2 * i + a, 2 * ((i - 1) % n_pipe) + 1 - a) for i in range(n_pipe) for a in range(2)
    ]

    (w_blocks,) = call(blocks_body, [((PEERS, PAD, FEATS), BF16)], 0, 1, bytes_accessed=10**6)(w_proj)
    w_own = lax.all_to_all(w_blocks, "dp", 0, 0, axis_index_groups=peers, tiled=True).reshape(HALF, FEATS)
    own_targets = targets[0]
    low = lax.ppermute(own_targets, "dp", upward)
    high = lax.ppermute(own_targets, "dp", downward)
    positions = mask_pos[0, 0] - shard * FRAMES

    frames = jnp.concatenate([mask_pos[0, 0][None, :], negatives[0, 0]], axis=0) - (shard - 1) * FRAMES
    frames = jnp.pad(frames, ((0, LANES - COLUMNS), (0, 0)), constant_values=-1)

    rows_own, rows_other, rows = call(
        rows_body,
        [((SLOTS, HALF), BF16)] * 2 + [((SLOTS, MODEL), BF16)],
        1, 2, flops=2 * 10**9, bytes_accessed=4 * 10**6,
    )(core, positions[:, None], hidden[0])
    turned_own, turned_other = call(
        turned_body, [((HALF, SLOTS), BF16)] * 2, 1, 1, flops=10**9, bytes_accessed=2 * 10**6
    )(core, rows)
    turned_got = lax.ppermute(turned_other, "dp", swap)

    packed, times, frames = call(
        index_body, [((SLOTS, WORDS * LANES), I32), ((SLOTS, LANES), F32), ((SLOTS, LANES), I32)], 0, 1,
        scratch=[pltpu.VMEM((2 * WORDS + 2, LANES, SLOTS), I32)], flops=5 * 10**9, bytes_accessed=10**6,
    )(frames)

    window, norms = call(
        window_body, [((WINDOW, FEATS), BF16), ((16, LANES), F32)], 0, 3, flops=10**6, bytes_accessed=3 * 10**6
    )(low, own_targets, high)
    w_own, rows_own, rows_other, turned_own, turned_got, packed, times, frames, window, norms = lax.optimization_barrier(
        (w_own, rows_own, rows_other, turned_own, turned_got, packed, times, frames, window, norms)
    )
    w_other = lax.ppermute(w_own, "dp", swap)

    (part,) = call(
        part_body, [((SLOTS, FEATS), F32)], 0, 2, flops=3 * 10**8, bytes_accessed=2 * 10**6
    )(rows_own, w_own)
    sent, context = call(
        score_body, [((SLOTS + 16, LANES), F32), ((SLOTS, FEATS), F32)], 0, 6,
        scratch=[pltpu.VMEM((SLOTS, WINDOW), F32)], flops=10**9, bytes_accessed=6 * 10**6,
    )(part, rows_other, w_other, window, frames, norms)
    got = lax.ppermute(sent, "param", [(0, 1), (1, 0)])

    dctx, unit, step, along = call(
        slots_body,
        [((SLOTS + 16, FEATS), BF16), ((SLOTS, FEATS), BF16)] + [((SLOTS, LANES), F32)] * 2,
        1, 8,
        scratch=[pltpu.VMEM((SLOTS, LANES), F32)] * 2 + [pltpu.VMEM((SLOTS, WINDOW), BF16)],
        flops=5 * 10**8, bytes_accessed=5 * 10**6,
    )(mask_counts[0], positions[None, :], sent, got, context, frames, times, packed, window)
    dctx_got = lax.ppermute(dctx, "dp", swap)

    (share,) = call(
        share_body, [((HALF, FEATS), BF16)], 0, 4, flops=5 * 10**8, bytes_accessed=3 * 10**6
    )(turned_own, turned_got, dctx, dctx_got)
    shares = lax.all_to_all(
        share.reshape(PEERS, PAD, FEATS), "dp", 0, 0, axis_index_groups=peers, tiled=True
    )
    same = lax.ppermute(dctx, "pipe", back)
    shares, same = lax.optimization_barrier((shares, same))
    (copies,) = call(
        total_body, [((n_pipe, PAD, FEATS), F32)], 0, 1, flops=10**6, bytes_accessed=10**6
    )(shares)

    to_low, dtgt, to_high, line = call(
        frames_body,
        [((FRAMES + 16, FEATS), BF16), ((FRAMES, FEATS), F32), ((FRAMES + 16, FEATS), BF16), ((8, FRAMES), F32)],
        0, 4,
        scratch=[pltpu.VMEM((SLOTS, WINDOW), BF16), pltpu.VMEM((8, WINDOW), F32)],
        flops=5 * 10**8, bytes_accessed=5 * 10**6,
    )(step, along, packed, unit)
    from_low = lax.ppermute(to_high, "dp", upward)
    from_high = lax.ppermute(to_low, "dp", downward)

    (cross,) = call(
        cross_body, [((SLOTS, HALF), BF16)], 1, 3, flops=5 * 10**8, bytes_accessed=2 * 10**6
    )(half, dctx, w_own, w_other)
    cross = lax.ppermute(cross, ("pipe", "param"), back_across)

    pipe_parts = lax.all_to_all(copies, "pipe", 0, 0, tiled=True)
    _, line = lax.optimization_barrier((copies, line))
    (grad_t,) = call(
        targets_body, [((FRAMES, FEATS), BF16)], 0, 7, flops=10**7, bytes_accessed=3 * 10**6
    )(own_targets, dtgt, from_low, from_high, line, sent, got)
    cross, _ = lax.optimization_barrier((cross, grad_t))
    (upstream,) = call(
        spread_body, [((FRAMES, MODEL // 2), BF16)], 2, 5,
        scratch=[pltpu.VMEM((SLOTS, MODEL // 2), F32)], flops=10**9, bytes_accessed=4 * 10**6,
    )(core, half, same, cross, w_own, w_other, line)
    (grad_w,) = call(sum_body, [((BLOCK, FEATS), F32)], 0, 1, flops=10**5, bytes_accessed=10**5)(pipe_parts)
    return (grad_w, upstream[None], grad_t[None])


def solution(mesh):
    return jax.shard_map(
        local,
        mesh=mesh,
        in_specs=(
            P("pipe", "dp", None),
            P("pipe", "dp", "param"),
            P("dp", "param"),
            P("pipe", "dp"),
            P("pipe", "dp", None),
            P("pipe", "dp", None, None),
        ),
        out_specs=(P("dp", "param"), P("pipe", "dp", "param"), P("pipe", "dp", "param")),
        check_vma=False,
    )
```

time: 173 us -> 157 us (0.908)
  the two profiles are of different devices: /device:TPU:56 before, /device:TPU:50 now
where the time goes in v2:
time: 157 us; the launch traced here: 156 us
  starting transfers between devices  56.8 us (36%)
  waiting for transfers between devices  44.2 us (28%)
  Pallas kernels  30.4 us (19%)
  local copies, waits for them, and re-layouts  23.2 us (15%)
  between operations  1.68 us (1%)
    unnamed x66, local copies, waits for them, and re-layouts  23 us
    ppermute x1, waiting for transfers between devices, local(): cross = lax.ppermute(cross, ('pipe', 'param'), back_across)  18.8 us
    all_to_all x1, starting transfers between devices, local(): lax.all_to_all(w_blocks, 'dp', 0, 0, axis_index_groups=peers, tiled=True)  13.5 us
    all_to_all x1, starting transfers between devices, local(): lax.all_to_all(share.reshape(PEERS, PAD, FEATS), 'dp', 0, 0, axis_index_g...  11.8 us
    ppermute x1, waiting for transfers between devices, local(): got = lax.ppermute(sent, 'param', [(0, 1), (1, 0)])  10.5 us
    all_to_all x1, waiting for transfers between devices, local(): lax.all_to_all(share.reshape(PEERS, PAD, FEATS), 'dp', 0, 0, axis_index_g...  6.89 us
    all_to_all x1, waiting for transfers between devices, local(): lax.all_to_all(w_blocks, 'dp', 0, 0, axis_index_groups=peers, tiled=True)  6.01 us
    all_to_all x1, starting transfers between devices, local(): pipe_parts = lax.all_to_all(copies, 'pipe', 0, 0, tiled=True)  5.64 us
  transfers between devices with their start and end apart: 13, of which 6 were waited for; matrix products, arithmetic and copies ran while one was open for 1% of the time, Pallas kernels for 13%

profile of v2, /device:TPU:50, one launch (start us, length us, event | category | flops | bytes accessed | tf_op | source)
XLA Modules:
  0.0 156.3 jit_solution(7580172159934756374)
XLA Ops:
  2.6 13.5 %all-to-all-start = ((bf16[32,32,512]{2,1,0:T(8,128)(2,1)}), bf16[32,32,512]{2,1,0:T(8,128)(2,1)S(1)}, u32[]{:S(2)}, u32[]{:S(2)}) async-start(bf16[32,32,512]{2,1,0:T(8,128)(2,1)} %shard_map.85), calls=%async_computation | async-start | bytes 2097152 | tf_op jit(solution)/shard_map/all_to_all | solution.py:358
  16.0 1.9 %collective-permute-start.2 = (bf16[512,512]{1,0:T(8,128)(2,1)S(1)}, bf16[512,512]{1,0:T(8,128)(2,1)S(1)}, u32[]{:S(2)}, u32[]{:S(2)}) collective-permute-start(bf16[512,512]{1,0:T(8,128)(2,1)S(1)} %bitcast.23), channel_id=1, source_target_pairs={{2,0},{4,2},{6,4},{8,6},{10,8},{12,10},{14,12},{16,14},{18,16},{20... | collective-permute-start | bytes 1572872 | tf_op jit(solution)/shard_map/ppermute | solution.py:361
  18.0 2.4 %collective-permute-start.1 = (bf16[512,512]{1,0:T(8,128)(2,1)S(1)}, bf16[512,512]{1,0:T(8,128)(2,1)S(1)}, u32[]{:S(2)}, u32[]{:S(2)}) collective-permute-start(bf16[512,512]{1,0:T(8,128)(2,1)S(1)} %bitcast.24), channel_id=1, source_target_pairs={{0,2},{2,4},{4,6},{6,8},{8,10},{10,12},{12,14},{14,16},{16,18},{18... | collective-permute-start | bytes 1572872 | tf_op jit(solution)/shard_map/ppermute | solution.py:360
  25.3 1.8 %shard_map.87 = (bf16[1024,256]{1,0:T(8,128)(2,1)S(1)}, bf16[1024,256]{1,0:T(8,128)(2,1)}) custom-call(s32[1]{0:T(128)} %bitcast.1.core_ref, bf16[256,1920]{1,0:T(8,128)(2,1)S(1)} %get-tuple-element.39.rows_ref), custom_call_target="tpu_custom_call" | custom-call | flops 1000000000 | bytes 2000000 | tf_op jit(solution)/shard_map/pallas_call | solution.py:372
  27.1 3.0 %collective-permute-start = (bf16[1024,256]{1,0:T(8,128)(2,1)}, bf16[1024,256]{1,0:T(8,128)(2,1)}, u32[]{:S(2)}, u32[]{:S(2)}) collective-permute-start(bf16[1024,256]{1,0:T(8,128)(2,1)} %get-tuple-element.41), channel_id=1, source_target_pairs={{0,2},{2,0},{4,6},{6,4},{8,10},{10,8},{12,14},{14,12},{16,18},{18,... | collective-permute-start | bytes 1572872 | tf_op jit(solution)/shard_map/ppermute | solution.py:375
  30.1 5.6 %shard_map.88 = (s32[256,384]{1,0:T(8,128)S(1)}, f32[256,128]{1,0:T(8,128)S(1)}, s32[256,128]{1,0:T(8,128)S(1)}) custom-call(s32[128,256]{1,0:T(8,128)S(1)} %pad.4.named_ref), custom_call_target="tpu_custom_call" | custom-call | flops 5000000000 | bytes 1000000 | tf_op jit(solution)/shard_map/pallas_call | solution.py:377
  38.1 6.0 %all-to-all-done = bf16[32,32,512]{2,1,0:T(8,128)(2,1)S(1)} async-done(((bf16[32,32,512]{2,1,0:T(8,128)(2,1)}), bf16[32,32,512]{2,1,0:T(8,128)(2,1)S(1)}, u32[]{:S(2)}, u32[]{:S(2)}) %all-to-all-start) | async-done | bytes 1048608 | tf_op jit(solution)/shard_map/all_to_all | solution.py:358
  44.1 2.0 %collective-permute-start.3 = (bf16[1024,512]{1,0:T(8,128)(2,1)S(1)}, bf16[1024,512]{1,0:T(8,128)(2,1)S(1)}, u32[]{:S(2)}, u32[]{:S(2)}) collective-permute-start(bf16[1024,512]{1,0:T(8,128)(2,1)S(1)} %bitcast.17), channel_id=1, source_target_pairs={{0,2},{2,0},{4,6},{6,4},{8,10},{10,8},{12,14},{14,12},{16,18},{18,... | collective-permute-start | bytes 3145736 | tf_op jit(solution)/shard_map/ppermute | solution.py:388
  49.8 2.3 %shard_map.91 = (f32[272,128]{1,0:T(8,128)S(1)}, f32[256,512]{1,0:T(8,128)S(1)}) custom-call(f32[256,512]{1,0:T(8,128)S(1)} %shard_map.90.part_ref, bf16[256,1024]{1,0:T(8,128)(2,1)S(1)} %copy-done.14, bf16[1024,512]{1,0:T(8,128)(2,1)S(1)} %collective-permute-done.3.w_other_ref, bf16[1536,512]{1,0:T(8,128)(2,1)S(1)} %copy-done.1, ...), custom_call_target="tpu_custom_call" | custom-call | flops 1000000000 | bytes 6000000 | tf_op jit(solution)/shard_map/pallas_call | solution.py:393
  52.1 3.8 %collective-permute-start.4 = (f32[272,128]{1,0:T(8,128)S(1)}, f32[272,128]{1,0:T(8,128)S(1)}, u32[]{:S(2)}, u32[]{:S(2)}) collective-permute-start(f32[272,128]{1,0:T(8,128)S(1)} %get-tuple-element.55.sent_ref), channel_id=1, source_target_pairs={{0,1},{1,0},{2,3},{3,2},{4,5},{5,4},{6,7},{7,6},{8,9},{9,8},{10,11... | collective-permute-start | bytes 417800 | tf_op jit(solution)/shard_map/ppermute | solution.py:397
  56.0 10.5 %collective-permute-done.4.got_ref = f32[272,128]{1,0:T(8,128)S(1)} collective-permute-done((f32[272,128]{1,0:T(8,128)S(1)}, f32[272,128]{1,0:T(8,128)S(1)}, u32[]{:S(2)}, u32[]{:S(2)}) %collective-permute-start.4) | collective-permute-done | bytes 139296 | tf_op jit(solution)/shard_map/ppermute | solution.py:397
  67.4 3.9 %shard_map.92 = (bf16[272,512]{1,0:T(8,128)(2,1)S(1)}, bf16[256,512]{1,0:T(8,128)(2,1)S(1)}, f32[256,128]{1,0:T(8,128)S(1)}, f32[256,128]{1,0:T(8,128)S(1)}) custom-call(s32[1]{0:T(128)} %bitcast.16.count_ref, s32[1,256]{1,0:T(1,128)S(1)} %broadcast_subtract_fusion.place_ref, f32[272,128]{1,0:T(8,128)S(1)} %get-tuple-element.55.sent_ref, ...), custom_call_target="tpu_custom_call" | custom-call | flops 500000000 | bytes 5000000 | tf_op jit(solution)/shard_map/pallas_call | solution.py:399
  72.7 1.9 %collective-permute-start.5 = (bf16[272,512]{1,0:T(8,128)(2,1)S(1)}, bf16[272,512]{1,0:T(8,128)(2,1)S(1)}, u32[]{:S(2)}, u32[]{:S(2)}) collective-permute-start(bf16[272,512]{1,0:T(8,128)(2,1)S(1)} %get-tuple-element.59.own_ref.dctx_ref), channel_id=1, source_target_pairs={{0,2},{2,0},{4,6},{6,4},{8,10},{10,8},{12,14},{14,12},{16,18},{18,... | collective-permute-start | bytes 835592 | tf_op jit(solution)/shard_map/ppermute | solution.py:406
  79.0 11.8 %all-to-all-start.1 = ((bf16[32,32,512]{2,1,0:T(8,128)(2,1)}), bf16[32,32,512]{2,1,0:T(8,128)(2,1)S(1)}, u32[]{:S(2)}, u32[]{:S(2)}) async-start(bf16[32,32,512]{2,1,0:T(8,128)(2,1)} %bitcast.22), calls=%async_computation.1 | async-start | bytes 2097152 | tf_op jit(solution)/shard_map/all_to_all | solution.py:411
  90.8 3.3 %collective-permute-start.6 = (bf16[272,512]{1,0:T(8,128)(2,1)S(1)}, bf16[272,512]{1,0:T(8,128)(2,1)S(1)}, u32[]{:S(2)}, u32[]{:S(2)}) collective-permute-start(bf16[272,512]{1,0:T(8,128)(2,1)S(1)} %get-tuple-element.59.own_ref.dctx_ref), channel_id=1, source_target_pairs={{0,384},{128,0},{256,128},{384,256},{1,385},{129,1},{257,129},{385... | collective-permute-start | bytes 835592 | tf_op jit(solution)/shard_map/ppermute | solution.py:414
  97.9 3.9 %shard_map.97 = (bf16[528,512]{1,0:T(8,128)(2,1)}, f32[512,512]{1,0:T(8,128)S(1)}, bf16[528,512]{1,0:T(8,128)(2,1)}, f32[8,512]{1,0:T(8,128)S(1)}) custom-call(f32[256,128]{1,0:T(8,128)S(1)} %copy-done.27, f32[256,128]{1,0:T(8,128)S(1)} %copy-done.29, s32[256,384]{1,0:T(8,128)S(1)} %copy-done.17, bf16[256,512]{1,0:T(8,128)(2,1)S(1)} %copy-done.25), custom_call_target="tpu_custom_call" | custom-call | flops 500000000 | bytes 5000000 | tf_op jit(solution)/shard_map/pallas_call | solution.py:420
  102.8 1.9 %collective-permute-start.8 = (bf16[528,512]{1,0:T(8,128)(2,1)}, bf16[528,512]{1,0:T(8,128)(2,1)}, u32[]{:S(2)}, u32[]{:S(2)}) collective-permute-start(bf16[528,512]{1,0:T(8,128)(2,1)} %get-tuple-element.66), channel_id=1, source_target_pairs={{0,2},{2,4},{4,6},{6,8},{8,10},{10,12},{12,14},{14,16},{16,18},{18... | collective-permute-start | bytes 1622024 | tf_op jit(solution)/shard_map/ppermute | solution.py:427
  104.7 3.6 %collective-permute-start.9 = (bf16[528,512]{1,0:T(8,128)(2,1)}, bf16[528,512]{1,0:T(8,128)(2,1)}, u32[]{:S(2)}, u32[]{:S(2)}) collective-permute-start(bf16[528,512]{1,0:T(8,128)(2,1)} %get-tuple-element.67), channel_id=1, source_target_pairs={{2,0},{4,2},{6,4},{8,6},{10,8},{12,10},{14,12},{16,14},{18,16},{20... | collective-permute-start | bytes 1622024 | tf_op jit(solution)/shard_map/ppermute | solution.py:428
  109.6 1.9 %collective-permute-start.7 = (bf16[256,1024]{1,0:T(8,128)(2,1)}, bf16[256,1024]{1,0:T(8,128)(2,1)}, u32[]{:S(2)}, u32[]{:S(2)}) collective-permute-start(bf16[256,1024]{1,0:T(8,128)(2,1)} %shard_map.96), channel_id=1, source_target_pairs={{0,385},{1,384},{128,1},{129,0},{256,129},{257,128},{384,257},{385... | collective-permute-start | bytes 1572872 | tf_op jit(solution)/shard_map/ppermute | solution.py:433
  112.3 6.9 %all-to-all-done.1.parts_ref = bf16[32,32,512]{2,1,0:T(8,128)(2,1)S(1)} async-done(((bf16[32,32,512]{2,1,0:T(8,128)(2,1)}), bf16[32,32,512]{2,1,0:T(8,128)(2,1)S(1)}, u32[]{:S(2)}, u32[]{:S(2)}) %all-to-all-start.1) | async-done | bytes 1048608 | tf_op jit(solution)/shard_map/all_to_all | solution.py:411
  120.0 5.6 %all-to-all-start.2 = ((f32[4,32,512]{2,1,0:T(8,128)}), f32[4,32,512]{2,1,0:T(8,128)S(1)}, u32[]{:S(2)}, u32[]{:S(2)}) async-start(f32[4,32,512]{2,1,0:T(8,128)} %shard_map.94), calls=%async_computation.2 | async-start | bytes 524288 | tf_op jit(solution)/shard_map/all_to_all | solution.py:435
  129.8 2.5 %shard_map.98 = bf16[512,512]{1,0:T(8,128)(2,1)} custom-call(bf16[512,512]{1,0:T(8,128)(2,1)S(1)} %bitcast.26, f32[512,512]{1,0:T(8,128)S(1)} %copy-done.6, bf16[528,512]{1,0:T(8,128)(2,1)} %collective-permute-done.8.low_ref, bf16[528,512]{1,0:T(8,128)(2,1)} %collective-permute-done.9.high_ref, f32[8,512]{1,0:T(8,128)S(1)} %get-tuple-element.69.line_ref, ...), custom_call_target="tpu_custom_call" | custom-call | flops 10000000 | bytes 3000000 | tf_op jit(solution)/shard_map/pallas_call | solution.py:437
  132.2 18.8 %collective-permute-done.7.cross_ref = bf16[256,1024]{1,0:T(8,128)(2,1)} collective-permute-done((bf16[256,1024]{1,0:T(8,128)(2,1)}, bf16[256,1024]{1,0:T(8,128)(2,1)}, u32[]{:S(2)}, u32[]{:S(2)}) %collective-permute-start.7) | collective-permute-done | bytes 524320 | tf_op jit(solution)/shard_map/ppermute | solution.py:433
  152.0 2.4 %shard_map.99 = bf16[512,960]{1,0:T(8,128)(2,1)S(1)} custom-call(s32[1]{0:T(128)} %bitcast.1.core_ref, s32[1]{0:T(128)} %bitcast.8.half_ref, bf16[272,512]{1,0:T(8,128)(2,1)S(1)} %copy-done.19, bf16[256,1024]{1,0:T(8,128)(2,1)} %collective-permute-done.7.cross_ref, bf16[1024,512]{1,0:T(8,128)(2,1)S(1)} %bitcast.20, ...), custom_call_target="tpu_custom_call" | custom-call | flops 1000000000 | bytes 4000000 | tf_op jit(solution)/shard_map/pallas_call | solution.py:441
  (88 shorter events, 33.2 us)
Async XLA Ops:
  0.6 15.4 %copy-start.3 = (bf16[1,512,512]{2,1,0:T(8,128)(2,1)S(1)}, bf16[1,512,512]{2,1,0:T(8,128)(2,1)}, u32[]{:S(2)}) copy-start(bf16[1,512,512]{2,1,0:T(8,128)(2,1)} %param.7) | copy-start | bytes 1572868
  1.5 18.9 %copy-start.31 = (s32[1,1,256]{2,1,0:T(1,128)S(1)}, s32[1,1,256]{2,1,0:T(1,128)}, u32[]{:S(2)}) copy-start(s32[1,1,256]{2,1,0:T(1,128)} %param.10) | copy-start | bytes 3076
  2.6 41.5 %all-to-all-start = ((bf16[32,32,512]{2,1,0:T(8,128)(2,1)}), bf16[32,32,512]{2,1,0:T(8,128)(2,1)S(1)}, u32[]{:S(2)}, u32[]{:S(2)}) async-start(bf16[32,32,512]{2,1,0:T(8,128)(2,1)} %shard_map.85), calls=%async_computation | async-start | bytes 2097152 | tf_op jit(solution)/shard_map/all_to_all | solution.py:358
  16.0 20.5 %collective-permute-start.2 = (bf16[512,512]{1,0:T(8,128)(2,1)S(1)}, bf16[512,512]{1,0:T(8,128)(2,1)S(1)}, u32[]{:S(2)}, u32[]{:S(2)}) collective-permute-start(bf16[512,512]{1,0:T(8,128)(2,1)S(1)} %bitcast.23), channel_id=1, source_target_pairs={{2,0},{4,2},{6,4},{8,6},{10,8},{12,10},{14,12},{16,14},{18,16},{20... | collective-permute-start | bytes 1572872 | tf_op jit(solution)/shard_map/ppermute | solution.py:361
  18.0 18.6 %collective-permute-start.1 = (bf16[512,512]{1,0:T(8,128)(2,1)S(1)}, bf16[512,512]{1,0:T(8,128)(2,1)S(1)}, u32[]{:S(2)}, u32[]{:S(2)}) collective-permute-start(bf16[512,512]{1,0:T(8,128)(2,1)S(1)} %bitcast.24), channel_id=1, source_target_pairs={{0,2},{2,4},{4,6},{6,8},{8,10},{10,12},{12,14},{14,16},{16,18},{18... | collective-permute-start | bytes 1572872 | tf_op jit(solution)/shard_map/ppermute | solution.py:360
  20.6 1.5 copy-start.23
  25.3 4.8 %copy-start.30 = (s32[1,1,100,256]{3,1,2,0:T(1,128)S(1)}, s32[1,1,100,256]{3,1,2,0:T(1,128)}, u32[]{:S(2)}) copy-start(s32[1,1,100,256]{3,1,2,0:T(1,128)} %param.11) | copy-start | bytes 307204
  27.1 11.0 %collective-permute-start = (bf16[1024,256]{1,0:T(8,128)(2,1)}, bf16[1024,256]{1,0:T(8,128)(2,1)}, u32[]{:S(2)}, u32[]{:S(2)}) collective-permute-start(bf16[1024,256]{1,0:T(8,128)(2,1)} %get-tuple-element.41), channel_id=1, source_target_pairs={{0,2},{2,0},{4,6},{6,4},{8,10},{10,8},{12,14},{14,12},{16,18},{18,... | collective-permute-start | bytes 1572872 | tf_op jit(solution)/shard_map/ppermute | solution.py:375
  36.5 15.6 %copy-start.20 = (f32[256,128]{1,0:T(8,128)}, f32[256,128]{1,0:T(8,128)S(1)}, u32[]{:S(2)}) copy-start(f32[256,128]{1,0:T(8,128)S(1)} %get-tuple-element.57.times_ref) | copy-start | bytes 393220
  44.1 4.7 %copy-start.1 = (bf16[1536,512]{1,0:T(8,128)(2,1)S(1)}, bf16[1536,512]{1,0:T(8,128)(2,1)}, u32[]{:S(2)}) copy-start(bf16[1536,512]{1,0:T(8,128)(2,1)} %copy-done) | copy-start | bytes 4718596
  44.1 4.7 %collective-permute-start.3 = (bf16[1024,512]{1,0:T(8,128)(2,1)S(1)}, bf16[1024,512]{1,0:T(8,128)(2,1)S(1)}, u32[]{:S(2)}, u32[]{:S(2)}) collective-permute-start(bf16[1024,512]{1,0:T(8,128)(2,1)S(1)} %bitcast.17), channel_id=1, source_target_pairs={{0,2},{2,0},{4,6},{6,4},{8,10},{10,8},{12,14},{14,12},{16,18},{18,... | collective-permute-start | bytes 3145736 | tf_op jit(solution)/shard_map/ppermute | solution.py:388
  49.8 16.7 %copy-start.16 = (s32[256,384]{1,0:T(8,128)S(1)}, s32[256,384]{1,0:T(8,128)}, u32[]{:S(2)}) copy-start(s32[256,384]{1,0:T(8,128)} %copy-done.15) | copy-start | bytes 1179652
  52.1 25.8 %copy-start.7 = (f32[272,128]{1,0:T(8,128)}, f32[272,128]{1,0:T(8,128)S(1)}, u32[]{:S(2)}) copy-start(f32[272,128]{1,0:T(8,128)S(1)} %get-tuple-element.55.sent_ref) | copy-start | bytes 417796
  52.1 14.4 %collective-permute-start.4 = (f32[272,128]{1,0:T(8,128)S(1)}, f32[272,128]{1,0:T(8,128)S(1)}, u32[]{:S(2)}, u32[]{:S(2)}) collective-permute-start(f32[272,128]{1,0:T(8,128)S(1)} %get-tuple-element.55.sent_ref), channel_id=1, source_target_pairs={{0,1},{1,0},{2,3},{3,2},{4,5},{5,4},{6,7},{7,6},{8,9},{9,8},{10,11... | collective-permute-start | bytes 417800 | tf_op jit(solution)/shard_map/ppermute | solution.py:397
  66.5 11.5 %copy-start.9 = (f32[272,128]{1,0:T(8,128)}, f32[272,128]{1,0:T(8,128)S(1)}, u32[]{:S(2)}) copy-start(f32[272,128]{1,0:T(8,128)S(1)} %collective-permute-done.4.got_ref) | copy-start | bytes 417796
  72.7 5.2 %copy-start.26 = (f32[256,128]{1,0:T(8,128)}, f32[256,128]{1,0:T(8,128)S(1)}, u32[]{:S(2)}) copy-start(f32[256,128]{1,0:T(8,128)S(1)} %get-tuple-element.62.step_ref) | copy-start | bytes 393220
  72.7 3.4 %collective-permute-start.5 = (bf16[272,512]{1,0:T(8,128)(2,1)S(1)}, bf16[272,512]{1,0:T(8,128)(2,1)S(1)}, u32[]{:S(2)}, u32[]{:S(2)}) collective-permute-start(bf16[272,512]{1,0:T(8,128)(2,1)S(1)} %get-tuple-element.59.own_ref.dctx_ref), channel_id=1, source_target_pairs={{0,2},{2,0},{4,6},{6,4},{8,10},{10,8},{12,14},{14,12},{16,18},{18,... | collective-permute-start | bytes 835592 | tf_op jit(solution)/shard_map/ppermute | solution.py:406
  79.0 40.2 %all-to-all-start.1 = ((bf16[32,32,512]{2,1,0:T(8,128)(2,1)}), bf16[32,32,512]{2,1,0:T(8,128)(2,1)S(1)}, u32[]{:S(2)}, u32[]{:S(2)}) async-start(bf16[32,32,512]{2,1,0:T(8,128)(2,1)} %bitcast.22), calls=%async_computation.1 | async-start | bytes 2097152 | tf_op jit(solution)/shard_map/all_to_all | solution.py:411
  90.8 20.8 %collective-permute-start.6 = (bf16[272,512]{1,0:T(8,128)(2,1)S(1)}, bf16[272,512]{1,0:T(8,128)(2,1)S(1)}, u32[]{:S(2)}, u32[]{:S(2)}) collective-permute-start(bf16[272,512]{1,0:T(8,128)(2,1)S(1)} %get-tuple-element.59.own_ref.dctx_ref), channel_id=1, source_target_pairs={{0,384},{128,0},{256,128},{384,256},{1,385},{129,1},{257,129},{385... | collective-permute-start | bytes 835592 | tf_op jit(solution)/shard_map/ppermute | solution.py:414
  102.8 22.9 %collective-permute-start.8 = (bf16[528,512]{1,0:T(8,128)(2,1)}, bf16[528,512]{1,0:T(8,128)(2,1)}, u32[]{:S(2)}, u32[]{:S(2)}) collective-permute-start(bf16[528,512]{1,0:T(8,128)(2,1)} %get-tuple-element.66), channel_id=1, source_target_pairs={{0,2},{2,4},{4,6},{6,8},{8,10},{10,12},{12,14},{14,16},{16,18},{18... | collective-permute-start | bytes 1622024 | tf_op jit(solution)/shard_map/ppermute | solution.py:427
  104.7 21.0 %collective-permute-start.9 = (bf16[528,512]{1,0:T(8,128)(2,1)}, bf16[528,512]{1,0:T(8,128)(2,1)}, u32[]{:S(2)}, u32[]{:S(2)}) collective-permute-start(bf16[528,512]{1,0:T(8,128)(2,1)} %get-tuple-element.67), channel_id=1, source_target_pairs={{2,0},{4,2},{6,4},{8,6},{10,8},{12,10},{14,12},{16,14},{18,16},{20... | collective-permute-start | bytes 1622024 | tf_op jit(solution)/shard_map/ppermute | solution.py:428
  109.6 41.4 %collective-permute-start.7 = (bf16[256,1024]{1,0:T(8,128)(2,1)}, bf16[256,1024]{1,0:T(8,128)(2,1)}, u32[]{:S(2)}, u32[]{:S(2)}) collective-permute-start(bf16[256,1024]{1,0:T(8,128)(2,1)} %shard_map.96), channel_id=1, source_target_pairs={{0,385},{1,384},{128,1},{129,0},{256,129},{257,128},{384,257},{385... | collective-permute-start | bytes 1572872 | tf_op jit(solution)/shard_map/ppermute | solution.py:433
  120.0 35.6 %all-to-all-start.2 = ((f32[4,32,512]{2,1,0:T(8,128)}), f32[4,32,512]{2,1,0:T(8,128)S(1)}, u32[]{:S(2)}, u32[]{:S(2)}) async-start(f32[4,32,512]{2,1,0:T(8,128)} %shard_map.94), calls=%async_computation.2 | async-start | bytes 524288 | tf_op jit(solution)/shard_map/all_to_all | solution.py:435
  126.7 1.2 copy-start.6
  (21 other events, 19.0 us)

commit v3 on v2

--- a/solution.py
+++ b/solution.py
@@ -28,6 +28,9 @@
 PAD = 32
 PEERS = 32
 HALF = PEERS * PAD
+X_CHIPS = 4
+Z_CHIPS = 8
+QUARTER = HALF // X_CHIPS // 2
 
 
 def iota(shape, dim):
@@ -54,12 +57,13 @@
     return jnp.take_along_axis(table, index, axis=1, mode="promise_in_bounds")
 
 
-def call(body, outs, n_scalars, n_arrays, scratch=(), flops=0, bytes_accessed=0, vmem=8):
+def call(body, outs, n_scalars, n_arrays, scratch=(), flops=0, bytes_accessed=0, vmem=8, n_far=0):
     return pl.pallas_call(
         body,
         out_shape=tuple(jax.ShapeDtypeStruct(shape, dtype) for shape, dtype in outs),
         in_specs=[pl.BlockSpec(memory_space=pltpu.SMEM)] * n_scalars
-        + [pl.BlockSpec(memory_space=pltpu.VMEM)] * n_arrays,
+        + [pl.BlockSpec(memory_space=pltpu.VMEM)] * n_arrays
+        + [pl.BlockSpec(memory_space=pl.ANY)] * n_far,
         out_specs=tuple(pl.BlockSpec(memory_space=pltpu.VMEM) for _ in outs),
         scratch_shapes=list(scratch),
         compiler_params=pltpu.CompilerParams(vmem_limit_bytes=vmem * 1024 * 1024),
@@ -90,29 +94,27 @@
             norm_ref[t : t + 1, :] = jnp.sum(partial.T, axis=0, keepdims=True)
 
 
-def spans_of(core):
+def rows_body(core_ref, pos_ref, hidden_ref, own_ref, other_ref, own_t_ref, other_t_ref, turn_ref):
+    chosen = one_hot(pos_ref[...] == iota((SLOTS, FRAMES), 1))
+    rows = dot(chosen, hidden_ref[...]).astype(BF16)
+    core = core_ref[0]
     step = 256
-    for side, parity in enumerate((core, 1 - core)):
+    for parity, straight, turned in ((core, own_ref, own_t_ref), (1 - core, other_ref, other_t_ref)):
         for k in range(HALF // step):
             low = (2 * BLOCK * step // PAD * k) // LANES * LANES
             wide = min(MODEL, low + 640) - low
             q = iota((step, wide), 0) + step * k
             wanted = BLOCK * (2 * (q >> 5) + parity) + (q & 31)
             spread = one_hot((wanted == iota((step, wide), 1) + low) & ((q & 31) < BLOCK))
-            yield side, slice(step * k, step * (k + 1)), slice(low, low + wide), spread
-
-
-def rows_body(core_ref, pos_ref, hidden_ref, own_ref, other_ref, rows_ref):
-    chosen = one_hot(pos_ref[...] == iota((SLOTS, FRAMES), 1))
-    rows = dot(chosen, hidden_ref[...]).astype(BF16)
-    rows_ref[...] = rows
-    for side, to, of, spread in spans_of(core_ref[0]):
-        (own_ref, other_ref)[side][:, to] = dot_cols(rows[:, of], spread).astype(BF16)
-
-
-def turned_body(core_ref, rows_ref, own_ref, other_ref):
-    for side, to, of, spread in spans_of(core_ref[0]):
-        (own_ref, other_ref)[side][to, :] = dot_cols(spread, rows_ref[:, of]).astype(BF16)
+            piece = dot_cols(spread, rows[:, low : low + wide])
+            for i in range(step // PAD):
+                z, x = divmod(step // PAD * k + i, X_CHIPS)
+                at = PAD * (x * Z_CHIPS + z)
+                turn_ref[at : at + PAD, :] = piece[PAD * i : PAD * (i + 1), :]
+        turned[...] = turn_ref[...].astype(BF16)
+        for g in range(HALF // LANES):
+            span = slice(LANES * g, LANES * (g + 1))
+            straight[:, span] = turn_ref[span, :].T.astype(BF16)
 
 
 def index_body(named_ref, packed_ref, times_ref, frame_ref, words_ref):
@@ -281,7 +283,15 @@
     out_ref[...] = (own + dot(turned_got_ref[...], got_ref[0:SLOTS, :])).astype(BF16)
 
 
-def total_body(parts_ref, out_ref):
+def merge_body(parts_ref, out_ref):
+    out_ref[...] = jnp.sum(parts_ref[...].astype(F32), axis=0).astype(BF16)
+
+
+def token_body(cross_ref, same_ref, out_ref):
+    out_ref[...] = jnp.zeros((8, LANES), F32)
+
+
+def total_body(parts_ref, token_ref, out_ref):
     total = jnp.sum(parts_ref[...].astype(F32), axis=0)
     for i in range(out_ref.shape[0]):
         out_ref[i] = total
@@ -291,34 +301,39 @@
     out_ref[...] = jnp.sum(parts_ref[...], axis=0)[0:BLOCK, :]
 
 
+def half_of(w_ref, half):
+    return jnp.concatenate(
+        [
+            w_ref[pl.ds(pl.multiple_of(2 * QUARTER * x + half * QUARTER, QUARTER), QUARTER), :]
+            for x in range(X_CHIPS)
+        ],
+        axis=0,
+    )
+
+
 def cross_body(half_ref, dctx_ref, w_own_ref, w_other_ref, cross_ref):
-    rows = pl.ds(pl.multiple_of((1 - half_ref[0]) * (HALF // 2), HALF // 2), HALF // 2)
+    half = 1 - half_ref[0]
     dctx = dctx_ref[0:SLOTS, :]
-    cross_ref[:, 0 : HALF // 2] = dot_cols(dctx, w_own_ref[rows, :]).astype(BF16)
-    cross_ref[:, HALF // 2 : HALF] = dot_cols(dctx, w_other_ref[rows, :]).astype(BF16)
-
-
-def spread_body(core_ref, half_ref, same_ref, cross_ref, w_own_ref, w_other_ref, line_ref, out_ref, rows_ref):
+    cross_ref[:, 0 : HALF // 2] = dot_cols(dctx, half_of(w_own_ref, half)).astype(BF16)
+    cross_ref[:, HALF // 2 : HALF] = dot_cols(dctx, half_of(w_other_ref, half)).astype(BF16)
+
+
+def spread_body(core_ref, half_ref, same_ref, cross_ref, w_own_ref, w_other_ref, line_ref, out_ref):
     core = core_ref[0]
-    which = pl.ds(pl.multiple_of(half_ref[0] * (HALF // 2), HALF // 2), HALF // 2)
     dctx = same_ref[0:SLOTS, :]
     parts = same_ref[SLOTS : SLOTS + 16, 0:SLOTS].astype(F32)
     places = (parts[0:1, :] * 16.0 + parts[1:2, :]).astype(I32)
     placed = one_hot(iota((FRAMES, SLOTS), 0) == places)
-    rows_ref[...] = jnp.zeros((SLOTS, MODEL // 2), F32)
-    step = 256
+    shape = (HALF // 2, MODEL // 2)
+    rows = jnp.zeros((SLOTS, MODEL // 2), F32)
     for side, (parity, w_ref) in enumerate(((core, w_own_ref), (1 - core, w_other_ref))):
         span = slice(HALF // 2 * side, HALF // 2 * (side + 1))
-        drows = (dot_cols(dctx, w_ref[which, :]) + cross_ref[:, span].astype(F32)).astype(BF16)
-        for k in range(HALF // 2 // step):
-            first = 2 * BLOCK * step // PAD * k
-            low = first // LANES * LANES
-            high = min(MODEL // 2, -(-(first + 2 * BLOCK * step // PAD) // LANES) * LANES)
-            q = iota((step, high - low), 0) + step * k
-            wanted = BLOCK * (2 * (q >> 5) + parity) + (q & 31)
-            unpad = one_hot((wanted == iota((step, high - low), 1) + low) & ((q & 31) < BLOCK))
-            rows_ref[:, low:high] += dot(drows[:, step * k : step * (k + 1)], unpad)
-    out_ref[...] = dot(placed, rows_ref[...].astype(BF16)).astype(BF16)
+        drows = (dot_cols(dctx, half_of(w_ref, half_ref[0])) + cross_ref[:, span].astype(F32)).astype(BF16)
+        q = iota(shape, 0)
+        block = 2 * (X_CHIPS * ((q >> 5) & (Z_CHIPS // 2 - 1)) + (q >> 7)) + parity
+        unpad = one_hot((BLOCK * block + (q & 31) == iota(shape, 1)) & ((q & 31) < BLOCK))
+        rows = rows + dot(drows, unpad)
+    out_ref[...] = dot(placed, rows.astype(BF16)).astype(BF16)
 
 
 def targets_body(targets_ref, own_ref, low_ref, high_ref, line_ref, sent_ref, got_ref, out_ref):
@@ -345,7 +360,9 @@
     half = lax.axis_index("param").astype(I32).reshape(1)
     n_dp = lax.axis_size("dp")
     n_pipe = lax.axis_size("pipe")
-    peers = [[2 * i + c for i in range(n_dp // 2)] for c in range(2)]
+    peers = [[2 * (X_CHIPS * z + x) + c for x in range(X_CHIPS) for z in range(Z_CHIPS)] for c in range(2)]
+    in_x = [[2 * (X_CHIPS * z + x) + c for x in range(X_CHIPS)] for z in range(Z_CHIPS) for c in range(2)]
+    in_z = [[2 * (X_CHIPS * z + x) + c for z in range(Z_CHIPS)] for x in range(X_CHIPS) for c in range(2)]
     swap = [(i, i ^ 1) for i in range(n_dp)]
     upward = [(i, i + 1) for i in range(n_dp - 1)]
     downward = [(i + 1, i) for i in range(n_dp - 1)]
@@ -364,14 +381,11 @@
     frames = jnp.concatenate([mask_pos[0, 0][None, :], negatives[0, 0]], axis=0) - (shard - 1) * FRAMES
     frames = jnp.pad(frames, ((0, LANES - COLUMNS), (0, 0)), constant_values=-1)
 
-    rows_own, rows_other, rows = call(
+    rows_own, rows_other, turned_own, turned_other = call(
         rows_body,
-        [((SLOTS, HALF), BF16)] * 2 + [((SLOTS, MODEL), BF16)],
-        1, 2, flops=2 * 10**9, bytes_accessed=4 * 10**6,
+        [((SLOTS, HALF), BF16)] * 2 + [((HALF, SLOTS), BF16)] * 2,
+        1, 2, scratch=[pltpu.VMEM((HALF, SLOTS), F32)], flops=2 * 10**9, bytes_accessed=4 * 10**6, vmem=16,
     )(core, positions[:, None], hidden[0])
-    turned_own, turned_other = call(
-        turned_body, [((HALF, SLOTS), BF16)] * 2, 1, 1, flops=10**9, bytes_accessed=2 * 10**6
-    )(core, rows)
     turned_got = lax.ppermute(turned_other, "dp", swap)
 
     packed, times, frames = call(
@@ -405,43 +419,53 @@
     )(mask_counts[0], positions[None, :], sent, got, context, frames, times, packed, window)
     dctx_got = lax.ppermute(dctx, "dp", swap)
 
+    (cross,) = call(
+        cross_body, [((SLOTS, HALF), BF16)], 1, 3, flops=5 * 10**8, bytes_accessed=2 * 10**6
+    )(half, dctx, w_own, w_other)
+    cross, dctx_got = lax.optimization_barrier((cross, dctx_got))
+    cross = lax.ppermute(cross, ("pipe", "param"), back_across)
     (share,) = call(
         share_body, [((HALF, FEATS), BF16)], 0, 4, flops=5 * 10**8, bytes_accessed=3 * 10**6
     )(turned_own, turned_got, dctx, dctx_got)
+    step, share, dctx = lax.optimization_barrier((step, share, dctx))
+    same = lax.ppermute(dctx, "pipe", back)
     shares = lax.all_to_all(
-        share.reshape(PEERS, PAD, FEATS), "dp", 0, 0, axis_index_groups=peers, tiled=True
-    )
-    same = lax.ppermute(dctx, "pipe", back)
-    shares, same = lax.optimization_barrier((shares, same))
-    (copies,) = call(
-        total_body, [((n_pipe, PAD, FEATS), F32)], 0, 1, flops=10**6, bytes_accessed=10**6
-    )(shares)
-
+        share.reshape(X_CHIPS, HALF // X_CHIPS, FEATS), "dp", 0, 0, axis_index_groups=in_x, tiled=True
+    )
     to_low, dtgt, to_high, line = call(
         frames_body,
         [((FRAMES + 16, FEATS), BF16), ((FRAMES, FEATS), F32), ((FRAMES + 16, FEATS), BF16), ((8, FRAMES), F32)],
         0, 4,
         scratch=[pltpu.VMEM((SLOTS, WINDOW), BF16), pltpu.VMEM((8, WINDOW), F32)],
-        flops=5 * 10**8, bytes_accessed=5 * 10**6,
+        flops=10**5, bytes_accessed=10**4,
     )(step, along, packed, unit)
+    shares, line = lax.optimization_barrier((shares, line))
+    (share,) = call(
+        merge_body, [((HALF // X_CHIPS, FEATS), BF16)], 0, 1, flops=10**6, bytes_accessed=10**6
+    )(shares)
+    shares = lax.all_to_all(
+        share.reshape(Z_CHIPS, PAD, FEATS), "dp", 0, 0, axis_index_groups=in_z, tiled=True
+    )
     from_low = lax.ppermute(to_high, "dp", upward)
     from_high = lax.ppermute(to_low, "dp", downward)
 
-    (cross,) = call(
-        cross_body, [((SLOTS, HALF), BF16)], 1, 3, flops=5 * 10**8, bytes_accessed=2 * 10**6
-    )(half, dctx, w_own, w_other)
-    cross = lax.ppermute(cross, ("pipe", "param"), back_across)
-
+
+    (token,) = call(
+        token_body, [((8, LANES), F32)], 0, 0, flops=15 * 10**9, bytes_accessed=10**5, n_far=2
+    )(cross, same)
+    (copies,) = call(
+        total_body, [((n_pipe, PAD, FEATS), F32)], 0, 1, flops=10**6, bytes_accessed=10**6, n_far=1
+    )(shares, token)
+
+    copies, line = lax.optimization_barrier((copies, line))
     pipe_parts = lax.all_to_all(copies, "pipe", 0, 0, tiled=True)
-    _, line = lax.optimization_barrier((copies, line))
+    (upstream,) = call(
+        spread_body, [((FRAMES, MODEL // 2), BF16)], 2, 5,
+        flops=1 * 10**9, bytes_accessed=4 * 10**6, vmem=16,
+    )(core, half, same, cross, w_own, w_other, line)
     (grad_t,) = call(
         targets_body, [((FRAMES, FEATS), BF16)], 0, 7, flops=10**7, bytes_accessed=3 * 10**6
     )(own_targets, dtgt, from_low, from_high, line, sent, got)
-    cross, _ = lax.optimization_barrier((cross, grad_t))
-    (upstream,) = call(
-        spread_body, [((FRAMES, MODEL // 2), BF16)], 2, 5,
-        scratch=[pltpu.VMEM((SLOTS, MODEL // 2), F32)], flops=10**9, bytes_accessed=4 * 10**6,
-    )(core, half, same, cross, w_own, w_other, line)
     (grad_w,) = call(sum_body, [((BLOCK, FEATS), F32)], 0, 1, flops=10**5, bytes_accessed=10**5)(pipe_parts)
     return (grad_w, upstream[None], grad_t[None])
 

time: 157 us -> 145 us (0.924)
  the two profiles are of different devices: /device:TPU:50 before, /device:TPU:56 now
where the time goes in v3:
time: 145 us; the launch traced here: 142 us
  starting transfers between devices  64.1 us (44%)
  waiting for transfers between devices  29.7 us (20%)
  Pallas kernels  29.6 us (20%)
  local copies, waits for them, and re-layouts  17.3 us (12%)
  between operations  1.69 us (1%)
    unnamed x64, local copies, waits for them, and re-layouts  17.1 us
    all_to_all x1, starting transfers between devices, local(): lax.all_to_all(share.reshape(Z_CHIPS, PAD, FEATS), 'dp', 0, 0, axis_index...  13.4 us
    all_to_all x1, starting transfers between devices, local(): lax.all_to_all(w_blocks, 'dp', 0, 0, axis_index_groups=peers, tiled=True)  13.2 us
    ppermute x1, waiting for transfers between devices, local(): got = lax.ppermute(sent, 'param', [(0, 1), (1, 0)])  10.1 us
    all_to_all x1, waiting for transfers between devices, local(): lax.all_to_all(w_blocks, 'dp', 0, 0, axis_index_groups=peers, tiled=True)  8.23 us
    all_to_all x1, starting transfers between devices, local(): pipe_parts = lax.all_to_all(copies, 'pipe', 0, 0, tiled=True)  7.08 us
    ppermute x1, waiting for transfers between devices, local(): cross = lax.ppermute(cross, ('pipe', 'param'), back_across)  6.21 us
    pallas_call x1, Pallas kernels, local(): call(index_body, [((SLOTS, WORDS * LANES), I32), ((SLOTS, LANES), F32), (...  5.64 us
  transfers between devices with their start and end apart: 14, of which 6 were waited for; matrix products, arithmetic and copies ran while one was open for 1% of the time, Pallas kernels for 14%

profile of v3, /device:TPU:56, one launch (start us, length us, event | category | flops | bytes accessed | tf_op | source)
XLA Modules:
  0.0 142.5 jit_solution(4552150298975771282)
XLA Ops:
  2.6 13.2 %all-to-all-start = ((bf16[32,32,512]{2,1,0:T(8,128)(2,1)}), bf16[32,32,512]{2,1,0:T(8,128)(2,1)S(1)}, u32[]{:S(2)}, u32[]{:S(2)}) async-start(bf16[32,32,512]{2,1,0:T(8,128)(2,1)} %shard_map.85), calls=%async_computation | async-start | bytes 2097152 | tf_op jit(solution)/shard_map/all_to_all | solution.py:375
  18.7 1.5 %copy-done.28 = bf16[1,512,1920]{2,1,0:T(8,128)(2,1)S(1)} copy-done((bf16[1,512,1920]{2,1,0:T(8,128)(2,1)S(1)}, bf16[1,512,1920]{2,1,0:T(8,128)(2,1)}, u32[]{:S(2)}) %copy-start.28) | copy-done | bytes 1966104
  20.3 2.4 %shard_map.86 = (bf16[256,1024]{1,0:T(8,128)(2,1)S(1)}, bf16[256,1024]{1,0:T(8,128)(2,1)S(1)}, bf16[1024,256]{1,0:T(8,128)(2,1)S(1)}, bf16[1024,256]{1,0:T(8,128)(2,1)}) custom-call(s32[1]{0:T(128)} %bitcast.3.core_ref, s32[256,1]{1,0:T(8,128)S(1)} %copy.10.pos_ref, bf16[512,1920]{1,0:T(8,128)(2,1)S(1)} %bitcast.28), custom_call_target="tpu_custom_call" | custom-call | flops 2000000000 | bytes 4000000 | tf_op jit(solution)/shard_map/pallas_call | solution.py:384
  24.2 4.9 %collective-permute-start = (bf16[1024,256]{1,0:T(8,128)(2,1)}, bf16[1024,256]{1,0:T(8,128)(2,1)}, u32[]{:S(2)}, u32[]{:S(2)}) collective-permute-start(bf16[1024,256]{1,0:T(8,128)(2,1)} %get-tuple-element.44), channel_id=1, source_target_pairs={{0,2},{2,0},{4,6},{6,4},{8,10},{10,8},{12,14},{14,12},{16,18},{18,... | collective-permute-start | bytes 1572872 | tf_op jit(solution)/shard_map/ppermute | solution.py:389
  29.2 5.6 %shard_map.87 = (s32[256,384]{1,0:T(8,128)S(1)}, f32[256,128]{1,0:T(8,128)S(1)}, s32[256,128]{1,0:T(8,128)S(1)}) custom-call(s32[128,256]{1,0:T(8,128)S(1)} %pad.4.named_ref), custom_call_target="tpu_custom_call" | custom-call | flops 5000000000 | bytes 1000000 | tf_op jit(solution)/shard_map/pallas_call | solution.py:391
  37.7 8.2 %all-to-all-done = bf16[32,32,512]{2,1,0:T(8,128)(2,1)S(1)} async-done(((bf16[32,32,512]{2,1,0:T(8,128)(2,1)}), bf16[32,32,512]{2,1,0:T(8,128)(2,1)S(1)}, u32[]{:S(2)}, u32[]{:S(2)}) %all-to-all-start) | async-done | bytes 1048608 | tf_op jit(solution)/shard_map/all_to_all | solution.py:375
  45.9 2.0 %collective-permute-start.3 = (bf16[1024,512]{1,0:T(8,128)(2,1)S(1)}, bf16[1024,512]{1,0:T(8,128)(2,1)S(1)}, u32[]{:S(2)}, u32[]{:S(2)}) collective-permute-start(bf16[1024,512]{1,0:T(8,128)(2,1)S(1)} %bitcast.18), channel_id=1, source_target_pairs={{0,2},{2,0},{4,6},{6,4},{8,10},{10,8},{12,14},{14,12},{16,18},{18,... | collective-permute-start | bytes 3145736 | tf_op jit(solution)/shard_map/ppermute | solution.py:402
  51.7 2.3 %shard_map.90 = (f32[272,128]{1,0:T(8,128)S(1)}, f32[256,512]{1,0:T(8,128)S(1)}) custom-call(f32[256,512]{1,0:T(8,128)S(1)} %shard_map.89.part_ref, bf16[256,1024]{1,0:T(8,128)(2,1)S(1)} %copy-done.16, bf16[1024,512]{1,0:T(8,128)(2,1)S(1)} %collective-permute-done.3.w_other_ref, bf16[1536,512]{1,0:T(8,128)(2,1)S(1)} %copy-done.1, s32[256,128]{1,0:T(8,128)S(1)} %copy-done.18, ...), custom_call_target="tpu_custom_call" | custom-call | flops 1000000000 | bytes 6000000 | tf_op jit(solution)/shard_map/pallas_call | solution.py:407
  53.9 4.7 %collective-permute-start.4 = (f32[272,128]{1,0:T(8,128)S(1)}, f32[272,128]{1,0:T(8,128)S(1)}, u32[]{:S(2)}, u32[]{:S(2)}) collective-permute-start(f32[272,128]{1,0:T(8,128)S(1)} %get-tuple-element.56.sent_ref), channel_id=1, source_target_pairs={{0,1},{1,0},{2,3},{3,2},{4,5},{5,4},{6,7},{7,6},{8,9},{9,8},{10,11... | collective-permute-start | bytes 417800 | tf_op jit(solution)/shard_map/ppermute | solution.py:411
  58.7 10.1 %collective-permute-done.4.got_ref = f32[272,128]{1,0:T(8,128)S(1)} collective-permute-done((f32[272,128]{1,0:T(8,128)S(1)}, f32[272,128]{1,0:T(8,128)S(1)}, u32[]{:S(2)}, u32[]{:S(2)}) %collective-permute-start.4) | collective-permute-done | bytes 139296 | tf_op jit(solution)/shard_map/ppermute | solution.py:411
  68.8 3.9 %shard_map.91 = (bf16[272,512]{1,0:T(8,128)(2,1)S(1)}, bf16[256,512]{1,0:T(8,128)(2,1)S(1)}, f32[256,128]{1,0:T(8,128)S(1)}, f32[256,128]{1,0:T(8,128)S(1)}) custom-call(s32[1]{0:T(128)} %bitcast.17.count_ref, s32[1,256]{1,0:T(1,128)S(1)} %broadcast_subtract_fusion.place_ref, f32[272,128]{1,0:T(8,128)S(1)} %get-tuple-element.56.sent_ref, ...), custom_call_target="tpu_custom_call" | custom-call | flops 500000000 | bytes 5000000 | tf_op jit(solution)/shard_map/pallas_call | solution.py:413
  74.1 1.9 %collective-permute-start.5 = (bf16[272,512]{1,0:T(8,128)(2,1)S(1)}, bf16[272,512]{1,0:T(8,128)(2,1)}, u32[]{:S(2)}, u32[]{:S(2)}) collective-permute-start(bf16[272,512]{1,0:T(8,128)(2,1)S(1)} %get-tuple-element.72.dctx_ref.own_ref), channel_id=1, source_target_pairs={{0,2},{2,0},{4,6},{6,4},{8,10},{10,8},{12,14},{14,12},{16,18},{18,... | collective-permute-start | bytes 835592 | tf_op jit(solution)/shard_map/ppermute | solution.py:420
  77.7 1.8 %shard_map.93 = bf16[1024,512]{1,0:T(8,128)(2,1)S(1)} custom-call(bf16[1024,256]{1,0:T(8,128)(2,1)S(1)} %get-tuple-element.61.turned_own_ref, bf16[1024,256]{1,0:T(8,128)(2,1)} %collective-permute-done.turned_got_ref, bf16[272,512]{1,0:T(8,128)(2,1)S(1)} %get-tuple-element.72.dctx_ref.own_ref, bf16[272,512]{1,0:T(8,128)(2,1)} %collective-permute-done.5.got_ref), custom_call_target="tpu_custom_call" | custom-call | flops 500000000 | bytes 3000000 | tf_op jit(solution)/shard_map/pallas_call | solution.py:427
  80.5 5.0 %all-to-all-start.1 = ((bf16[4,256,512]{2,1,0:T(8,128)(2,1)}), bf16[4,256,512]{2,1,0:T(8,128)(2,1)S(1)}, u32[]{:S(2)}, u32[]{:S(2)}) async-start(bf16[4,256,512]{2,1,0:T(8,128)(2,1)} %bitcast.23), calls=%async_computation.1 | async-start | bytes 2097152 | tf_op jit(solution)/shard_map/all_to_all | solution.py:432
  85.6 3.7 %collective-permute-start.6 = (bf16[256,1024]{1,0:T(8,128)(2,1)}, bf16[256,1024]{1,0:T(8,128)(2,1)}, u32[]{:S(2)}, u32[]{:S(2)}) collective-permute-start(bf16[256,1024]{1,0:T(8,128)(2,1)} %copy-done.12), channel_id=1, source_target_pairs={{0,385},{1,384},{128,1},{129,0},{256,129},{257,128},{384,257},{385... | collective-permute-start | bytes 1572872 | tf_op jit(solution)/shard_map/ppermute | solution.py:426
  89.3 2.0 %collective-permute-start.7 = (bf16[272,512]{1,0:T(8,128)(2,1)}, bf16[272,512]{1,0:T(8,128)(2,1)}, u32[]{:S(2)}, u32[]{:S(2)}) collective-permute-start(bf16[272,512]{1,0:T(8,128)(2,1)} %copy-done.5), channel_id=1, source_target_pairs={{0,384},{128,0},{256,128},{384,256},{1,385},{129,1},{257,129},{385... | collective-permute-start | bytes 835592 | tf_op jit(solution)/shard_map/ppermute | solution.py:431
  94.1 4.0 %shard_map.94 = (bf16[528,512]{1,0:T(8,128)(2,1)}, f32[512,512]{1,0:T(8,128)S(1)}, bf16[528,512]{1,0:T(8,128)(2,1)}, f32[8,512]{1,0:T(8,128)S(1)}) custom-call(f32[256,128]{1,0:T(8,128)S(1)} %copy-done.24, f32[256,128]{1,0:T(8,128)S(1)} %copy-done.26, s32[256,384]{1,0:T(8,128)S(1)} %get-tuple-element.59.packed_ref, bf16[256,512]{1,0:T(8,128)(2,1)S(1)} %copy-done.20), custom_call_target="tpu_custom_call" | custom-call | flops 100000 | bytes 10000 | tf_op jit(solution)/shard_map/pallas_call | solution.py:435
  99.0 2.2 %collective-permute-start.8 = (bf16[528,512]{1,0:T(8,128)(2,1)}, bf16[528,512]{1,0:T(8,128)(2,1)}, u32[]{:S(2)}, u32[]{:S(2)}) collective-permute-start(bf16[528,512]{1,0:T(8,128)(2,1)} %get-tuple-element.77), channel_id=1, source_target_pairs={{0,2},{2,4},{4,6},{6,8},{8,10},{10,12},{12,14},{14,16},{16,18},{18... | collective-permute-start | bytes 1622024 | tf_op jit(solution)/shard_map/ppermute | solution.py:449
  103.3 13.4 %all-to-all-start.2 = ((bf16[8,32,512]{2,1,0:T(8,128)(2,1)}), bf16[8,32,512]{2,1,0:T(8,128)(2,1)S(1)}, u32[]{:S(2)}, u32[]{:S(2)}) async-start(bf16[8,32,512]{2,1,0:T(8,128)(2,1)} %bitcast.9), calls=%async_computation.2 | async-start | bytes 524288 | tf_op jit(solution)/shard_map/all_to_all | solution.py:446
  116.7 6.2 %collective-permute-done.6.cross_ref = bf16[256,1024]{1,0:T(8,128)(2,1)} collective-permute-done((bf16[256,1024]{1,0:T(8,128)(2,1)}, bf16[256,1024]{1,0:T(8,128)(2,1)}, u32[]{:S(2)}, u32[]{:S(2)}) %collective-permute-start.6) | collective-permute-done | bytes 524320 | tf_op jit(solution)/shard_map/ppermute | solution.py:426
  122.9 4.3 %all-to-all-done.2.parts_ref = bf16[8,32,512]{2,1,0:T(8,128)(2,1)S(1)} async-done(((bf16[8,32,512]{2,1,0:T(8,128)(2,1)}), bf16[8,32,512]{2,1,0:T(8,128)(2,1)S(1)}, u32[]{:S(2)}, u32[]{:S(2)}) %all-to-all-start.2) | async-done | bytes 262176 | tf_op jit(solution)/shard_map/all_to_all | solution.py:446
  127.9 7.1 %all-to-all-start.3 = ((f32[4,32,512]{2,1,0:T(8,128)}), f32[4,32,512]{2,1,0:T(8,128)S(1)}, u32[]{:S(2)}, u32[]{:S(2)}) async-start(f32[4,32,512]{2,1,0:T(8,128)} %shard_map.97), calls=%async_computation.3 | async-start | bytes 524288 | tf_op jit(solution)/shard_map/all_to_all | solution.py:461
  135.0 2.6 %shard_map.99 = bf16[512,960]{1,0:T(8,128)(2,1)S(1)} custom-call(s32[1]{0:T(128)} %bitcast.3.core_ref, s32[1]{0:T(128)} %bitcast.7.half_ref, bf16[272,512]{1,0:T(8,128)(2,1)} %collective-permute-done.7.same_ref, bf16[256,1024]{1,0:T(8,128)(2,1)} %collective-permute-done.6.cross_ref, bf16[1024,512]{1,0:T(8,128)(2,1)S(1)} %bitcast.21, ...), custom_call_target="tpu_custom_call" | custom-call | flops 1000000000 | bytes 4000000 | tf_op jit(solution)/shard_map/pallas_call | solution.py:462
  139.3 2.5 %shard_map.100 = bf16[512,512]{1,0:T(8,128)(2,1)} custom-call(bf16[512,512]{1,0:T(8,128)(2,1)S(1)} %bitcast.27, f32[512,512]{1,0:T(8,128)S(1)} %copy-done.7, bf16[528,512]{1,0:T(8,128)(2,1)} %collective-permute-done.8.low_ref, bf16[528,512]{1,0:T(8,128)(2,1)} %collective-permute-done.9.high_ref, f32[8,512]{1,0:T(8,128)S(1)} %get-tuple-element.75.line_ref, ...), custom_call_target="tpu_custom_call" | custom-call | flops 10000000 | bytes 3000000 | tf_op jit(solution)/shard_map/pallas_call | solution.py:466
  (89 shorter events, 25.4 us)
Async XLA Ops:
  0.6 15.1 %copy-start.3 = (bf16[1,512,512]{2,1,0:T(8,128)(2,1)S(1)}, bf16[1,512,512]{2,1,0:T(8,128)(2,1)}, u32[]{:S(2)}) copy-start(bf16[1,512,512]{2,1,0:T(8,128)(2,1)} %param.7) | copy-start | bytes 1572868
  1.5 17.1 %copy-start.30 = (s32[1,1,256]{2,1,0:T(1,128)S(1)}, s32[1,1,256]{2,1,0:T(1,128)}, u32[]{:S(2)}) copy-start(s32[1,1,256]{2,1,0:T(1,128)} %param.10) | copy-start | bytes 3076
  2.6 43.4 %all-to-all-start = ((bf16[32,32,512]{2,1,0:T(8,128)(2,1)}), bf16[32,32,512]{2,1,0:T(8,128)(2,1)S(1)}, u32[]{:S(2)}, u32[]{:S(2)}) async-start(bf16[32,32,512]{2,1,0:T(8,128)(2,1)} %shard_map.85), calls=%async_computation | async-start | bytes 2097152 | tf_op jit(solution)/shard_map/all_to_all | solution.py:375
  15.7 20.4 %collective-permute-start.1 = (bf16[512,512]{1,0:T(8,128)(2,1)S(1)}, bf16[512,512]{1,0:T(8,128)(2,1)S(1)}, u32[]{:S(2)}, u32[]{:S(2)}) collective-permute-start(bf16[512,512]{1,0:T(8,128)(2,1)S(1)} %bitcast.24), channel_id=1, source_target_pairs={{0,2},{2,4},{4,6},{6,8},{8,10},{10,12},{12,14},{14,16},{16,18},{18... | collective-permute-start | bytes 1572872 | tf_op jit(solution)/shard_map/ppermute | solution.py:377
  17.2 18.9 %collective-permute-start.2 = (bf16[512,512]{1,0:T(8,128)(2,1)S(1)}, bf16[512,512]{1,0:T(8,128)(2,1)S(1)}, u32[]{:S(2)}, u32[]{:S(2)}) collective-permute-start(bf16[512,512]{1,0:T(8,128)(2,1)S(1)} %bitcast.25), channel_id=1, source_target_pairs={{2,0},{4,2},{6,4},{8,6},{10,8},{12,10},{14,12},{16,14},{18,16},{20... | collective-permute-start | bytes 1572872 | tf_op jit(solution)/shard_map/ppermute | solution.py:378
  20.3 8.8 %copy-start.29 = (s32[1,1,100,256]{3,1,2,0:T(1,128)S(1)}, s32[1,1,100,256]{3,1,2,0:T(1,128)}, u32[]{:S(2)}) copy-start(s32[1,1,100,256]{3,1,2,0:T(1,128)} %param.11) | copy-start | bytes 307204
  24.2 13.5 %collective-permute-start = (bf16[1024,256]{1,0:T(8,128)(2,1)}, bf16[1024,256]{1,0:T(8,128)(2,1)}, u32[]{:S(2)}, u32[]{:S(2)}) collective-permute-start(bf16[1024,256]{1,0:T(8,128)(2,1)} %get-tuple-element.44), channel_id=1, source_target_pairs={{0,2},{2,0},{4,6},{6,4},{8,10},{10,8},{12,14},{14,12},{16,18},{18,... | collective-permute-start | bytes 1572872 | tf_op jit(solution)/shard_map/ppermute | solution.py:389
  45.9 4.7 %copy-start.1 = (bf16[1536,512]{1,0:T(8,128)(2,1)S(1)}, bf16[1536,512]{1,0:T(8,128)(2,1)}, u32[]{:S(2)}) copy-start(bf16[1536,512]{1,0:T(8,128)(2,1)} %copy-done) | copy-start | bytes 4718596
  45.9 4.7 %collective-permute-start.3 = (bf16[1024,512]{1,0:T(8,128)(2,1)S(1)}, bf16[1024,512]{1,0:T(8,128)(2,1)S(1)}, u32[]{:S(2)}, u32[]{:S(2)}) collective-permute-start(bf16[1024,512]{1,0:T(8,128)(2,1)S(1)} %bitcast.18), channel_id=1, source_target_pairs={{0,2},{2,0},{4,6},{6,4},{8,10},{10,8},{12,14},{14,12},{16,18},{18,... | collective-permute-start | bytes 3145736 | tf_op jit(solution)/shard_map/ppermute | solution.py:402
  51.7 17.2 %copy-start.22 = (f32[256,128]{1,0:T(8,128)S(1)}, f32[256,128]{1,0:T(8,128)}, u32[]{:S(2)}) copy-start(f32[256,128]{1,0:T(8,128)} %copy-done.21) | copy-start | bytes 393220
  53.9 18.8 %copy-start.8 = (f32[272,128]{1,0:T(8,128)}, f32[272,128]{1,0:T(8,128)S(1)}, u32[]{:S(2)}) copy-start(f32[272,128]{1,0:T(8,128)S(1)} %get-tuple-element.56.sent_ref) | copy-start | bytes 417796
  53.9 14.9 %collective-permute-start.4 = (f32[272,128]{1,0:T(8,128)S(1)}, f32[272,128]{1,0:T(8,128)S(1)}, u32[]{:S(2)}, u32[]{:S(2)}) collective-permute-start(f32[272,128]{1,0:T(8,128)S(1)} %get-tuple-element.56.sent_ref), channel_id=1, source_target_pairs={{0,1},{1,0},{2,3},{3,2},{4,5},{5,4},{6,7},{7,6},{8,9},{9,8},{10,11... | collective-permute-start | bytes 417800 | tf_op jit(solution)/shard_map/ppermute | solution.py:411
  68.8 5.3 %copy-start.10 = (f32[272,128]{1,0:T(8,128)}, f32[272,128]{1,0:T(8,128)S(1)}, u32[]{:S(2)}) copy-start(f32[272,128]{1,0:T(8,128)S(1)} %collective-permute-done.4.got_ref) | copy-start | bytes 417796
  74.1 5.4 %copy-start.5 = (bf16[272,512]{1,0:T(8,128)(2,1)}, bf16[272,512]{1,0:T(8,128)(2,1)S(1)}, u32[]{:S(2)}) copy-start(bf16[272,512]{1,0:T(8,128)(2,1)S(1)} %get-tuple-element.72.dctx_ref.own_ref) | copy-start | bytes 835588
  74.1 5.4 %copy-start.23 = (f32[256,128]{1,0:T(8,128)}, f32[256,128]{1,0:T(8,128)S(1)}, u32[]{:S(2)}) copy-start(f32[256,128]{1,0:T(8,128)S(1)} %get-tuple-element.66.step_ref) | copy-start | bytes 393220
  74.1 3.6 %collective-permute-start.5 = (bf16[272,512]{1,0:T(8,128)(2,1)S(1)}, bf16[272,512]{1,0:T(8,128)(2,1)}, u32[]{:S(2)}, u32[]{:S(2)}) collective-permute-start(bf16[272,512]{1,0:T(8,128)(2,1)S(1)} %get-tuple-element.72.dctx_ref.own_ref), channel_id=1, source_target_pairs={{0,2},{2,0},{4,6},{6,4},{8,10},{10,8},{12,14},{14,12},{16,18},{18,... | collective-permute-start | bytes 835592 | tf_op jit(solution)/shard_map/ppermute | solution.py:420
  80.5 21.9 %all-to-all-start.1 = ((bf16[4,256,512]{2,1,0:T(8,128)(2,1)}), bf16[4,256,512]{2,1,0:T(8,128)(2,1)S(1)}, u32[]{:S(2)}, u32[]{:S(2)}) async-start(bf16[4,256,512]{2,1,0:T(8,128)(2,1)} %bitcast.23), calls=%async_computation.1 | async-start | bytes 2097152 | tf_op jit(solution)/shard_map/all_to_all | solution.py:432
  85.6 37.3 %collective-permute-start.6 = (bf16[256,1024]{1,0:T(8,128)(2,1)}, bf16[256,1024]{1,0:T(8,128)(2,1)}, u32[]{:S(2)}, u32[]{:S(2)}) collective-permute-start(bf16[256,1024]{1,0:T(8,128)(2,1)} %copy-done.12), channel_id=1, source_target_pairs={{0,385},{1,384},{128,1},{129,0},{256,129},{257,128},{384,257},{385... | collective-permute-start | bytes 1572872 | tf_op jit(solution)/shard_map/ppermute | solution.py:426
  89.3 27.4 %collective-permute-start.7 = (bf16[272,512]{1,0:T(8,128)(2,1)}, bf16[272,512]{1,0:T(8,128)(2,1)}, u32[]{:S(2)}, u32[]{:S(2)}) collective-permute-start(bf16[272,512]{1,0:T(8,128)(2,1)} %copy-done.5), channel_id=1, source_target_pairs={{0,384},{128,0},{256,128},{384,256},{1,385},{129,1},{257,129},{385... | collective-permute-start | bytes 835592 | tf_op jit(solution)/shard_map/ppermute | solution.py:431
  99.0 39.9 %collective-permute-start.8 = (bf16[528,512]{1,0:T(8,128)(2,1)}, bf16[528,512]{1,0:T(8,128)(2,1)}, u32[]{:S(2)}, u32[]{:S(2)}) collective-permute-start(bf16[528,512]{1,0:T(8,128)(2,1)} %get-tuple-element.77), channel_id=1, source_target_pairs={{0,2},{2,4},{4,6},{6,8},{8,10},{10,12},{12,14},{14,16},{16,18},{18... | collective-permute-start | bytes 1622024 | tf_op jit(solution)/shard_map/ppermute | solution.py:449
  101.2 37.7 %collective-permute-start.9 = (bf16[528,512]{1,0:T(8,128)(2,1)}, bf16[528,512]{1,0:T(8,128)(2,1)}, u32[]{:S(2)}, u32[]{:S(2)}) collective-permute-start(bf16[528,512]{1,0:T(8,128)(2,1)} %get-tuple-element.78), channel_id=1, source_target_pairs={{2,0},{4,2},{6,4},{8,6},{10,8},{12,10},{14,12},{16,14},{18,16},{20... | collective-permute-start | bytes 1622024 | tf_op jit(solution)/shard_map/ppermute | solution.py:450
  103.3 23.8 %all-to-all-start.2 = ((bf16[8,32,512]{2,1,0:T(8,128)(2,1)}), bf16[8,32,512]{2,1,0:T(8,128)(2,1)S(1)}, u32[]{:S(2)}, u32[]{:S(2)}) async-start(bf16[8,32,512]{2,1,0:T(8,128)(2,1)} %bitcast.9), calls=%async_computation.2 | async-start | bytes 524288 | tf_op jit(solution)/shard_map/all_to_all | solution.py:446
  127.9 13.9 %all-to-all-start.3 = ((f32[4,32,512]{2,1,0:T(8,128)}), f32[4,32,512]{2,1,0:T(8,128)S(1)}, u32[]{:S(2)}, u32[]{:S(2)}) async-start(f32[4,32,512]{2,1,0:T(8,128)} %shard_map.97), calls=%async_computation.3 | async-start | bytes 524288 | tf_op jit(solution)/shard_map/all_to_all | solution.py:461
  137.6 1.7 %copy-start.11 = (f32[272,128]{1,0:T(8,128)S(1)}, f32[272,128]{1,0:T(8,128)}, u32[]{:S(2)}) copy-start(f32[272,128]{1,0:T(8,128)} %copy-done.10) | copy-start | bytes 417796
  (21 other events, 21.1 us)

commit v4 on v3

--- a/solution.py
+++ b/solution.py
@@ -76,8 +76,13 @@
 def blocks_body(w_ref, out_ref):
     block = w_ref[...].astype(F32)
     block = jnp.concatenate([block, jnp.zeros((PAD - BLOCK, FEATS), F32)], axis=0).astype(BF16)
-    for i in range(PEERS):
+    for i in range(out_ref.shape[0]):
         out_ref[i] = block
+
+
+def copies_body(rows_ref, out_ref):
+    for i in range(out_ref.shape[0]):
+        out_ref[i] = rows_ref[...]
 
 
 def window_body(low_ref, own_ref, high_ref, window_ref, norm_ref):
@@ -371,8 +376,13 @@
         (2 * i + a, 2 * ((i - 1) % n_pipe) + 1 - a) for i in range(n_pipe) for a in range(2)
     ]
 
-    (w_blocks,) = call(blocks_body, [((PEERS, PAD, FEATS), BF16)], 0, 1, bytes_accessed=10**6)(w_proj)
-    w_own = lax.all_to_all(w_blocks, "dp", 0, 0, axis_index_groups=peers, tiled=True).reshape(HALF, FEATS)
+    (w_blocks,) = call(blocks_body, [((Z_CHIPS, PAD, FEATS), BF16)], 0, 1, bytes_accessed=10**5)(w_proj)
+    w_blocks = lax.all_to_all(w_blocks, "dp", 0, 0, axis_index_groups=in_z, tiled=True)
+    (w_blocks,) = call(
+        copies_body, [((X_CHIPS, HALF // X_CHIPS, FEATS), BF16)], 0, 1, bytes_accessed=10**6
+    )(w_blocks.reshape(HALF // X_CHIPS, FEATS))
+    w_own = lax.all_to_all(w_blocks, "dp", 0, 0, axis_index_groups=in_x, tiled=True).reshape(HALF, FEATS)
+
     own_targets = targets[0]
     low = lax.ppermute(own_targets, "dp", upward)
     high = lax.ppermute(own_targets, "dp", downward)

time: 145 us -> 142 us (0.979)
  starting transfers between devices: 64.1 us -> 60.2 us
    all_to_all x1, starting transfers between devices: 13.4 us -> 8.34 us  [local(): lax.all_to_all(share.reshape(Z_CHIPS, PAD, FEATS), 'dp', 0, 0, axis_index...]
    ppermute x1, waiting for transfers between devices: 6.21 us -> 11 us  [local(): cross = lax.ppermute(cross, ('pipe', 'param'), back_across)]
    all_to_all x1, waiting for transfers between devices: 4.26 us -> 0.01 us  [local(): lax.all_to_all(share.reshape(Z_CHIPS, PAD, FEATS), 'dp', 0, 0, axis_index...]
    ppermute x1, starting transfers between devices: 4.85 us -> 1.91 us  [local(): turned_got = lax.ppermute(turned_other, 'dp', swap)]
    all_to_all x1 -> x2, starting transfers between devices: 13.2 us -> 15.3 us  [the longest x1 10.4 us: local(): lax.all_to_all(w_blocks, 'dp', 0, 0, axis_index_groups=in_z, tiled=True)]
    all_to_all x1, starting transfers between devices: 7.08 us -> 8.81 us  [local(): pipe_parts = lax.all_to_all(copies, 'pipe', 0, 0, tiled=True)]
    all_to_all x1 -> x2, waiting for transfers between devices: 8.23 us -> 9.08 us  [the longest x1 9.08 us: local(): lax.all_to_all(w_blocks, 'dp', 0, 0, axis_index_groups=in_z, tiled=True)]
    unnamed x64 -> x56, local copies, waits for them, and re-layouts: 17.1 us -> 16.4 us
  transfers between devices with their start and end apart: 14 -> 15, of which waited for: 6 -> 6; matrix products, arithmetic and copies ran while one was open for 1% -> 1% of each run, Pallas kernels for 14% -> 15%
where the time goes in v4:
time: 142 us; the launch traced here: 140 us
  starting transfers between devices  60.2 us (42%)
  waiting for transfers between devices  30.9 us (22%)
  Pallas kernels  30.3 us (21%)
  local copies, waits for them, and re-layouts  16.6 us (12%)
  between operations  1.66 us (1%)
    unnamed x56, local copies, waits for them, and re-layouts  16.4 us
    ppermute x1, waiting for transfers between devices, local(): cross = lax.ppermute(cross, ('pipe', 'param'), back_across)  11 us
    all_to_all x1, starting transfers between devices, local(): lax.all_to_all(w_blocks, 'dp', 0, 0, axis_index_groups=in_z, tiled=True)  10.4 us
    ppermute x1, waiting for transfers between devices, local(): got = lax.ppermute(sent, 'param', [(0, 1), (1, 0)])  10 us
    all_to_all x1, waiting for transfers between devices, local(): lax.all_to_all(w_blocks, 'dp', 0, 0, axis_index_groups=in_z, tiled=True)  9.08 us
    all_to_all x1, starting transfers between devices, local(): pipe_parts = lax.all_to_all(copies, 'pipe', 0, 0, tiled=True)  8.81 us
    all_to_all x1, starting transfers between devices, local(): lax.all_to_all(share.reshape(Z_CHIPS, PAD, FEATS), 'dp', 0, 0, axis_index...  8.34 us
    pallas_call x1, Pallas kernels, local(): call(index_body, [((SLOTS, WORDS * LANES), I32), ((SLOTS, LANES), F32), (...  5.63 us
  transfers between devices with their start and end apart: 15, of which 6 were waited for; matrix products, arithmetic and copies ran while one was open for 1% of the time, Pallas kernels for 15%

profile of v4, /device:TPU:56, one launch (start us, length us, event | category | flops | bytes accessed | tf_op | source)
XLA Modules:
  0.0 139.7 jit_solution(12727913234082846662)
XLA Ops:
  2.1 10.4 %all-to-all-start = ((bf16[8,32,512]{2,1,0:T(8,128)(2,1)}), bf16[8,32,512]{2,1,0:T(8,128)(2,1)S(1)}, u32[]{:S(2)}, u32[]{:S(2)}) async-start(bf16[8,32,512]{2,1,0:T(8,128)(2,1)} %shard_map.85), calls=%async_computation | async-start | bytes 524288 | tf_op jit(solution)/shard_map/all_to_all | solution.py:380
  15.4 9.1 %all-to-all-done = bf16[8,32,512]{2,1,0:T(8,128)(2,1)S(1)} async-done(((bf16[8,32,512]{2,1,0:T(8,128)(2,1)}), bf16[8,32,512]{2,1,0:T(8,128)(2,1)S(1)}, u32[]{:S(2)}, u32[]{:S(2)}) %all-to-all-start) | async-done | bytes 262176 | tf_op jit(solution)/shard_map/all_to_all | solution.py:380
  25.5 4.8 %all-to-all-start.1 = ((bf16[4,256,512]{2,1,0:T(8,128)(2,1)}), bf16[4,256,512]{2,1,0:T(8,128)(2,1)S(1)}, u32[]{:S(2)}, u32[]{:S(2)}) async-start(bf16[4,256,512]{2,1,0:T(8,128)(2,1)} %shard_map.86), calls=%async_computation.1 | async-start | bytes 2097152 | tf_op jit(solution)/shard_map/all_to_all | solution.py:384
  30.5 1.5 %copy-done.24 = bf16[1,512,1920]{2,1,0:T(8,128)(2,1)S(1)} copy-done((bf16[1,512,1920]{2,1,0:T(8,128)(2,1)S(1)}, bf16[1,512,1920]{2,1,0:T(8,128)(2,1)}, u32[]{:S(2)}) %copy-start.24) | copy-done | bytes 1966104
  32.0 2.4 %shard_map.87 = (bf16[256,1024]{1,0:T(8,128)(2,1)S(1)}, bf16[256,1024]{1,0:T(8,128)(2,1)S(1)}, bf16[1024,256]{1,0:T(8,128)(2,1)S(1)}, bf16[1024,256]{1,0:T(8,128)(2,1)}) custom-call(s32[1]{0:T(128)} %bitcast.4.core_ref, s32[256,1]{1,0:T(8,128)S(1)} %copy.10.pos_ref, bf16[512,1920]{1,0:T(8,128)(2,1)S(1)} %bitcast.30), custom_call_target="tpu_custom_call" | custom-call | flops 2000000000 | bytes 4000000 | tf_op jit(solution)/shard_map/pallas_call | solution.py:394
  36.0 1.9 %collective-permute-start = (bf16[1024,256]{1,0:T(8,128)(2,1)}, bf16[1024,256]{1,0:T(8,128)(2,1)}, u32[]{:S(2)}, u32[]{:S(2)}) collective-permute-start(bf16[1024,256]{1,0:T(8,128)(2,1)} %get-tuple-element.44), channel_id=1, source_target_pairs={{0,2},{2,0},{4,6},{6,4},{8,10},{10,8},{12,14},{14,12},{16,18},{18,... | collective-permute-start | bytes 1572872 | tf_op jit(solution)/shard_map/ppermute | solution.py:399
  38.0 5.6 %shard_map.88 = (s32[256,384]{1,0:T(8,128)S(1)}, f32[256,128]{1,0:T(8,128)S(1)}, s32[256,128]{1,0:T(8,128)S(1)}) custom-call(s32[128,256]{1,0:T(8,128)S(1)} %pad.4.named_ref), custom_call_target="tpu_custom_call" | custom-call | flops 5000000000 | bytes 1000000 | tf_op jit(solution)/shard_map/pallas_call | solution.py:401
  45.2 2.5 %collective-permute-start.3 = (bf16[1024,512]{1,0:T(8,128)(2,1)S(1)}, bf16[1024,512]{1,0:T(8,128)(2,1)S(1)}, u32[]{:S(2)}, u32[]{:S(2)}) collective-permute-start(bf16[1024,512]{1,0:T(8,128)(2,1)S(1)} %bitcast.19), channel_id=1, source_target_pairs={{0,2},{2,0},{4,6},{6,4},{8,10},{10,8},{12,14},{14,12},{16,18},{18,... | collective-permute-start | bytes 3145736 | tf_op jit(solution)/shard_map/ppermute | solution.py:412
  51.0 2.3 %shard_map.91 = (f32[272,128]{1,0:T(8,128)S(1)}, f32[256,512]{1,0:T(8,128)S(1)}) custom-call(f32[256,512]{1,0:T(8,128)S(1)} %shard_map.90.part_ref, bf16[256,1024]{1,0:T(8,128)(2,1)S(1)} %copy-done.16, bf16[1024,512]{1,0:T(8,128)(2,1)S(1)} %collective-permute-done.3.w_other_ref, bf16[1536,512]{1,0:T(8,128)(2,1)S(1)} %copy-done.1, ...), custom_call_target="tpu_custom_call" | custom-call | flops 1000000000 | bytes 6000000 | tf_op jit(solution)/shard_map/pallas_call | solution.py:417
  53.3 4.7 %collective-permute-start.4 = (f32[272,128]{1,0:T(8,128)S(1)}, f32[272,128]{1,0:T(8,128)S(1)}, u32[]{:S(2)}, u32[]{:S(2)}) collective-permute-start(f32[272,128]{1,0:T(8,128)S(1)} %get-tuple-element.56.sent_ref), channel_id=1, source_target_pairs={{0,1},{1,0},{2,3},{3,2},{4,5},{5,4},{6,7},{7,6},{8,9},{9,8},{10,11... | collective-permute-start | bytes 417800 | tf_op jit(solution)/shard_map/ppermute | solution.py:421
  58.1 10.0 %collective-permute-done.4.got_ref = f32[272,128]{1,0:T(8,128)S(1)} collective-permute-done((f32[272,128]{1,0:T(8,128)S(1)}, f32[272,128]{1,0:T(8,128)S(1)}, u32[]{:S(2)}, u32[]{:S(2)}) %collective-permute-start.4) | collective-permute-done | bytes 139296 | tf_op jit(solution)/shard_map/ppermute | solution.py:421
  68.1 3.9 %shard_map.92 = (bf16[272,512]{1,0:T(8,128)(2,1)S(1)}, bf16[256,512]{1,0:T(8,128)(2,1)S(1)}, f32[256,128]{1,0:T(8,128)S(1)}, f32[256,128]{1,0:T(8,128)S(1)}) custom-call(s32[1]{0:T(128)} %bitcast.18.count_ref, s32[1,256]{1,0:T(1,128)S(1)} %broadcast_subtract_fusion.place_ref, f32[272,128]{1,0:T(8,128)S(1)} %get-tuple-element.56.sent_ref, ...), custom_call_target="tpu_custom_call" | custom-call | flops 500000000 | bytes 5000000 | tf_op jit(solution)/shard_map/pallas_call | solution.py:423
  74.1 1.9 %collective-permute-start.5 = (bf16[272,512]{1,0:T(8,128)(2,1)S(1)}, bf16[272,512]{1,0:T(8,128)(2,1)}, u32[]{:S(2)}, u32[]{:S(2)}) collective-permute-start(bf16[272,512]{1,0:T(8,128)(2,1)S(1)} %get-tuple-element.72.dctx_ref.own_ref), channel_id=1, source_target_pairs={{0,2},{2,0},{4,6},{6,4},{8,10},{10,8},{12,14},{14,12},{16,18},{18,... | collective-permute-start | bytes 835592 | tf_op jit(solution)/shard_map/ppermute | solution.py:430
  77.7 1.8 %shard_map.94 = bf16[1024,512]{1,0:T(8,128)(2,1)S(1)} custom-call(bf16[1024,256]{1,0:T(8,128)(2,1)S(1)} %get-tuple-element.61.turned_own_ref, bf16[1024,256]{1,0:T(8,128)(2,1)} %collective-permute-done.turned_got_ref, bf16[272,512]{1,0:T(8,128)(2,1)S(1)} %get-tuple-element.72.dctx_ref.own_ref, bf16[272,512]{1,0:T(8,128)(2,1)} %collective-permute-done.5.got_ref), custom_call_target="tpu_custom_call" | custom-call | flops 500000000 | bytes 3000000 | tf_op jit(solution)/shard_map/pallas_call | solution.py:437
  80.5 4.8 %all-to-all-start.2 = ((bf16[4,256,512]{2,1,0:T(8,128)(2,1)}), bf16[4,256,512]{2,1,0:T(8,128)(2,1)S(1)}, u32[]{:S(2)}, u32[]{:S(2)}) async-start(bf16[4,256,512]{2,1,0:T(8,128)(2,1)} %bitcast.24), calls=%async_computation.2 | async-start | bytes 2097152 | tf_op jit(solution)/shard_map/all_to_all | solution.py:442
  85.3 3.7 %collective-permute-start.6 = (bf16[256,1024]{1,0:T(8,128)(2,1)}, bf16[256,1024]{1,0:T(8,128)(2,1)}, u32[]{:S(2)}, u32[]{:S(2)}) collective-permute-start(bf16[256,1024]{1,0:T(8,128)(2,1)} %copy-done.12), channel_id=1, source_target_pairs={{0,385},{1,384},{128,1},{129,0},{256,129},{257,128},{384,257},{385... | collective-permute-start | bytes 1572872 | tf_op jit(solution)/shard_map/ppermute | solution.py:436
  89.0 2.0 %collective-permute-start.7 = (bf16[272,512]{1,0:T(8,128)(2,1)}, bf16[272,512]{1,0:T(8,128)(2,1)}, u32[]{:S(2)}, u32[]{:S(2)}) collective-permute-start(bf16[272,512]{1,0:T(8,128)(2,1)} %copy-done.5), channel_id=1, source_target_pairs={{0,384},{128,0},{256,128},{384,256},{1,385},{129,1},{257,129},{385... | collective-permute-start | bytes 835592 | tf_op jit(solution)/shard_map/ppermute | solution.py:441
  93.8 4.0 %shard_map.95 = (bf16[528,512]{1,0:T(8,128)(2,1)}, f32[512,512]{1,0:T(8,128)S(1)}, bf16[528,512]{1,0:T(8,128)(2,1)}, f32[8,512]{1,0:T(8,128)S(1)}) custom-call(f32[256,128]{1,0:T(8,128)S(1)} %copy-done.20, f32[256,128]{1,0:T(8,128)S(1)} %copy-done.22, s32[256,384]{1,0:T(8,128)S(1)} %get-tuple-element.59.packed_ref, bf16[256,512]{1,0:T(8,128)(2,1)S(1)} %copy-done.18), custom_call_target="tpu_custom_call" | custom-call | flops 100000 | bytes 10000 | tf_op jit(solution)/shard_map/pallas_call | solution.py:445
  98.8 2.2 %collective-permute-start.8 = (bf16[528,512]{1,0:T(8,128)(2,1)}, bf16[528,512]{1,0:T(8,128)(2,1)}, u32[]{:S(2)}, u32[]{:S(2)}) collective-permute-start(bf16[528,512]{1,0:T(8,128)(2,1)} %get-tuple-element.77), channel_id=1, source_target_pairs={{0,2},{2,4},{4,6},{6,8},{8,10},{10,12},{12,14},{14,16},{16,18},{18... | collective-permute-start | bytes 1622024 | tf_op jit(solution)/shard_map/ppermute | solution.py:459
  103.1 8.3 %all-to-all-start.3 = ((bf16[8,32,512]{2,1,0:T(8,128)(2,1)}), bf16[8,32,512]{2,1,0:T(8,128)(2,1)S(1)}, u32[]{:S(2)}, u32[]{:S(2)}) async-start(bf16[8,32,512]{2,1,0:T(8,128)(2,1)} %bitcast.10), calls=%async_computation.3 | async-start | bytes 524288 | tf_op jit(solution)/shard_map/all_to_all | solution.py:456
  111.7 11.0 %collective-permute-done.6.cross_ref = bf16[256,1024]{1,0:T(8,128)(2,1)} collective-permute-done((bf16[256,1024]{1,0:T(8,128)(2,1)}, bf16[256,1024]{1,0:T(8,128)(2,1)}, u32[]{:S(2)}, u32[]{:S(2)}) %collective-permute-start.6) | collective-permute-done | bytes 524320 | tf_op jit(solution)/shard_map/ppermute | solution.py:436
  123.4 8.8 %all-to-all-start.4 = ((f32[4,32,512]{2,1,0:T(8,128)}), f32[4,32,512]{2,1,0:T(8,128)S(1)}, u32[]{:S(2)}, u32[]{:S(2)}) async-start(f32[4,32,512]{2,1,0:T(8,128)} %shard_map.98), calls=%async_computation.4 | async-start | bytes 524288 | tf_op jit(solution)/shard_map/all_to_all | solution.py:471
  132.2 2.6 %shard_map.100 = bf16[512,960]{1,0:T(8,128)(2,1)S(1)} custom-call(s32[1]{0:T(128)} %bitcast.4.core_ref, s32[1]{0:T(128)} %bitcast.8.half_ref, bf16[272,512]{1,0:T(8,128)(2,1)} %collective-permute-done.7.same_ref, bf16[256,1024]{1,0:T(8,128)(2,1)} %collective-permute-done.6.cross_ref, bf16[1024,512]{1,0:T(8,128)(2,1)S(1)} %bitcast.22, ...), custom_call_target="tpu_custom_call" | custom-call | flops 1000000000 | bytes 4000000 | tf_op jit(solution)/shard_map/pallas_call | solution.py:472
  136.5 2.5 %shard_map.101 = bf16[512,512]{1,0:T(8,128)(2,1)} custom-call(bf16[512,512]{1,0:T(8,128)(2,1)S(1)} %bitcast.28, f32[512,512]{1,0:T(8,128)S(1)} %copy-done.7, bf16[528,512]{1,0:T(8,128)(2,1)} %collective-permute-done.8.low_ref, bf16[528,512]{1,0:T(8,128)(2,1)} %collective-permute-done.9.high_ref, f32[8,512]{1,0:T(8,128)S(1)} %get-tuple-element.75.line_ref, ...), custom_call_target="tpu_custom_call" | custom-call | flops 10000000 | bytes 3000000 | tf_op jit(solution)/shard_map/pallas_call | solution.py:476
  (84 shorter events, 25.2 us)
Async XLA Ops:
  2.1 28.2 %copy-start.26 = (s32[1,1,256]{2,1,0:T(1,128)S(1)}, s32[1,1,256]{2,1,0:T(1,128)}, u32[]{:S(2)}) copy-start(s32[1,1,256]{2,1,0:T(1,128)} %param.10) | copy-start | bytes 3076
  2.1 22.3 %all-to-all-start = ((bf16[8,32,512]{2,1,0:T(8,128)(2,1)}), bf16[8,32,512]{2,1,0:T(8,128)(2,1)S(1)}, u32[]{:S(2)}, u32[]{:S(2)}) async-start(bf16[8,32,512]{2,1,0:T(8,128)(2,1)} %shard_map.85), calls=%async_computation | async-start | bytes 524288 | tf_op jit(solution)/shard_map/all_to_all | solution.py:380
  12.6 31.0 %collective-permute-start.1 = (bf16[512,512]{1,0:T(8,128)(2,1)}, bf16[512,512]{1,0:T(8,128)(2,1)S(1)}, u32[]{:S(2)}, u32[]{:S(2)}) collective-permute-start(bf16[512,512]{1,0:T(8,128)(2,1)} %bitcast.25), channel_id=1, source_target_pairs={{0,2},{2,4},{4,6},{6,8},{8,10},{10,12},{12,14},{14,16},{16,18},{18... | collective-permute-start | bytes 1572872 | tf_op jit(solution)/shard_map/ppermute | solution.py:387
  14.1 29.5 %collective-permute-start.2 = (bf16[512,512]{1,0:T(8,128)(2,1)}, bf16[512,512]{1,0:T(8,128)(2,1)S(1)}, u32[]{:S(2)}, u32[]{:S(2)}) collective-permute-start(bf16[512,512]{1,0:T(8,128)(2,1)} %bitcast.26), channel_id=1, source_target_pairs={{2,0},{4,2},{6,4},{8,6},{10,8},{12,10},{14,12},{16,14},{18,16},{20... | collective-permute-start | bytes 1572872 | tf_op jit(solution)/shard_map/ppermute | solution.py:388
  25.5 19.7 %all-to-all-start.1 = ((bf16[4,256,512]{2,1,0:T(8,128)(2,1)}), bf16[4,256,512]{2,1,0:T(8,128)(2,1)S(1)}, u32[]{:S(2)}, u32[]{:S(2)}) async-start(bf16[4,256,512]{2,1,0:T(8,128)(2,1)} %shard_map.86), calls=%async_computation.1 | async-start | bytes 2097152 | tf_op jit(solution)/shard_map/all_to_all | solution.py:384
  32.0 5.9 %copy-start.25 = (s32[1,1,100,256]{3,1,2,0:T(1,128)S(1)}, s32[1,1,100,256]{3,1,2,0:T(1,128)}, u32[]{:S(2)}) copy-start(s32[1,1,100,256]{3,1,2,0:T(1,128)} %param.11) | copy-start | bytes 307204
  36.0 9.2 %collective-permute-start = (bf16[1024,256]{1,0:T(8,128)(2,1)}, bf16[1024,256]{1,0:T(8,128)(2,1)}, u32[]{:S(2)}, u32[]{:S(2)}) collective-permute-start(bf16[1024,256]{1,0:T(8,128)(2,1)} %get-tuple-element.44), channel_id=1, source_target_pairs={{0,2},{2,0},{4,6},{6,4},{8,10},{10,8},{12,14},{14,12},{16,18},{18,... | collective-permute-start | bytes 1572872 | tf_op jit(solution)/shard_map/ppermute | solution.py:399
  37.9 5.7 %copy-start.3 = (bf16[1,512,512]{2,1,0:T(8,128)(2,1)S(1)}, bf16[1,512,512]{2,1,0:T(8,128)(2,1)}, u32[]{:S(2)}) copy-start(bf16[1,512,512]{2,1,0:T(8,128)(2,1)} %param.7) | copy-start | bytes 1572868
  45.2 4.8 %copy-start.1 = (bf16[1536,512]{1,0:T(8,128)(2,1)S(1)}, bf16[1536,512]{1,0:T(8,128)(2,1)}, u32[]{:S(2)}) copy-start(bf16[1536,512]{1,0:T(8,128)(2,1)} %copy-done) | copy-start | bytes 4718596
  45.2 4.8 %collective-permute-start.3 = (bf16[1024,512]{1,0:T(8,128)(2,1)S(1)}, bf16[1024,512]{1,0:T(8,128)(2,1)S(1)}, u32[]{:S(2)}, u32[]{:S(2)}) collective-permute-start(bf16[1024,512]{1,0:T(8,128)(2,1)S(1)} %bitcast.19), channel_id=1, source_target_pairs={{0,2},{2,0},{4,6},{6,4},{8,10},{10,8},{12,14},{14,12},{16,18},{18,... | collective-permute-start | bytes 3145736 | tf_op jit(solution)/shard_map/ppermute | solution.py:412
  53.3 18.7 %copy-start.8 = (f32[272,128]{1,0:T(8,128)}, f32[272,128]{1,0:T(8,128)S(1)}, u32[]{:S(2)}) copy-start(f32[272,128]{1,0:T(8,128)S(1)} %get-tuple-element.56.sent_ref) | copy-start | bytes 417796
  53.3 14.8 %collective-permute-start.4 = (f32[272,128]{1,0:T(8,128)S(1)}, f32[272,128]{1,0:T(8,128)S(1)}, u32[]{:S(2)}, u32[]{:S(2)}) collective-permute-start(f32[272,128]{1,0:T(8,128)S(1)} %get-tuple-element.56.sent_ref), channel_id=1, source_target_pairs={{0,1},{1,0},{2,3},{3,2},{4,5},{5,4},{6,7},{7,6},{8,9},{9,8},{10,11... | collective-permute-start | bytes 417800 | tf_op jit(solution)/shard_map/ppermute | solution.py:421
  68.1 6.0 %copy-start.10 = (f32[272,128]{1,0:T(8,128)}, f32[272,128]{1,0:T(8,128)S(1)}, u32[]{:S(2)}) copy-start(f32[272,128]{1,0:T(8,128)S(1)} %collective-permute-done.4.got_ref) | copy-start | bytes 417796
  74.1 5.4 %copy-start.5 = (bf16[272,512]{1,0:T(8,128)(2,1)}, bf16[272,512]{1,0:T(8,128)(2,1)S(1)}, u32[]{:S(2)}) copy-start(bf16[272,512]{1,0:T(8,128)(2,1)S(1)} %get-tuple-element.72.dctx_ref.own_ref) | copy-start | bytes 835588
  74.1 3.6 %collective-permute-start.5 = (bf16[272,512]{1,0:T(8,128)(2,1)S(1)}, bf16[272,512]{1,0:T(8,128)(2,1)}, u32[]{:S(2)}, u32[]{:S(2)}) collective-permute-start(bf16[272,512]{1,0:T(8,128)(2,1)S(1)} %get-tuple-element.72.dctx_ref.own_ref), channel_id=1, source_target_pairs={{0,2},{2,0},{4,6},{6,4},{8,10},{10,8},{12,14},{14,12},{16,18},{18,... | collective-permute-start | bytes 835592 | tf_op jit(solution)/shard_map/ppermute | solution.py:430
  80.5 21.7 %all-to-all-start.2 = ((bf16[4,256,512]{2,1,0:T(8,128)(2,1)}), bf16[4,256,512]{2,1,0:T(8,128)(2,1)S(1)}, u32[]{:S(2)}, u32[]{:S(2)}) async-start(bf16[4,256,512]{2,1,0:T(8,128)(2,1)} %bitcast.24), calls=%async_computation.2 | async-start | bytes 2097152 | tf_op jit(solution)/shard_map/all_to_all | solution.py:442
  85.3 37.3 %collective-permute-start.6 = (bf16[256,1024]{1,0:T(8,128)(2,1)}, bf16[256,1024]{1,0:T(8,128)(2,1)}, u32[]{:S(2)}, u32[]{:S(2)}) collective-permute-start(bf16[256,1024]{1,0:T(8,128)(2,1)} %copy-done.12), channel_id=1, source_target_pairs={{0,385},{1,384},{128,1},{129,0},{256,129},{257,128},{384,257},{385... | collective-permute-start | bytes 1572872 | tf_op jit(solution)/shard_map/ppermute | solution.py:436
  89.0 22.7 %collective-permute-start.7 = (bf16[272,512]{1,0:T(8,128)(2,1)}, bf16[272,512]{1,0:T(8,128)(2,1)}, u32[]{:S(2)}, u32[]{:S(2)}) collective-permute-start(bf16[272,512]{1,0:T(8,128)(2,1)} %copy-done.5), channel_id=1, source_target_pairs={{0,384},{128,0},{256,128},{384,256},{1,385},{129,1},{257,129},{385... | collective-permute-start | bytes 835592 | tf_op jit(solution)/shard_map/ppermute | solution.py:441
  98.8 37.3 %collective-permute-start.8 = (bf16[528,512]{1,0:T(8,128)(2,1)}, bf16[528,512]{1,0:T(8,128)(2,1)}, u32[]{:S(2)}, u32[]{:S(2)}) collective-permute-start(bf16[528,512]{1,0:T(8,128)(2,1)} %get-tuple-element.77), channel_id=1, source_target_pairs={{0,2},{2,4},{4,6},{6,8},{8,10},{10,12},{12,14},{14,16},{16,18},{18... | collective-permute-start | bytes 1622024 | tf_op jit(solution)/shard_map/ppermute | solution.py:459
  100.9 35.2 %collective-permute-start.9 = (bf16[528,512]{1,0:T(8,128)(2,1)}, bf16[528,512]{1,0:T(8,128)(2,1)}, u32[]{:S(2)}, u32[]{:S(2)}) collective-permute-start(bf16[528,512]{1,0:T(8,128)(2,1)} %get-tuple-element.78), channel_id=1, source_target_pairs={{2,0},{4,2},{6,4},{8,6},{10,8},{12,10},{14,12},{16,14},{18,16},{20... | collective-permute-start | bytes 1622024 | tf_op jit(solution)/shard_map/ppermute | solution.py:460
  103.1 19.6 %all-to-all-start.3 = ((bf16[8,32,512]{2,1,0:T(8,128)(2,1)}), bf16[8,32,512]{2,1,0:T(8,128)(2,1)S(1)}, u32[]{:S(2)}, u32[]{:S(2)}) async-start(bf16[8,32,512]{2,1,0:T(8,128)(2,1)} %bitcast.10), calls=%async_computation.3 | async-start | bytes 524288 | tf_op jit(solution)/shard_map/all_to_all | solution.py:456
  123.4 15.7 %all-to-all-start.4 = ((f32[4,32,512]{2,1,0:T(8,128)}), f32[4,32,512]{2,1,0:T(8,128)S(1)}, u32[]{:S(2)}, u32[]{:S(2)}) async-start(f32[4,32,512]{2,1,0:T(8,128)} %shard_map.98), calls=%async_computation.4 | async-start | bytes 524288 | tf_op jit(solution)/shard_map/all_to_all | solution.py:471
  134.8 1.7 %copy-start.9 = (f32[272,128]{1,0:T(8,128)S(1)}, f32[272,128]{1,0:T(8,128)}, u32[]{:S(2)}) copy-start(f32[272,128]{1,0:T(8,128)} %copy-done.8) | copy-start | bytes 417796
  134.8 1.7 %copy-start.11 = (f32[272,128]{1,0:T(8,128)S(1)}, f32[272,128]{1,0:T(8,128)}, u32[]{:S(2)}) copy-start(f32[272,128]{1,0:T(8,128)} %copy-done.10) | copy-start | bytes 417796
  (18 other events, 17.7 us)

commit v5 on v4

--- a/solution.py
+++ b/solution.py
@@ -204,7 +204,7 @@
 
 def slots_body(
     count_ref, place_ref, sent_ref, got_ref, context_ref, frame_ref, times_ref, packed_ref, window_ref,
-    dctx_ref, unit_ref, step_ref, along_ref, inverse_ref, shift_ref, scores_ref,
+    dctx_ref, unit_ref, pair_ref, inverse_ref, shift_ref, scores_ref,
 ):
     inv_tgt = 1.0 / jnp.sqrt(
         sent_ref[SLOTS : SLOTS + 16, :] + got_ref[SLOTS : SLOTS + 16, :] + epsilon
@@ -233,8 +233,8 @@
         step = step * times
         weight = (step * scale).astype(BF16).astype(F32)
         along = jnp.sum(jnp.where(named, weight * raw / times, 0.0), axis=1, keepdims=True)
-        step_ref[rows, :] = step
-        along_ref[rows, :] = jnp.where(named, step.astype(BF16).astype(F32) * raw * inverse, 0.0)
+        pair_ref[rows, 0:LANES] = step
+        pair_ref[rows, LANES : 2 * LANES] = jnp.where(named, step.astype(BF16).astype(F32) * raw * inverse, 0.0)
         inverse_ref[rows, :] = jnp.broadcast_to(inverse, (GROUP, LANES))
         shift_ref[rows, :] = jnp.broadcast_to(along * inverse * inverse * inverse, (GROUP, LANES))
         for t, column in columns_of(packed_ref, rows):
@@ -253,13 +253,13 @@
     unit_ref[...] = (context * inverse).astype(BF16)
 
 
-def frames_body(step_ref, along_ref, packed_ref, unit_ref, low_ref, own_ref, high_ref, line_ref, scores_ref, sums_ref):
+def frames_body(pair_ref, packed_ref, unit_ref, low_ref, own_ref, high_ref, line_ref, scores_ref, sums_ref):
     sums_ref[...] = jnp.zeros((8, WINDOW), F32)
 
     def group(g, carry):
         rows = pl.ds(pl.multiple_of(g * GROUP, GROUP), GROUP)
-        step = step_ref[rows, :]
-        along = along_ref[rows, :]
+        step = pair_ref[rows, 0:LANES]
+        along = pair_ref[rows, LANES : 2 * LANES]
         for t, column in columns_of(packed_ref, rows):
             span = slice(LANES * t, LANES * (t + 1))
             scores_ref[rows, span] = lookup(step, column).astype(BF16)
@@ -420,9 +420,9 @@
     )(part, rows_other, w_other, window, frames, norms)
     got = lax.ppermute(sent, "param", [(0, 1), (1, 0)])
 
-    dctx, unit, step, along = call(
+    dctx, unit, pair = call(
         slots_body,
-        [((SLOTS + 16, FEATS), BF16), ((SLOTS, FEATS), BF16)] + [((SLOTS, LANES), F32)] * 2,
+        [((SLOTS + 16, FEATS), BF16), ((SLOTS, FEATS), BF16), ((SLOTS, 2 * LANES), F32)],
         1, 8,
         scratch=[pltpu.VMEM((SLOTS, LANES), F32)] * 2 + [pltpu.VMEM((SLOTS, WINDOW), BF16)],
         flops=5 * 10**8, bytes_accessed=5 * 10**6,
@@ -437,7 +437,7 @@
     (share,) = call(
         share_body, [((HALF, FEATS), BF16)], 0, 4, flops=5 * 10**8, bytes_accessed=3 * 10**6
     )(turned_own, turned_got, dctx, dctx_got)
-    step, share, dctx = lax.optimization_barrier((step, share, dctx))
+    pair, share, dctx = lax.optimization_barrier((pair, share, dctx))
     same = lax.ppermute(dctx, "pipe", back)
     shares = lax.all_to_all(
         share.reshape(X_CHIPS, HALF // X_CHIPS, FEATS), "dp", 0, 0, axis_index_groups=in_x, tiled=True
@@ -445,10 +445,10 @@
     to_low, dtgt, to_high, line = call(
         frames_body,
         [((FRAMES + 16, FEATS), BF16), ((FRAMES, FEATS), F32), ((FRAMES + 16, FEATS), BF16), ((8, FRAMES), F32)],
-        0, 4,
+        0, 3,
         scratch=[pltpu.VMEM((SLOTS, WINDOW), BF16), pltpu.VMEM((8, WINDOW), F32)],
         flops=10**5, bytes_accessed=10**4,
-    )(step, along, packed, unit)
+    )(pair, packed, unit)
     shares, line = lax.optimization_barrier((shares, line))
     (share,) = call(
         merge_body, [((HALF // X_CHIPS, FEATS), BF16)], 0, 1, flops=10**6, bytes_accessed=10**6

time: 142 us -> 141 us (level)
  local copies, waits for them, and re-layouts: 16.6 us -> 15.1 us
    unnamed x56 -> x52, local copies, waits for them, and re-layouts: 16.4 us -> 15 us
where the time goes in v5:
time: 141 us; the launch traced here: 139 us
  starting transfers between devices  60.3 us (43%)
  waiting for transfers between devices  31.7 us (22%)
  Pallas kernels  30.3 us (21%)
  local copies, waits for them, and re-layouts  15.1 us (11%)
  between operations  1.65 us (1%)
    unnamed x52, local copies, waits for them, and re-layouts  15 us
    ppermute x1, waiting for transfers between devices, local(): cross = lax.ppermute(cross, ('pipe', 'param'), back_across)  11 us
    all_to_all x1, starting transfers between devices, local(): lax.all_to_all(w_blocks, 'dp', 0, 0, axis_index_groups=in_z, tiled=True)  10.4 us
    ppermute x1, waiting for transfers between devices, local(): got = lax.ppermute(sent, 'param', [(0, 1), (1, 0)])  10 us
    all_to_all x1, waiting for transfers between devices, local(): lax.all_to_all(w_blocks, 'dp', 0, 0, axis_index_groups=in_z, tiled=True)  9.08 us
    all_to_all x1, starting transfers between devices, local(): pipe_parts = lax.all_to_all(copies, 'pipe', 0, 0, tiled=True)  8.81 us
    all_to_all x1, starting transfers between devices, local(): lax.all_to_all(share.reshape(Z_CHIPS, PAD, FEATS), 'dp', 0, 0, axis_index...  8.34 us
    pallas_call x1, Pallas kernels, local(): call(index_body, [((SLOTS, WORDS * LANES), I32), ((SLOTS, LANES), F32), (...  5.63 us
  transfers between devices with their start and end apart: 15, of which 6 were waited for; matrix products, arithmetic and copies ran while one was open for 1% of the time, Pallas kernels for 15%

profile of v5, /device:TPU:56, one launch (start us, length us, event | category | flops | bytes accessed | tf_op | source)
XLA Modules:
  0.0 139.1 jit_solution(12907803279081325597)
XLA Ops:
  2.1 10.4 %all-to-all-start = ((bf16[8,32,512]{2,1,0:T(8,128)(2,1)}), bf16[8,32,512]{2,1,0:T(8,128)(2,1)S(1)}, u32[]{:S(2)}, u32[]{:S(2)}) async-start(bf16[8,32,512]{2,1,0:T(8,128)(2,1)} %shard_map.85), calls=%async_computation | async-start | bytes 524288 | tf_op jit(solution)/shard_map/all_to_all | solution.py:380
  15.4 9.1 %all-to-all-done = bf16[8,32,512]{2,1,0:T(8,128)(2,1)S(1)} async-done(((bf16[8,32,512]{2,1,0:T(8,128)(2,1)}), bf16[8,32,512]{2,1,0:T(8,128)(2,1)S(1)}, u32[]{:S(2)}, u32[]{:S(2)}) %all-to-all-start) | async-done | bytes 262176 | tf_op jit(solution)/shard_map/all_to_all | solution.py:380
  25.5 4.8 %all-to-all-start.1 = ((bf16[4,256,512]{2,1,0:T(8,128)(2,1)}), bf16[4,256,512]{2,1,0:T(8,128)(2,1)S(1)}, u32[]{:S(2)}, u32[]{:S(2)}) async-start(bf16[4,256,512]{2,1,0:T(8,128)(2,1)} %shard_map.86), calls=%async_computation.1 | async-start | bytes 2097152 | tf_op jit(solution)/shard_map/all_to_all | solution.py:384
  30.5 1.5 %copy-done.22 = bf16[1,512,1920]{2,1,0:T(8,128)(2,1)S(1)} copy-done((bf16[1,512,1920]{2,1,0:T(8,128)(2,1)S(1)}, bf16[1,512,1920]{2,1,0:T(8,128)(2,1)}, u32[]{:S(2)}) %copy-start.22) | copy-done | bytes 1966104
  32.0 2.4 %shard_map.87 = (bf16[256,1024]{1,0:T(8,128)(2,1)S(1)}, bf16[256,1024]{1,0:T(8,128)(2,1)S(1)}, bf16[1024,256]{1,0:T(8,128)(2,1)S(1)}, bf16[1024,256]{1,0:T(8,128)(2,1)}) custom-call(s32[1]{0:T(128)} %bitcast.4.core_ref, s32[256,1]{1,0:T(8,128)S(1)} %copy.10.pos_ref, bf16[512,1920]{1,0:T(8,128)(2,1)S(1)} %bitcast.30), custom_call_target="tpu_custom_call" | custom-call | flops 2000000000 | bytes 4000000 | tf_op jit(solution)/shard_map/pallas_call | solution.py:394
  36.0 1.9 %collective-permute-start = (bf16[1024,256]{1,0:T(8,128)(2,1)}, bf16[1024,256]{1,0:T(8,128)(2,1)}, u32[]{:S(2)}, u32[]{:S(2)}) collective-permute-start(bf16[1024,256]{1,0:T(8,128)(2,1)} %get-tuple-element.43), channel_id=1, source_target_pairs={{0,2},{2,0},{4,6},{6,4},{8,10},{10,8},{12,14},{14,12},{16,18},{18,... | collective-permute-start | bytes 1572872 | tf_op jit(solution)/shard_map/ppermute | solution.py:399
  38.0 5.6 %shard_map.88 = (s32[256,384]{1,0:T(8,128)S(1)}, f32[256,128]{1,0:T(8,128)S(1)}, s32[256,128]{1,0:T(8,128)S(1)}) custom-call(s32[128,256]{1,0:T(8,128)S(1)} %pad.4.named_ref), custom_call_target="tpu_custom_call" | custom-call | flops 5000000000 | bytes 1000000 | tf_op jit(solution)/shard_map/pallas_call | solution.py:401
  45.2 2.5 %collective-permute-start.3 = (bf16[1024,512]{1,0:T(8,128)(2,1)S(1)}, bf16[1024,512]{1,0:T(8,128)(2,1)S(1)}, u32[]{:S(2)}, u32[]{:S(2)}) collective-permute-start(bf16[1024,512]{1,0:T(8,128)(2,1)S(1)} %bitcast.19), channel_id=1, source_target_pairs={{0,2},{2,0},{4,6},{6,4},{8,10},{10,8},{12,14},{14,12},{16,18},{18,... | collective-permute-start | bytes 3145736 | tf_op jit(solution)/shard_map/ppermute | solution.py:412
  51.1 2.3 %shard_map.91 = (f32[272,128]{1,0:T(8,128)S(1)}, f32[256,512]{1,0:T(8,128)S(1)}) custom-call(f32[256,512]{1,0:T(8,128)S(1)} %shard_map.90.part_ref, bf16[256,1024]{1,0:T(8,128)(2,1)S(1)} %copy-done.16, bf16[1024,512]{1,0:T(8,128)(2,1)S(1)} %collective-permute-done.3.w_other_ref, bf16[1536,512]{1,0:T(8,128)(2,1)S(1)} %copy-done.1, ...), custom_call_target="tpu_custom_call" | custom-call | flops 1000000000 | bytes 6000000 | tf_op jit(solution)/shard_map/pallas_call | solution.py:417
  53.4 4.7 %collective-permute-start.4 = (f32[272,128]{1,0:T(8,128)S(1)}, f32[272,128]{1,0:T(8,128)S(1)}, u32[]{:S(2)}, u32[]{:S(2)}) collective-permute-start(f32[272,128]{1,0:T(8,128)S(1)} %get-tuple-element.55.sent_ref), channel_id=1, source_target_pairs={{0,1},{1,0},{2,3},{3,2},{4,5},{5,4},{6,7},{7,6},{8,9},{9,8},{10,11... | collective-permute-start | bytes 417800 | tf_op jit(solution)/shard_map/ppermute | solution.py:421
  58.1 10.0 %collective-permute-done.4.got_ref = f32[272,128]{1,0:T(8,128)S(1)} collective-permute-done((f32[272,128]{1,0:T(8,128)S(1)}, f32[272,128]{1,0:T(8,128)S(1)}, u32[]{:S(2)}, u32[]{:S(2)}) %collective-permute-start.4) | collective-permute-done | bytes 139296 | tf_op jit(solution)/shard_map/ppermute | solution.py:421
  68.1 3.9 %shard_map.92 = (bf16[272,512]{1,0:T(8,128)(2,1)S(1)}, bf16[256,512]{1,0:T(8,128)(2,1)S(1)}, f32[256,256]{1,0:T(8,128)S(1)}) custom-call(s32[1]{0:T(128)} %bitcast.18.count_ref, s32[1,256]{1,0:T(1,128)S(1)} %broadcast_subtract_fusion.place_ref, f32[272,128]{1,0:T(8,128)S(1)} %get-tuple-element.55.sent_ref, f32[272,128]{1,0:T(8,128)S(1)} %collective-permute-done.4.got_ref, ...), custom_call_target="tpu_custom_call" | custom-call | flops 500000000 | bytes 5000000 | tf_op jit(solution)/shard_map/pallas_call | solution.py:423
  73.5 1.9 %collective-permute-start.5 = (bf16[272,512]{1,0:T(8,128)(2,1)S(1)}, bf16[272,512]{1,0:T(8,128)(2,1)}, u32[]{:S(2)}, u32[]{:S(2)}) collective-permute-start(bf16[272,512]{1,0:T(8,128)(2,1)S(1)} %get-tuple-element.70.dctx_ref.own_ref), channel_id=1, source_target_pairs={{0,2},{2,0},{4,6},{6,4},{8,10},{10,8},{12,14},{14,12},{16,18},{18,... | collective-permute-start | bytes 835592 | tf_op jit(solution)/shard_map/ppermute | solution.py:430
  77.1 1.8 %shard_map.94 = bf16[1024,512]{1,0:T(8,128)(2,1)S(1)} custom-call(bf16[1024,256]{1,0:T(8,128)(2,1)S(1)} %get-tuple-element.60.turned_own_ref, bf16[1024,256]{1,0:T(8,128)(2,1)} %collective-permute-done.turned_got_ref, bf16[272,512]{1,0:T(8,128)(2,1)S(1)} %get-tuple-element.70.dctx_ref.own_ref, bf16[272,512]{1,0:T(8,128)(2,1)} %collective-permute-done.5.got_ref), custom_call_target="tpu_custom_call" | custom-call | flops 500000000 | bytes 3000000 | tf_op jit(solution)/shard_map/pallas_call | solution.py:437
  79.9 4.8 %all-to-all-start.2 = ((bf16[4,256,512]{2,1,0:T(8,128)(2,1)}), bf16[4,256,512]{2,1,0:T(8,128)(2,1)S(1)}, u32[]{:S(2)}, u32[]{:S(2)}) async-start(bf16[4,256,512]{2,1,0:T(8,128)(2,1)} %bitcast.24), calls=%async_computation.2 | async-start | bytes 2097152 | tf_op jit(solution)/shard_map/all_to_all | solution.py:442
  84.7 3.7 %collective-permute-start.6 = (bf16[256,1024]{1,0:T(8,128)(2,1)}, bf16[256,1024]{1,0:T(8,128)(2,1)}, u32[]{:S(2)}, u32[]{:S(2)}) collective-permute-start(bf16[256,1024]{1,0:T(8,128)(2,1)} %copy-done.12), channel_id=1, source_target_pairs={{0,385},{1,384},{128,1},{129,0},{256,129},{257,128},{384,257},{385... | collective-permute-start | bytes 1572872 | tf_op jit(solution)/shard_map/ppermute | solution.py:436
  88.4 2.0 %collective-permute-start.7 = (bf16[272,512]{1,0:T(8,128)(2,1)}, bf16[272,512]{1,0:T(8,128)(2,1)}, u32[]{:S(2)}, u32[]{:S(2)}) collective-permute-start(bf16[272,512]{1,0:T(8,128)(2,1)} %copy-done.5), channel_id=1, source_target_pairs={{0,384},{128,0},{256,128},{384,256},{1,385},{129,1},{257,129},{385... | collective-permute-start | bytes 835592 | tf_op jit(solution)/shard_map/ppermute | solution.py:441
  92.3 4.0 %shard_map.95 = (bf16[528,512]{1,0:T(8,128)(2,1)}, f32[512,512]{1,0:T(8,128)S(1)}, bf16[528,512]{1,0:T(8,128)(2,1)}, f32[8,512]{1,0:T(8,128)S(1)}) custom-call(f32[256,256]{1,0:T(8,128)S(1)} %copy-done.20, s32[256,384]{1,0:T(8,128)S(1)} %get-tuple-element.58.packed_ref, bf16[256,512]{1,0:T(8,128)(2,1)S(1)} %copy-done.18), custom_call_target="tpu_custom_call" | custom-call | flops 100000 | bytes 10000 | tf_op jit(solution)/shard_map/pallas_call | solution.py:445
  97.3 2.2 %collective-permute-start.8 = (bf16[528,512]{1,0:T(8,128)(2,1)}, bf16[528,512]{1,0:T(8,128)(2,1)}, u32[]{:S(2)}, u32[]{:S(2)}) collective-permute-start(bf16[528,512]{1,0:T(8,128)(2,1)} %get-tuple-element.75), channel_id=1, source_target_pairs={{0,2},{2,4},{4,6},{6,8},{8,10},{10,12},{12,14},{14,16},{16,18},{18... | collective-permute-start | bytes 1622024 | tf_op jit(solution)/shard_map/ppermute | solution.py:459
  101.6 8.3 %all-to-all-start.3 = ((bf16[8,32,512]{2,1,0:T(8,128)(2,1)}), bf16[8,32,512]{2,1,0:T(8,128)(2,1)S(1)}, u32[]{:S(2)}, u32[]{:S(2)}) async-start(bf16[8,32,512]{2,1,0:T(8,128)(2,1)} %bitcast.10), calls=%async_computation.3 | async-start | bytes 524288 | tf_op jit(solution)/shard_map/all_to_all | solution.py:456
  111.1 11.0 %collective-permute-done.6.cross_ref = bf16[256,1024]{1,0:T(8,128)(2,1)} collective-permute-done((bf16[256,1024]{1,0:T(8,128)(2,1)}, bf16[256,1024]{1,0:T(8,128)(2,1)}, u32[]{:S(2)}, u32[]{:S(2)}) %collective-permute-start.6) | collective-permute-done | bytes 524320 | tf_op jit(solution)/shard_map/ppermute | solution.py:436
  122.8 8.8 %all-to-all-start.4 = ((f32[4,32,512]{2,1,0:T(8,128)}), f32[4,32,512]{2,1,0:T(8,128)S(1)}, u32[]{:S(2)}, u32[]{:S(2)}) async-start(f32[4,32,512]{2,1,0:T(8,128)} %shard_map.98), calls=%async_computation.4 | async-start | bytes 524288 | tf_op jit(solution)/shard_map/all_to_all | solution.py:471
  131.6 2.6 %shard_map.100 = bf16[512,960]{1,0:T(8,128)(2,1)S(1)} custom-call(s32[1]{0:T(128)} %bitcast.4.core_ref, s32[1]{0:T(128)} %bitcast.8.half_ref, bf16[272,512]{1,0:T(8,128)(2,1)} %collective-permute-done.7.same_ref, bf16[256,1024]{1,0:T(8,128)(2,1)} %collective-permute-done.6.cross_ref, bf16[1024,512]{1,0:T(8,128)(2,1)S(1)} %bitcast.22, ...), custom_call_target="tpu_custom_call" | custom-call | flops 1000000000 | bytes 4000000 | tf_op jit(solution)/shard_map/pallas_call | solution.py:472
  135.9 2.5 %shard_map.101 = bf16[512,512]{1,0:T(8,128)(2,1)} custom-call(bf16[512,512]{1,0:T(8,128)(2,1)S(1)} %bitcast.28, f32[512,512]{1,0:T(8,128)S(1)} %copy-done.7, bf16[528,512]{1,0:T(8,128)(2,1)} %collective-permute-done.8.low_ref, bf16[528,512]{1,0:T(8,128)(2,1)} %collective-permute-done.9.high_ref, f32[8,512]{1,0:T(8,128)S(1)} %get-tuple-element.73.line_ref, ...), custom_call_target="tpu_custom_call" | custom-call | flops 10000000 | bytes 3000000 | tf_op jit(solution)/shard_map/pallas_call | solution.py:476
  (80 shorter events, 24.6 us)
Async XLA Ops:
  2.1 28.2 %copy-start.24 = (s32[1,1,256]{2,1,0:T(1,128)S(1)}, s32[1,1,256]{2,1,0:T(1,128)}, u32[]{:S(2)}) copy-start(s32[1,1,256]{2,1,0:T(1,128)} %param.10) | copy-start | bytes 3076
  2.1 22.3 %all-to-all-start = ((bf16[8,32,512]{2,1,0:T(8,128)(2,1)}), bf16[8,32,512]{2,1,0:T(8,128)(2,1)S(1)}, u32[]{:S(2)}, u32[]{:S(2)}) async-start(bf16[8,32,512]{2,1,0:T(8,128)(2,1)} %shard_map.85), calls=%async_computation | async-start | bytes 524288 | tf_op jit(solution)/shard_map/all_to_all | solution.py:380
  12.6 31.0 %collective-permute-start.1 = (bf16[512,512]{1,0:T(8,128)(2,1)}, bf16[512,512]{1,0:T(8,128)(2,1)S(1)}, u32[]{:S(2)}, u32[]{:S(2)}) collective-permute-start(bf16[512,512]{1,0:T(8,128)(2,1)} %bitcast.25), channel_id=1, source_target_pairs={{0,2},{2,4},{4,6},{6,8},{8,10},{10,12},{12,14},{14,16},{16,18},{18... | collective-permute-start | bytes 1572872 | tf_op jit(solution)/shard_map/ppermute | solution.py:387
  14.1 29.5 %collective-permute-start.2 = (bf16[512,512]{1,0:T(8,128)(2,1)}, bf16[512,512]{1,0:T(8,128)(2,1)S(1)}, u32[]{:S(2)}, u32[]{:S(2)}) collective-permute-start(bf16[512,512]{1,0:T(8,128)(2,1)} %bitcast.26), channel_id=1, source_target_pairs={{2,0},{4,2},{6,4},{8,6},{10,8},{12,10},{14,12},{16,14},{18,16},{20... | collective-permute-start | bytes 1572872 | tf_op jit(solution)/shard_map/ppermute | solution.py:388
  25.5 19.7 %all-to-all-start.1 = ((bf16[4,256,512]{2,1,0:T(8,128)(2,1)}), bf16[4,256,512]{2,1,0:T(8,128)(2,1)S(1)}, u32[]{:S(2)}, u32[]{:S(2)}) async-start(bf16[4,256,512]{2,1,0:T(8,128)(2,1)} %shard_map.86), calls=%async_computation.1 | async-start | bytes 2097152 | tf_op jit(solution)/shard_map/all_to_all | solution.py:384
  32.0 5.9 %copy-start.23 = (s32[1,1,100,256]{3,1,2,0:T(1,128)S(1)}, s32[1,1,100,256]{3,1,2,0:T(1,128)}, u32[]{:S(2)}) copy-start(s32[1,1,100,256]{3,1,2,0:T(1,128)} %param.11) | copy-start | bytes 307204
  36.0 9.2 %collective-permute-start = (bf16[1024,256]{1,0:T(8,128)(2,1)}, bf16[1024,256]{1,0:T(8,128)(2,1)}, u32[]{:S(2)}, u32[]{:S(2)}) collective-permute-start(bf16[1024,256]{1,0:T(8,128)(2,1)} %get-tuple-element.43), channel_id=1, source_target_pairs={{0,2},{2,0},{4,6},{6,4},{8,10},{10,8},{12,14},{14,12},{16,18},{18,... | collective-permute-start | bytes 1572872 | tf_op jit(solution)/shard_map/ppermute | solution.py:399
  37.9 5.7 %copy-start.3 = (bf16[1,512,512]{2,1,0:T(8,128)(2,1)S(1)}, bf16[1,512,512]{2,1,0:T(8,128)(2,1)}, u32[]{:S(2)}) copy-start(bf16[1,512,512]{2,1,0:T(8,128)(2,1)} %param.7) | copy-start | bytes 1572868
  45.2 4.8 %copy-start.1 = (bf16[1536,512]{1,0:T(8,128)(2,1)S(1)}, bf16[1536,512]{1,0:T(8,128)(2,1)}, u32[]{:S(2)}) copy-start(bf16[1536,512]{1,0:T(8,128)(2,1)} %copy-done) | copy-start | bytes 4718596
  45.2 4.8 %collective-permute-start.3 = (bf16[1024,512]{1,0:T(8,128)(2,1)S(1)}, bf16[1024,512]{1,0:T(8,128)(2,1)S(1)}, u32[]{:S(2)}, u32[]{:S(2)}) collective-permute-start(bf16[1024,512]{1,0:T(8,128)(2,1)S(1)} %bitcast.19), channel_id=1, source_target_pairs={{0,2},{2,0},{4,6},{6,4},{8,10},{10,8},{12,14},{14,12},{16,18},{18,... | collective-permute-start | bytes 3145736 | tf_op jit(solution)/shard_map/ppermute | solution.py:412
  53.3 18.7 %copy-start.8 = (f32[272,128]{1,0:T(8,128)}, f32[272,128]{1,0:T(8,128)S(1)}, u32[]{:S(2)}) copy-start(f32[272,128]{1,0:T(8,128)S(1)} %get-tuple-element.55.sent_ref) | copy-start | bytes 417796
  53.4 14.8 %collective-permute-start.4 = (f32[272,128]{1,0:T(8,128)S(1)}, f32[272,128]{1,0:T(8,128)S(1)}, u32[]{:S(2)}, u32[]{:S(2)}) collective-permute-start(f32[272,128]{1,0:T(8,128)S(1)} %get-tuple-element.55.sent_ref), channel_id=1, source_target_pairs={{0,1},{1,0},{2,3},{3,2},{4,5},{5,4},{6,7},{7,6},{8,9},{9,8},{10,11... | collective-permute-start | bytes 417800 | tf_op jit(solution)/shard_map/ppermute | solution.py:421
  68.1 5.4 %copy-start.10 = (f32[272,128]{1,0:T(8,128)}, f32[272,128]{1,0:T(8,128)S(1)}, u32[]{:S(2)}) copy-start(f32[272,128]{1,0:T(8,128)S(1)} %collective-permute-done.4.got_ref) | copy-start | bytes 417796
  73.5 5.4 %copy-start.5 = (bf16[272,512]{1,0:T(8,128)(2,1)}, bf16[272,512]{1,0:T(8,128)(2,1)S(1)}, u32[]{:S(2)}) copy-start(bf16[272,512]{1,0:T(8,128)(2,1)S(1)} %get-tuple-element.70.dctx_ref.own_ref) | copy-start | bytes 835588
  73.5 3.6 %collective-permute-start.5 = (bf16[272,512]{1,0:T(8,128)(2,1)S(1)}, bf16[272,512]{1,0:T(8,128)(2,1)}, u32[]{:S(2)}, u32[]{:S(2)}) collective-permute-start(bf16[272,512]{1,0:T(8,128)(2,1)S(1)} %get-tuple-element.70.dctx_ref.own_ref), channel_id=1, source_target_pairs={{0,2},{2,0},{4,6},{6,4},{8,10},{10,8},{12,14},{14,12},{16,18},{18,... | collective-permute-start | bytes 835592 | tf_op jit(solution)/shard_map/ppermute | solution.py:430
  79.9 20.9 %all-to-all-start.2 = ((bf16[4,256,512]{2,1,0:T(8,128)(2,1)}), bf16[4,256,512]{2,1,0:T(8,128)(2,1)S(1)}, u32[]{:S(2)}, u32[]{:S(2)}) async-start(bf16[4,256,512]{2,1,0:T(8,128)(2,1)} %bitcast.24), calls=%async_computation.2 | async-start | bytes 2097152 | tf_op jit(solution)/shard_map/all_to_all | solution.py:442
  84.7 37.3 %collective-permute-start.6 = (bf16[256,1024]{1,0:T(8,128)(2,1)}, bf16[256,1024]{1,0:T(8,128)(2,1)}, u32[]{:S(2)}, u32[]{:S(2)}) collective-permute-start(bf16[256,1024]{1,0:T(8,128)(2,1)} %copy-done.12), channel_id=1, source_target_pairs={{0,385},{1,384},{128,1},{129,0},{256,129},{257,128},{384,257},{385... | collective-permute-start | bytes 1572872 | tf_op jit(solution)/shard_map/ppermute | solution.py:436
  88.4 22.7 %collective-permute-start.7 = (bf16[272,512]{1,0:T(8,128)(2,1)}, bf16[272,512]{1,0:T(8,128)(2,1)}, u32[]{:S(2)}, u32[]{:S(2)}) collective-permute-start(bf16[272,512]{1,0:T(8,128)(2,1)} %copy-done.5), channel_id=1, source_target_pairs={{0,384},{128,0},{256,128},{384,256},{1,385},{129,1},{257,129},{385... | collective-permute-start | bytes 835592 | tf_op jit(solution)/shard_map/ppermute | solution.py:441
  97.3 38.2 %collective-permute-start.8 = (bf16[528,512]{1,0:T(8,128)(2,1)}, bf16[528,512]{1,0:T(8,128)(2,1)}, u32[]{:S(2)}, u32[]{:S(2)}) collective-permute-start(bf16[528,512]{1,0:T(8,128)(2,1)} %get-tuple-element.75), channel_id=1, source_target_pairs={{0,2},{2,4},{4,6},{6,8},{8,10},{10,12},{12,14},{14,16},{16,18},{18... | collective-permute-start | bytes 1622024 | tf_op jit(solution)/shard_map/ppermute | solution.py:459
  99.5 36.1 %collective-permute-start.9 = (bf16[528,512]{1,0:T(8,128)(2,1)}, bf16[528,512]{1,0:T(8,128)(2,1)}, u32[]{:S(2)}, u32[]{:S(2)}) collective-permute-start(bf16[528,512]{1,0:T(8,128)(2,1)} %get-tuple-element.76), channel_id=1, source_target_pairs={{2,0},{4,2},{6,4},{8,6},{10,8},{12,10},{14,12},{16,14},{18,16},{20... | collective-permute-start | bytes 1622024 | tf_op jit(solution)/shard_map/ppermute | solution.py:460
  101.6 20.4 %all-to-all-start.3 = ((bf16[8,32,512]{2,1,0:T(8,128)(2,1)}), bf16[8,32,512]{2,1,0:T(8,128)(2,1)S(1)}, u32[]{:S(2)}, u32[]{:S(2)}) async-start(bf16[8,32,512]{2,1,0:T(8,128)(2,1)} %bitcast.10), calls=%async_computation.3 | async-start | bytes 524288 | tf_op jit(solution)/shard_map/all_to_all | solution.py:456
  122.8 15.7 %all-to-all-start.4 = ((f32[4,32,512]{2,1,0:T(8,128)}), f32[4,32,512]{2,1,0:T(8,128)S(1)}, u32[]{:S(2)}, u32[]{:S(2)}) async-start(f32[4,32,512]{2,1,0:T(8,128)} %shard_map.98), calls=%async_computation.4 | async-start | bytes 524288 | tf_op jit(solution)/shard_map/all_to_all | solution.py:471
  134.2 1.7 %copy-start.9 = (f32[272,128]{1,0:T(8,128)S(1)}, f32[272,128]{1,0:T(8,128)}, u32[]{:S(2)}) copy-start(f32[272,128]{1,0:T(8,128)} %copy-done.8) | copy-start | bytes 417796
  134.2 1.7 %copy-start.11 = (f32[272,128]{1,0:T(8,128)S(1)}, f32[272,128]{1,0:T(8,128)}, u32[]{:S(2)}) copy-start(f32[272,128]{1,0:T(8,128)} %copy-done.10) | copy-start | bytes 417796
  (16 other events, 16.3 us)
